TPU v7x, 256 devices: a whole 4x4x8 slice. The times are simulated.
256 devices in a mesh: dp: 32 (over z_hi, y, x), owner: 8 (over z_lo, core).
Axes of the slice: x: 4, y: 4, z: 8 (z_hi: 2, z_lo: 4; z = z_hi * 4 + z_lo), core: 2. Of those that a mesh axis runs over, the one named last changes fastest.
Arguments:
- grad_partial: bfloat16 [32, 32, 1024, 1024], P('dp', None, 'owner')
- factor_stats: float32 [32, 8, 256, 1024], P('dp', 'owner'), as said below
- owner_table: int32 [32], P('dp'), may hold values from 0 to 7, as said below
Outputs:
- direction: float32 [32, 1024, 1024], P('dp', 'owner')
Inputs may be any that keep to these rules, and one draw needn't show every extreme that they name: `factor_stats`: left_stats and right_stats of every block are symmetric positive definite. `owner_table`: every slot is the first slot of the left factor of exactly 4 blocks.
All inputs are finite; a program needn't handle non-finite values.
Results may differ from a plain program's by a relative error of at most 0.0067.
Values may be sent and summed in bfloat16 or wider, within the bound.
No kernel may reach another device: no remote copies, remote signals or barrier semaphores. Data moves between devices by JAX's collectives and lax.ppermute only.
A program may use at most 128 MiB of HBM per device.

v0:
```python
import functools

import jax
import jax.numpy as jnp
from jax import lax
from jax.experimental import pallas as pl
from jax.experimental.pallas import tpu as pltpu
from jax.sharding import Mesh
from jax.sharding import PartitionSpec as P

FINE = ("zh", "y", "x", "zl", "c")


def fine_mesh(mesh):
    return Mesh(mesh.devices.reshape(2, 4, 4, 4, 2), FINE)


def shift(array, axis, step):
    size = lax.axis_size(axis)
    return lax.ppermute(array, axis, [(i, (i + step) % size) for i in range(size)])


def swap(array, axis, mask):
    size = lax.axis_size(axis)
    return lax.ppermute(array, axis, [(i, i ^ mask) for i in range(size)])


def f32sum(*terms):
    total = terms[0].astype(jnp.float32)
    for term in terms[1:]:
        total = total + term.astype(jnp.float32)
    return total


def narrow(*terms):
    return f32sum(*terms).astype(jnp.bfloat16)


VMEM = pl.BlockSpec(memory_space=pltpu.VMEM)
SMEM = pl.BlockSpec(memory_space=pltpu.SMEM)
HBM = pl.BlockSpec(memory_space=pltpu.HBM)


def call(kernel, name, out_shape, in_specs, operands, scratch=(), mib=16, flops=0, moved=0):
    outs = (VMEM,) * len(out_shape) if isinstance(out_shape, tuple) else VMEM
    return pl.pallas_call(
        kernel,
        out_shape=out_shape,
        in_specs=in_specs,
        out_specs=outs,
        scratch_shapes=list(scratch),
        compiler_params=pltpu.CompilerParams(vmem_limit_bytes=mib * 2**20),
        cost_estimate=pl.CostEstimate(flops=flops, bytes_accessed=moved, transcendentals=0),
        name=name,
    )(*operands)


def ring_first(up, down, axis):
    return shift(up, axis, 1), shift(down, axis, -1)


def pass_kernel(mid_ref, up_ref, down_ref, last_up_ref, last_down_ref):
    count, rows, _ = last_up_ref.shape
    for block in range(count):
        for row in range(0, rows, 32):
            at = pl.ds(row, 32)
            last_up_ref[block, at] = narrow(mid_ref[block, at], up_ref[block, at])
            last_down_ref[block, at] = narrow(mid_ref[count + block, at], down_ref[block, at])


def pass_on(mid, up, down):
    count = mid.shape[0] // 2
    last = jax.ShapeDtypeStruct((count,) + mid.shape[1:], mid.dtype)
    last_up, last_down = call(
        pass_kernel, "pass_on", (last, last), [VMEM] * 3, (mid, up, down), flops=mid.size, moved=6 * mid.size
    )
    return last_up, last_down


def turn_kernel(place_ref, own_ref, up_ref, down_ref, last_up_ref, last_down_ref, next_up, next_down, next_mid, next_own, sum_ref):
    rows = own_ref.shape[1]
    half = rows // 2
    for block in range(2):
        for row in range(0, rows, 32):
            at = pl.ds(row, 32)
            sum_ref[block, at] = narrow(own_ref[block, at], last_up_ref[block, at], down_ref[2 + block, at])
            sum_ref[2 + block, at] = narrow(own_ref[2 + block, at], up_ref[2 + block, at], last_down_ref[block, at])
    low, high = pl.ds(0, half), pl.ds(half, half)
    here = place_ref[0]
    ahead, across, behind = (lax.rem(here + step, 4) for step in (1, 2, 3))
    next_up[0] = sum_ref[across, low]
    next_up[1] = sum_ref[ahead, high]
    next_down[0] = sum_ref[across, high]
    next_down[1] = sum_ref[behind, low]
    next_mid[0] = sum_ref[ahead, low]
    next_mid[1] = sum_ref[behind, high]
    next_own[0] = sum_ref[here, low]
    next_own[1] = sum_ref[here, high]


def turn(place, own, up, down, last_up, last_down):
    rows, size = own.shape[1:]
    part = jax.ShapeDtypeStruct((2, rows // 2, size), own.dtype)
    return call(
        turn_kernel,
        "turn",
        (part,) * 4,
        [SMEM] + [VMEM] * 5,
        (place, own, up, down, last_up, last_down),
        scratch=[pltpu.VMEM(own.shape, own.dtype)],
        flops=2 * own.size,
        moved=8 * own.size,
    )


def pieces_kernel(*refs):
    out_ref = refs[-1]
    width = out_ref.shape[2]
    for side in range(2):
        own, up, down, last_up, last_down = refs[5 * side : 5 * side + 5]
        half = own.shape[1]
        for row in range(0, half, 32):
            at = pl.ds(row, 32)
            low = narrow(own[0, at], last_up[0, at], down[1, at])
            high = narrow(own[1, at], up[1, at], last_down[0, at])
            for piece in range(8):
                columns = slice(piece * width, (piece + 1) * width)
                out_ref[8 * side + piece, at] = low[:, columns]
                out_ref[8 * side + piece, pl.ds(half + row, 32)] = high[:, columns]


def make_pieces(*parts):
    rows, size = 2 * parts[0].shape[1], parts[0].shape[2]
    out = jax.ShapeDtypeStruct((16, rows, size // 8), jnp.bfloat16)
    return call(
        pieces_kernel, "pieces", out, [VMEM] * 10, parts, flops=4 * rows * size, moved=16 * rows * size
    )


def copy_blocks(grads_ref, moves, cut, sems):
    rows = grads_ref.shape[3] // cut
    copies = [
        pltpu.make_async_copy(
            grads_ref.at[where + (pl.ds(part * rows, rows),)],
            out.at[slot, pl.ds(part * rows, rows)],
            sems.at[cut * i + part],
        )
        for i, (where, out, slot) in enumerate(moves)
        for part in range(cut)
    ]
    for each in copies:
        each.start()
    for each in copies:
        each.wait()


def steps(place_ref, which):
    return tuple(lax.rem(place_ref[which] + step, 4) for step in range(4))


def trim_kernel(index_ref, stats_ref, out_ref):
    rows = stats_ref.shape[0]
    half = rows // 2

    def block(at):
        return pl.ds(at % 4 * rows, rows)

    for index in range(4):

        @pl.when(index_ref[0] == index)
        def _():
            out_ref[:, block(0)] = stats_ref[:, block(index)].astype(jnp.bfloat16)
            out_ref[:, block(1)] = stats_ref[:, block(index + 1)].astype(jnp.bfloat16)
            if index < 2:
                opposite = stats_ref[:, pl.ds((index + 2) * rows, half)]
            else:
                opposite = stats_ref[pl.ds(half, half), block(index + 2)].T
            out_ref[:, pl.ds(2 * rows, half)] = opposite.astype(jnp.bfloat16)


def trim(index, stats):
    rows = stats.shape[0]
    out = jax.ShapeDtypeStruct((rows, 2 * rows + rows // 2), jnp.bfloat16)
    return call(trim_kernel, "trim", out, [SMEM, VMEM], (index, stats), flops=stats.size, moved=6 * stats.size)


def send_kernel(place_ref, grads_ref, x_up, x_down, y_up, y_down, sems):
    x, y = steps(place_ref, 0), steps(place_ref, 1)
    moves = []
    for i in range(2):
        moves += [
            ((0, i, x[2]), x_up, i),
            ((0, 2 + i, x[1]), x_up, 2 + i),
            ((0, 2 + i, x[2]), x_down, i),
            ((0, i, x[3]), x_down, 2 + i),
            ((1, y[2], i), y_up, i),
            ((1, y[1], 2 + i), y_up, 2 + i),
            ((1, y[2], 2 + i), y_down, i),
            ((1, y[3], i), y_down, 2 + i),
        ]
    copy_blocks(grads_ref, moves, 4, sems)


def keep_kernel(place_ref, grads_ref, x_mid, x_own, y_mid, y_own, sems):
    x, y = steps(place_ref, 0), steps(place_ref, 1)
    moves = []
    for i in range(2):
        moves += [
            ((0, i, x[1]), x_mid, i),
            ((0, 2 + i, x[3]), x_mid, 2 + i),
            ((1, y[1], i), y_mid, i),
            ((1, y[3], 2 + i), y_mid, 2 + i),
        ]
    for i in range(4):
        moves += [((0, i, x[0]), x_own, i), ((1, y[0], i), y_own, i)]
    copy_blocks(grads_ref, moves, 1, sems)


def pack(kernel, mib, place, grads):
    payload = jax.ShapeDtypeStruct((4,) + grads.shape[3:], grads.dtype)
    return call(
        kernel,
        kernel.__name__[:4],
        (payload,) * 4,
        [SMEM, HBM],
        (place, grads),
        scratch=[pltpu.SemaphoreType.DMA((64,))],
        mib=mib,
        moved=2**23,
    )


def root_kernel(where_ref, *refs):
    given, (out_ref, slots_ref, start_ref, first_ref, second_ref, third_ref) = refs[:8], refs[8:]
    size = out_ref.shape[0]
    slot = size // 4
    half = slot // 2
    offset, zl, c = where_ref[0], where_ref[1], where_ref[2]

    def span(tile):
        return pl.ds(tile * slot, slot)

    for tile in range(4):
        position = lax.rem(offset + tile, 8)
        back = lax.rem(zl + 4 - lax.div(position, 2), 4)
        source = 2 * back + lax.rem(position + c, 2)
        for i, ref in enumerate(given):

            @pl.when(source == i)
            def _():
                slots_ref[tile] = ref[...]

    total = jnp.zeros((8, slot // 2), jnp.float32)
    for tile in range(4):
        values = slots_ref[tile].astype(jnp.float32)
        squares = values * values
        total = total + lanes(squares[:, :slot]) + 2.0 * lanes(squares[:, slot:])
    inverse = 1.0 / jnp.sqrt(jnp.sum(total))

    row_ids = lax.broadcasted_iota(jnp.int32, (slot, slot), 0)
    col_ids = lax.broadcasted_iota(jnp.int32, (slot, slot), 1)
    eye = jnp.where(row_ids == col_ids, 1.0, 0.0).astype(jnp.float32)

    def place(row, column, normed, diagonal):
        start_ref[span(row), span(column)] = normed.astype(jnp.bfloat16)
        term = 1.5 * eye - 0.5 * normed if diagonal else -0.5 * normed
        first_ref[span(row), span(column)] = term.astype(jnp.bfloat16)

    for tile in range(4):
        after = (tile + 1) % 4
        place(tile, tile, slots_ref[tile, :, :slot].astype(jnp.float32) * inverse, True)
        normed = slots_ref[tile, :, slot : 2 * slot].astype(jnp.float32) * inverse
        place(tile, after, normed, False)
        place(after, tile, normed.T, False)
    for tile in range(2):
        parts = [slots_ref[at, :, 2 * slot :].astype(jnp.float32) * inverse for at in (tile, tile + 2)]
        normed = jnp.concatenate(parts, axis=1)
        place(tile, tile + 2, normed, False)
        place(tile + 2, tile, normed.T, False)

    def eye_rows(tile):
        row_ids = lax.broadcasted_iota(jnp.int32, (slot, size), 0) + tile * slot
        col_ids = lax.broadcasted_iota(jnp.int32, (slot, size), 1)
        return jnp.where(row_ids == col_ids, 1.0, 0.0).astype(jnp.float32)

    for tile in range(4):
        product = jnp.dot(start_ref[span(tile), :], first_ref[...], preferred_element_type=jnp.float32)
        second_ref[span(tile), :] = product.astype(jnp.bfloat16)
    for tile in range(4):
        product = jnp.dot(first_ref[span(tile), :], second_ref[...], preferred_element_type=jnp.float32)
        third_ref[span(tile), :] = (1.5 * eye_rows(tile) - 0.5 * product).astype(jnp.bfloat16)
    for tile in range(4):
        product = jnp.dot(third_ref[span(tile), :], first_ref[...], preferred_element_type=jnp.float32)
        out_ref[span(tile), :] = product.astype(jnp.bfloat16)


def left_inverse_root(where, slots):
    rows, kept = slots[0].shape
    size = 4 * rows
    return call(
        root_kernel,
        "left_root",
        jax.ShapeDtypeStruct((size, size), jnp.bfloat16),
        [SMEM] + [VMEM] * 8,
        (where,) + slots,
        scratch=[pltpu.VMEM((4, rows, kept), jnp.bfloat16)] + [pltpu.VMEM((size, size), jnp.bfloat16)] * 4,
        flops=6 * size**3,
        moved=4 * size * size,
    )


def base_kernel(where_ref, *refs):
    given, (first_ref, diagonal_ref, slots_ref) = refs[:8], refs[8:]
    size = first_ref.shape[0]
    slot = size // 4
    half = slot // 2
    offset, zl, c = where_ref[0], where_ref[1], where_ref[2]

    def span(tile):
        return pl.ds(tile * slot, slot)

    for tile in range(4):
        position = lax.rem(offset + (4 + tile), 8)
        back = lax.rem(zl + 4 - lax.div(position, 2), 4)
        source = 2 * back + lax.rem(position + c, 2)
        for i, ref in enumerate(given):

            @pl.when(source == i)
            def _():
                slots_ref[tile] = ref[...]

    total = jnp.zeros((8, slot // 2), jnp.float32)
    for tile in range(4):
        values = slots_ref[tile].astype(jnp.float32)
        squares = values * values
        total = total + lanes(squares[:, :slot]) + 2.0 * lanes(squares[:, slot:])
    inverse = 1.0 / jnp.sqrt(jnp.sum(total))

    row_ids = lax.broadcasted_iota(jnp.int32, (slot, slot), 0)
    col_ids = lax.broadcasted_iota(jnp.int32, (slot, slot), 1)
    eye = jnp.where(row_ids == col_ids, 1.0, 0.0).astype(jnp.float32)

    def place(row, column, normed):
        first_ref[span(row), span(column)] = (-0.5 * normed).astype(jnp.bfloat16)

    for tile in range(4):
        following = (tile + 1) % 4
        normed = slots_ref[tile, :, :slot].astype(jnp.float32) * inverse
        first = (1.5 * eye - 0.5 * normed).astype(jnp.bfloat16)
        first_ref[span(tile), span(tile)] = first
        start = normed.astype(jnp.bfloat16).astype(jnp.float32)
        both = eye * (start + 2.0 * first.astype(jnp.float32))
        row = jnp.sum(both, axis=0, keepdims=True)
        diagonal_ref[:, span(tile)] = jnp.broadcast_to(row, (diagonal_ref.shape[0], slot))
        normed = slots_ref[tile, :, slot : 2 * slot].astype(jnp.float32) * inverse
        place(tile, following, normed)
        place(following, tile, normed.T)
    for tile in range(2):
        parts = [slots_ref[at, :, 2 * slot :].astype(jnp.float32) * inverse for at in (tile, tile + 2)]
        normed = jnp.concatenate(parts, axis=1)
        place(tile, tile + 2, normed)
        place(tile + 2, tile, normed.T)


def right_base(where, slots):
    rows, kept = slots[0].shape
    size = 4 * rows
    return call(
        base_kernel,
        "right_base",
        (
            jax.ShapeDtypeStruct((size, size), jnp.bfloat16),
            jax.ShapeDtypeStruct((8, size), jnp.float32),
        ),
        [SMEM] + [VMEM] * 8,
        (where,) + slots,
        scratch=[pltpu.VMEM((4, rows, kept), jnp.bfloat16)],
        flops=4 * size * size,
        moved=4 * size * size,
    )


def lanes(squares):
    rows, columns = squares.shape
    total = jnp.sum(squares.reshape(rows // 8, 8, columns), axis=0)
    return sum(total[:, at : at + 128] for at in range(0, columns, 128))


def mix_kernel(pieces_ref, left_ref, out_ref, energy_ref, grad_ref):
    count, rows, _ = out_ref.shape
    energy = jnp.zeros(energy_ref.shape, jnp.float32)
    for piece in range(count):
        grad = narrow(pieces_ref[piece], pieces_ref[count + piece])
        grad_ref[pl.ds(piece * rows, rows), :] = grad
        wide = grad.astype(jnp.float32)
        energy = energy + lanes(wide * wide)
    energy_ref[...] = energy
    for piece in range(0, count, 2):
        product = jnp.dot(
            left_ref[pl.ds(piece * rows, 2 * rows), :], grad_ref[...], preferred_element_type=jnp.float32
        ).astype(jnp.bfloat16)
        out_ref[piece] = product[:rows]
        out_ref[piece + 1] = product[rows:]


def mix(pieces, left_root):
    _, rows, width = pieces.shape
    return call(
        mix_kernel,
        "mix",
        (jax.ShapeDtypeStruct((8, rows, width), jnp.bfloat16), jax.ShapeDtypeStruct((8, 128), jnp.float32)),
        [VMEM] * 2,
        (pieces, left_root),
        scratch=[pltpu.VMEM((8 * rows, width), jnp.bfloat16)],
        flops=2 * left_root.size * width,
        moved=2 * left_root.size,
    )


def condition_kernel(mixed_ref, first_ref, diagonal_ref, energy_ref, out_ref, totals_ref, wide_ref, even_ref, odd_ref):
    count, _, width = mixed_ref.shape
    for piece in range(count):
        odd_ref[:, pl.ds(piece * width, width)] = mixed_ref[piece]

    def products(slab_ref):
        for column in range(0, out_ref.shape[1], 2 * width):
            at = pl.ds(column, 2 * width)
            yield at, jnp.dot(slab_ref[...], first_ref[:, at], preferred_element_type=jnp.float32)

    for at, product in products(odd_ref):
        wide_ref[:, at] = product
        even_ref[:, at] = product.astype(jnp.bfloat16)
    for at, product in products(even_ref):
        odd_ref[:, at] = product.astype(jnp.bfloat16)
    for at, product in products(odd_ref):
        started = diagonal_ref[:1, at] * odd_ref[:, at].astype(jnp.float32) - 2.0 * product
        even_ref[:, at] = started.astype(jnp.bfloat16)
    total = jnp.zeros(energy_ref.shape, jnp.float32)
    for at, product in products(even_ref):
        precond = 1.5 * wide_ref[:, at] - 0.5 * product
        out_ref[:, at] = precond
        total = total + lanes(precond * precond)
    totals_ref[:8] = energy_ref[...]
    totals_ref[8:] = total


def condition(mixed, first, diagonal, energy):
    _, rows, width = mixed.shape
    slab = (rows, 8 * width)
    return call(
        condition_kernel,
        "condition",
        (jax.ShapeDtypeStruct(slab, jnp.float32), jax.ShapeDtypeStruct((16, 128), jnp.float32)),
        [VMEM] * 4,
        (mixed, first, diagonal, energy),
        scratch=[pltpu.VMEM(slab, jnp.float32), pltpu.VMEM(slab, jnp.bfloat16), pltpu.VMEM(slab, jnp.bfloat16)],
        flops=8 * rows * first.size,
        moved=2 * first.size,
    )


def finish_kernel(count, totals_ref, precond_ref, out_ref):
    grad_mean = jnp.sum(totals_ref[:8]) / count
    cond_mean = jnp.sum(totals_ref[8:]) / count
    factor = jnp.sqrt(grad_mean / (cond_mean + 1e-06))
    for row in range(0, out_ref.shape[0], 32):
        at = pl.ds(row, 32)
        out_ref[at] = precond_ref[at] * factor


def finish(totals, precond, count):
    return call(
        functools.partial(finish_kernel, count),
        "finish",
        jax.ShapeDtypeStruct(precond.shape, jnp.float32),
        [VMEM] * 2,
        (totals, precond),
        flops=precond.size,
        moved=8 * precond.size,
    )


def after(dep, *values):
    return lax.optimization_barrier((dep,) + values)[1:]


def local(grad_partial, factor_stats, owner_table):
    size = grad_partial.shape[3]
    rows_here = grad_partial.shape[2]
    owner = ("zl", "c")
    grads = grad_partial.reshape(2, 4, 4, rows_here, size)
    zh, y, x, zl, c = (lax.axis_index(axis).astype(jnp.int32) for axis in FINE)
    place = jnp.stack((x, y))

    x_up, x_down, y_up, y_down = pack(send_kernel, 48, place, grads)
    x_ends = ring_first(x_up, x_down, "x")
    y_ends = ring_first(y_up, y_down, "y")

    place, table = after(x_up, place, owner_table)
    near = [trim((2 * zl + c - table + 8) % 4, factor_stats[0, 0])]
    near.append(shift(near[0], "zl", 1))
    x_mid, x_own, y_mid, y_own = pack(keep_kernel, 16, place, grads)
    near.append(shift(*after(x_mid, near[1]), "zl", 1))
    near.append(shift(near[2], "zl", 1))
    (x_mid,) = after(near[2], x_mid)
    x_last = pass_on(x_mid, *x_ends)
    y_last = pass_on(y_mid, *y_ends)
    far = [swap(each, "c", 1) for each in near[:3]]
    far.append(swap(*after(x_last[0], near[3]), "c", 1))
    slots = tuple(each for pair in zip(near, far) for each in pair)
    where = jnp.stack((table[0], zl, c))

    x_last = ring_first(*x_last, "x")
    y_last = ring_first(*y_last, "y")

    lower_up, lower_down, lower_mid, lower_own = turn(y[None], x_own, *x_ends, *x_last)
    lower_ends = ring_first(lower_up, lower_down, "y")
    upper_up, upper_down, upper_mid, upper_own = turn(x[None], y_own, *y_ends, *y_last)
    upper_ends = ring_first(upper_up, upper_down, "x")
    lower_last = ring_first(*pass_on(lower_mid, *lower_ends), "y")
    upper_last = ring_first(*pass_on(upper_mid, *upper_ends), "x")
    pieces = make_pieces(lower_own, *lower_ends, *lower_last, upper_own, *upper_ends, *upper_last)

    slots = after(pieces, *slots)
    pieces = lax.all_to_all(pieces, ("zh",) + owner, split_axis=0, concat_axis=0, tiled=True)
    mixed, energy = mix(pieces, left_inverse_root(where, slots))
    right = right_base(where, after(mixed, *slots))
    mixed = lax.all_to_all(mixed, owner, split_axis=0, concat_axis=0, tiled=True)
    precond, totals = condition(mixed, *right, energy)
    totals = totals + swap(totals, "c", 1)
    totals = totals + shift(totals, "zl", 1) + shift(totals, "zl", 2) + shift(totals, "zl", 3)
    return finish(totals, precond, float(size * size))[None]


def solution(mesh):
    dp, owner = ("zh", "y", "x"), ("zl", "c")
    placed = (P(dp, None, owner, None), P(dp, owner, None, None), P(dp))
    return jax.shard_map(
        local, mesh=fine_mesh(mesh), in_specs=placed, out_specs=P(dp, owner, None), check_vma=False
    )
```

profile of v0, /device:TPU:6, one launch (start us, length us, event | category | flops | bytes accessed | tf_op | source)
XLA Modules:
  0.0 120.1 jit_solution(4344962380911185375)
XLA Ops:
  0.1 5.3 %send.1 = (bf16[4,128,1024]{2,1,0:T(8,128)(2,1)}, bf16[4,128,1024]{2,1,0:T(8,128)(2,1)}, bf16[4,128,1024]{2,1,0:T(8,128)(2,1)}, bf16[4,128,1024]{2,1,0:T(8,128)(2,1)}) custom-call(s32[2]{0:T(128)S(1)} %pad_add_fusion.place_ref, bf16[2,4,4,128,1024]{4,3,2,1,0:T(8,128)(2,1)} %bitcast.8), custom_call_target="tpu_custom_call" | custom-call | bytes 8388608 | tf_op jit(solution)/shard_map/send/pallas_call | solution.py:46
  5.4 2.3 %collective-permute-start = (bf16[4,128,1024]{2,1,0:T(8,128)(2,1)}, bf16[4,128,1024]{2,1,0:T(8,128)(2,1)S(1)}, u32[]{:S(2)}, u32[]{:S(2)}) collective-permute-start(bf16[4,128,1024]{2,1,0:T(8,128)(2,1)} %get-tuple-element.56), channel_id=1, source_target_pairs={{0,8},{8,16},{16,24},{24,0},{1,9},{9,17},{17,25},{25,1},{2,10},{10... | collective-permute-start | bytes 3145736 | tf_op jit(solution)/shard_map/ppermute | solution.py:20
  7.7 1.4 %collective-permute-start.10 = (bf16[4,128,1024]{2,1,0:T(8,128)(2,1)}, bf16[4,128,1024]{2,1,0:T(8,128)(2,1)S(1)}, u32[]{:S(2)}, u32[]{:S(2)}) collective-permute-start(bf16[4,128,1024]{2,1,0:T(8,128)(2,1)} %get-tuple-element.73), channel_id=1, source_target_pairs={{0,32},{32,64},{64,96},{96,0},{1,33},{33,65},{65,97},{97,1},{2,34}... | collective-permute-start | bytes 3145736 | tf_op jit(solution)/shard_map/ppermute | solution.py:20
  9.1 1.9 %collective-permute-start.11 = (bf16[4,128,1024]{2,1,0:T(8,128)(2,1)}, bf16[4,128,1024]{2,1,0:T(8,128)(2,1)S(1)}, u32[]{:S(2)}, u32[]{:S(2)}) collective-permute-start(bf16[4,128,1024]{2,1,0:T(8,128)(2,1)} %get-tuple-element.74), channel_id=1, source_target_pairs={{0,96},{32,0},{64,32},{96,64},{1,97},{33,1},{65,33},{97,65},{2,98}... | collective-permute-start | bytes 3145736 | tf_op jit(solution)/shard_map/ppermute | solution.py:20
  11.6 1.2 %copy-done.1 = f32[1,1,256,1024]{3,2,1,0:T(8,128)S(1)} copy-done((f32[1,1,256,1024]{3,2,1,0:T(8,128)S(1)}, f32[1,1,256,1024]{3,2,1,0:T(8,128)}, u32[]{:S(2)}) %copy-start.1) | copy-done | bytes 1048600
  12.9 1.8 %collective-permute-start.2 = (bf16[256,640]{1,0:T(8,128)(2,1)S(1)}, bf16[256,640]{1,0:T(8,128)(2,1)S(1)}, u32[]{:S(2)}, u32[]{:S(2)}) collective-permute-start(bf16[256,640]{1,0:T(8,128)(2,1)S(1)} %trim.1.refs_0_), channel_id=1, source_target_pairs={{0,2},{2,4},{4,6},{6,0},{1,3},{3,5},{5,7},{7,1},{8,10},{10,12},{12... | collective-permute-start | bytes 983048 | tf_op jit(solution)/shard_map/ppermute | solution.py:20
  14.7 3.4 %copy-done = bf16[1,32,128,1024]{3,2,1,0:T(8,128)(2,1)S(1)} copy-done((bf16[1,32,128,1024]{3,2,1,0:T(8,128)(2,1)S(1)}, bf16[1,32,128,1024]{3,2,1,0:T(8,128)(2,1)}, u32[]{:S(2)}) %copy-start) | copy-done | bytes 8388632
  18.1 1.4 %keep.1 = (bf16[4,128,1024]{2,1,0:T(8,128)(2,1)S(1)}, bf16[4,128,1024]{2,1,0:T(8,128)(2,1)S(1)}, bf16[4,128,1024]{2,1,0:T(8,128)(2,1)S(1)}, bf16[4,128,1024]{2,1,0:T(8,128)(2,1)S(1)}) custom-call(s32[2]{0:T(128)S(1)} %pad_add_fusion.place_ref, bf16[2,4,4,128,1024]{4,3,2,1,0:T(8,128)(2,1)S(1)} %bitcast.9), custom_call_target="tpu_custom_call" | custom-call | bytes 8388608 | tf_op jit(solution)/shard_map/keep/pallas_call | solution.py:46
  19.6 4.5 %collective-permute-done.2.refs_2_ = bf16[256,640]{1,0:T(8,128)(2,1)S(1)} collective-permute-done((bf16[256,640]{1,0:T(8,128)(2,1)S(1)}, bf16[256,640]{1,0:T(8,128)(2,1)S(1)}, u32[]{:S(2)}, u32[]{:S(2)}) %collective-permute-start.2) | collective-permute-done | bytes 327712 | tf_op jit(solution)/shard_map/ppermute | solution.py:20
  24.1 9.6 %collective-permute-done.3.refs_4_ = bf16[256,640]{1,0:T(8,128)(2,1)} collective-permute-done((bf16[256,640]{1,0:T(8,128)(2,1)S(1)}, bf16[256,640]{1,0:T(8,128)(2,1)}, u32[]{:S(2)}, u32[]{:S(2)}) %collective-permute-start.3) | collective-permute-done | bytes 327712 | tf_op jit(solution)/shard_map/ppermute | solution.py:20
  33.7 1.5 %pass_on.4 = (bf16[2,128,1024]{2,1,0:T(8,128)(2,1)S(1)}, bf16[2,128,1024]{2,1,0:T(8,128)(2,1)S(1)}) custom-call(bf16[4,128,1024]{2,1,0:T(8,128)(2,1)S(1)} %get-tuple-element.63.mid_ref, bf16[4,128,1024]{2,1,0:T(8,128)(2,1)S(1)} %collective-permute-done.up_ref, bf16[4,128,1024]{2,1,0:T(8,128)(2,1)} %collective-permute-done.1.down_ref), custom_call_target="tpu_custom_call" | custom-call | flops 524288 | bytes 3145728 | tf_op jit(solution)/shard_map/pass_on/pallas_call | solution.py:46
  37.8 3.0 %collective-permute-start.13 = (bf16[2,128,1024]{2,1,0:T(8,128)(2,1)S(1)}, bf16[2,128,1024]{2,1,0:T(8,128)(2,1)S(1)}, u32[]{:S(2)}, u32[]{:S(2)}) collective-permute-start(bf16[2,128,1024]{2,1,0:T(8,128)(2,1)S(1)} %get-tuple-element.77), channel_id=1, source_target_pairs={{0,96},{32,0},{64,32},{96,64},{1,97},{33,1},{65,33},{97,65},{2,98}... | collective-permute-start | bytes 1572872 | tf_op jit(solution)/shard_map/ppermute | solution.py:20
  40.8 5.4 %collective-permute-done.4.last_up_ref = bf16[2,128,1024]{2,1,0:T(8,128)(2,1)S(1)} collective-permute-done((bf16[2,128,1024]{2,1,0:T(8,128)(2,1)S(1)}, bf16[2,128,1024]{2,1,0:T(8,128)(2,1)S(1)}, u32[]{:S(2)}, u32[]{:S(2)}) %collective-permute-start.4) | collective-permute-done | bytes 524320 | tf_op jit(solution)/shard_map/ppermute | solution.py:20
  46.2 1.3 %collective-permute-done.5.last_down_ref = bf16[2,128,1024]{2,1,0:T(8,128)(2,1)S(1)} collective-permute-done((bf16[2,128,1024]{2,1,0:T(8,128)(2,1)S(1)}, bf16[2,128,1024]{2,1,0:T(8,128)(2,1)S(1)}, u32[]{:S(2)}, u32[]{:S(2)}) %collective-permute-start.5) | collective-permute-done | bytes 524320 | tf_op jit(solution)/shard_map/ppermute | solution.py:20
  47.5 1.7 %turn.2 = (bf16[2,64,1024]{2,1,0:T(8,128)(2,1)S(1)}, bf16[2,64,1024]{2,1,0:T(8,128)(2,1)S(1)}, bf16[2,64,1024]{2,1,0:T(8,128)(2,1)S(1)}, bf16[2,64,1024]{2,1,0:T(8,128)(2,1)S(1)}) custom-call(s32[1]{0:T(128)} %bitcast.place_ref, bf16[4,128,1024]{2,1,0:T(8,128)(2,1)S(1)} %get-tuple-element.58.own_ref, bf16[4,128,1024]{2,1,0:T(8,128)(2,1)S(1)} %collective-permute-done.up_ref, ...), custom_call_target="tpu_custom_call" | custom-call | flops 1048576 | bytes 4194304 | tf_op jit(solution)/shard_map/turn/pallas_call | solution.py:46
  49.2 1.8 %collective-permute-start.6 = (bf16[2,64,1024]{2,1,0:T(8,128)(2,1)S(1)}, bf16[2,64,1024]{2,1,0:T(8,128)(2,1)S(1)}, u32[]{:S(2)}, u32[]{:S(2)}) collective-permute-start(bf16[2,64,1024]{2,1,0:T(8,128)(2,1)S(1)} %get-tuple-element.67), channel_id=1, source_target_pairs={{0,32},{32,64},{64,96},{96,0},{1,33},{33,65},{65,97},{97,1},{2,34}... | collective-permute-start | bytes 786440 | tf_op jit(solution)/shard_map/ppermute | solution.py:20
  51.0 1.5 %collective-permute-start.7 = (bf16[2,64,1024]{2,1,0:T(8,128)(2,1)S(1)}, bf16[2,64,1024]{2,1,0:T(8,128)(2,1)S(1)}, u32[]{:S(2)}, u32[]{:S(2)}) collective-permute-start(bf16[2,64,1024]{2,1,0:T(8,128)(2,1)S(1)} %get-tuple-element.68), channel_id=1, source_target_pairs={{0,96},{32,0},{64,32},{96,64},{1,97},{33,1},{65,33},{97,65},{2,98}... | collective-permute-start | bytes 786440 | tf_op jit(solution)/shard_map/ppermute | solution.py:20
  53.7 1.6 %collective-permute-start.15 = (bf16[2,64,1024]{2,1,0:T(8,128)(2,1)S(1)}, bf16[2,64,1024]{2,1,0:T(8,128)(2,1)S(1)}, u32[]{:S(2)}, u32[]{:S(2)}) collective-permute-start(bf16[2,64,1024]{2,1,0:T(8,128)(2,1)S(1)} %get-tuple-element.80), channel_id=1, source_target_pairs={{0,24},{8,0},{16,8},{24,16},{1,25},{9,1},{17,9},{25,17},{2,26},{10... | collective-permute-start | bytes 786440 | tf_op jit(solution)/shard_map/ppermute | solution.py:20
  55.3 1.9 %collective-permute-start.21 = (bf16[256,640]{1,0:T(8,128)(2,1)}, bf16[256,640]{1,0:T(8,128)(2,1)S(1)}, u32[]{:S(2)}, u32[]{:S(2)}) collective-permute-start(bf16[256,640]{1,0:T(8,128)(2,1)} %collective-permute-done.3.refs_4_), channel_id=1, source_target_pairs={{0,2},{2,4},{4,6},{6,0},{1,3},{3,5},{5,7},{7,1},{8,10},{10,12},{12... | collective-permute-start | bytes 983048 | tf_op jit(solution)/shard_map/ppermute | solution.py:20
  58.3 1.8 %collective-permute-start.8 = (bf16[1,64,1024]{2,1,0:T(8,128)(2,1)S(1)}, bf16[1,64,1024]{2,1,0:T(8,128)(2,1)S(1)}, u32[]{:S(2)}, u32[]{:S(2)}) collective-permute-start(bf16[1,64,1024]{2,1,0:T(8,128)(2,1)S(1)} %get-tuple-element.70), channel_id=1, source_target_pairs={{0,32},{32,64},{64,96},{96,0},{1,33},{33,65},{65,97},{97,1},{2,34}... | collective-permute-start | bytes 393224 | tf_op jit(solution)/shard_map/ppermute | solution.py:20
  60.1 1.6 %collective-permute-start.9 = (bf16[1,64,1024]{2,1,0:T(8,128)(2,1)S(1)}, bf16[1,64,1024]{2,1,0:T(8,128)(2,1)S(1)}, u32[]{:S(2)}, u32[]{:S(2)}) collective-permute-start(bf16[1,64,1024]{2,1,0:T(8,128)(2,1)S(1)} %get-tuple-element.71), channel_id=1, source_target_pairs={{0,96},{32,0},{64,32},{96,64},{1,97},{33,1},{65,33},{97,65},{2,98}... | collective-permute-start | bytes 393224 | tf_op jit(solution)/shard_map/ppermute | solution.py:20
  62.3 1.5 %collective-permute-start.17 = (bf16[1,64,1024]{2,1,0:T(8,128)(2,1)S(1)}, bf16[1,64,1024]{2,1,0:T(8,128)(2,1)S(1)}, u32[]{:S(2)}, u32[]{:S(2)}) collective-permute-start(bf16[1,64,1024]{2,1,0:T(8,128)(2,1)S(1)} %get-tuple-element.83), channel_id=1, source_target_pairs={{0,24},{8,0},{16,8},{24,16},{1,25},{9,1},{17,9},{25,17},{2,26},{10... | collective-permute-start | bytes 393224 | tf_op jit(solution)/shard_map/ppermute | solution.py:20
  65.0 1.7 %collective-permute-done.16.refs_8_ = bf16[1,64,1024]{2,1,0:T(8,128)(2,1)S(1)} collective-permute-done((bf16[1,64,1024]{2,1,0:T(8,128)(2,1)S(1)}, bf16[1,64,1024]{2,1,0:T(8,128)(2,1)S(1)}, u32[]{:S(2)}, u32[]{:S(2)}) %collective-permute-start.16) | collective-permute-done | bytes 131104 | tf_op jit(solution)/shard_map/ppermute | solution.py:20
  66.7 1.7 %collective-permute-done.17.refs_9_ = bf16[1,64,1024]{2,1,0:T(8,128)(2,1)S(1)} collective-permute-done((bf16[1,64,1024]{2,1,0:T(8,128)(2,1)S(1)}, bf16[1,64,1024]{2,1,0:T(8,128)(2,1)S(1)}, u32[]{:S(2)}, u32[]{:S(2)}) %collective-permute-start.17) | collective-permute-done | bytes 131104 | tf_op jit(solution)/shard_map/ppermute | solution.py:20
  69.4 7.8 %all-to-all-start = ((bf16[16,128,128]{2,1,0:T(8,128)(2,1)}), bf16[16,128,128]{2,1,0:T(8,128)(2,1)S(1)}, u32[]{:S(2)}, u32[]{:S(2)}) async-start(bf16[16,128,128]{2,1,0:T(8,128)(2,1)} %pieces.1), calls=%async_computation | async-start | bytes 1048576 | tf_op jit(solution)/shard_map/all_to_all | solution.py:525
  81.5 8.7 %left_root.1.left_ref = bf16[1024,1024]{1,0:T(8,128)(2,1)S(1)} custom-call(s32[3]{0:T(128)S(1)} %pad_add_fusion.1.where_ref, bf16[256,640]{1,0:T(8,128)(2,1)S(1)} %trim.1.refs_0_, bf16[256,640]{1,0:T(8,128)(2,1)S(1)} %collective-permute-done.18.refs_1_, bf16[256,640]{1,0:T(8,128)(2,1)S(1)} %copy-done.3, ...), custom_call_target="tpu_custom_call" | custom-call | flops 6442450944 | bytes 4194304 | tf_op jit(solution)/shard_map/left_root/pallas_call | solution.py:46
  94.7 4.8 %all-to-all-start.1 = ((bf16[8,128,128]{2,1,0:T(8,128)(2,1)}), bf16[8,128,128]{2,1,0:T(8,128)(2,1)S(1)}, u32[]{:S(2)}, u32[]{:S(2)}) async-start(bf16[8,128,128]{2,1,0:T(8,128)(2,1)} %copy-done.15), calls=%async_computation.1 | async-start | bytes 524288 | tf_op jit(solution)/shard_map/all_to_all | solution.py:528
  104.4 2.7 %right_base.1 = (bf16[1024,1024]{1,0:T(8,128)(2,1)S(1)}, f32[8,1024]{1,0:T(8,128)S(1)}) custom-call(s32[3]{0:T(128)S(1)} %pad_add_fusion.1.where_ref, bf16[256,640]{1,0:T(8,128)(2,1)S(1)} %trim.1.refs_0_, bf16[256,640]{1,0:T(8,128)(2,1)S(1)} %copy-done.8, bf16[256,640]{1,0:T(8,128)(2,1)S(1)} %copy-done.3, bf16[256,640]{1,0:T(8,128)(2,1)S(1)} %copy-done.10, ...), custom_call_target="tpu_custom_call" | custom-call | flops 4194304 | bytes 4194304 | tf_op jit(solution)/shard_map/right_base/pallas_call | solution.py:46
  107.1 2.2 %all-to-all-done.1.mixed_ref = bf16[8,128,128]{2,1,0:T(8,128)(2,1)S(1)} async-done(((bf16[8,128,128]{2,1,0:T(8,128)(2,1)}), bf16[8,128,128]{2,1,0:T(8,128)(2,1)S(1)}, u32[]{:S(2)}, u32[]{:S(2)}) %all-to-all-start.1) | async-done | bytes 262176 | tf_op jit(solution)/shard_map/all_to_all | solution.py:528
  109.3 1.4 %condition.1 = (f32[128,1024]{1,0:T(8,128)S(1)}, f32[16,128]{1,0:T(8,128)S(1)}) custom-call(bf16[8,128,128]{2,1,0:T(8,128)(2,1)S(1)} %all-to-all-done.1.mixed_ref, bf16[1024,1024]{1,0:T(8,128)(2,1)S(1)} %get-tuple-element.102.first_ref, f32[8,1024]{1,0:T(8,128)S(1)} %get-tuple-element.103.diagonal_ref, f32[8,128]{1,0:T(8,128)S(1)} %get-tuple-element.104.energy_ref), custom_call_target="tpu_custom_call" | custom-call | flops 1073741824 | bytes 2097152 | tf_op jit(solution)/shard_map/condition/pallas_call | solution.py:46
  112.0 1.6 %collective-permute-start.26 = (f32[16,128]{1,0:T(8,128)S(1)}, f32[16,128]{1,0:T(8,128)S(1)}, u32[]{:S(2)}, u32[]{:S(2)}) collective-permute-start(f32[16,128]{1,0:T(8,128)S(1)} %add.27), channel_id=1, source_target_pairs={{0,6},{2,0},{4,2},{6,4},{1,7},{3,1},{5,3},{7,5},{8,14},{10,8},{12,... | collective-permute-start | bytes 24584 | tf_op jit(solution)/shard_map/ppermute | solution.py:20
  115.6 2.5 %collective-permute-done.25 = f32[16,128]{1,0:T(8,128)S(1)} collective-permute-done((f32[16,128]{1,0:T(8,128)S(1)}, f32[16,128]{1,0:T(8,128)S(1)}, u32[]{:S(2)}, u32[]{:S(2)}) %collective-permute-start.25) | collective-permute-done | bytes 8224 | tf_op jit(solution)/shard_map/ppermute | solution.py:20
  (77 shorter events, 26.8 us)
Async XLA Ops:
  5.4 28.3 %collective-permute-start = (bf16[4,128,1024]{2,1,0:T(8,128)(2,1)}, bf16[4,128,1024]{2,1,0:T(8,128)(2,1)S(1)}, u32[]{:S(2)}, u32[]{:S(2)}) collective-permute-start(bf16[4,128,1024]{2,1,0:T(8,128)(2,1)} %get-tuple-element.56), channel_id=1, source_target_pairs={{0,8},{8,16},{16,24},{24,0},{1,9},{9,17},{17,25},{25,1},{2,10},{10... | collective-permute-start | bytes 3145736 | tf_op jit(solution)/shard_map/ppermute | solution.py:20
  7.7 26.0 %collective-permute-start.1 = (bf16[4,128,1024]{2,1,0:T(8,128)(2,1)}, bf16[4,128,1024]{2,1,0:T(8,128)(2,1)}, u32[]{:S(2)}, u32[]{:S(2)}) collective-permute-start(bf16[4,128,1024]{2,1,0:T(8,128)(2,1)} %get-tuple-element.59), channel_id=1, source_target_pairs={{0,24},{8,0},{16,8},{24,16},{1,25},{9,1},{17,9},{25,17},{2,26},{10... | collective-permute-start | bytes 3145736 | tf_op jit(solution)/shard_map/ppermute | solution.py:20
  7.7 29.6 %collective-permute-start.10 = (bf16[4,128,1024]{2,1,0:T(8,128)(2,1)}, bf16[4,128,1024]{2,1,0:T(8,128)(2,1)S(1)}, u32[]{:S(2)}, u32[]{:S(2)}) collective-permute-start(bf16[4,128,1024]{2,1,0:T(8,128)(2,1)} %get-tuple-element.73), channel_id=1, source_target_pairs={{0,32},{32,64},{64,96},{96,0},{1,33},{33,65},{65,97},{97,1},{2,34}... | collective-permute-start | bytes 3145736 | tf_op jit(solution)/shard_map/ppermute | solution.py:20
  9.1 28.2 %collective-permute-start.11 = (bf16[4,128,1024]{2,1,0:T(8,128)(2,1)}, bf16[4,128,1024]{2,1,0:T(8,128)(2,1)S(1)}, u32[]{:S(2)}, u32[]{:S(2)}) collective-permute-start(bf16[4,128,1024]{2,1,0:T(8,128)(2,1)} %get-tuple-element.74), channel_id=1, source_target_pairs={{0,96},{32,0},{64,32},{96,64},{1,97},{33,1},{65,33},{97,65},{2,98}... | collective-permute-start | bytes 3145736 | tf_op jit(solution)/shard_map/ppermute | solution.py:20
  12.9 11.2 %collective-permute-start.2 = (bf16[256,640]{1,0:T(8,128)(2,1)S(1)}, bf16[256,640]{1,0:T(8,128)(2,1)S(1)}, u32[]{:S(2)}, u32[]{:S(2)}) collective-permute-start(bf16[256,640]{1,0:T(8,128)(2,1)S(1)} %trim.1.refs_0_), channel_id=1, source_target_pairs={{0,2},{2,4},{4,6},{6,0},{1,3},{3,5},{5,7},{7,1},{8,10},{10,12},{12... | collective-permute-start | bytes 983048 | tf_op jit(solution)/shard_map/ppermute | solution.py:20
  14.7 3.4 %copy-start = (bf16[1,32,128,1024]{3,2,1,0:T(8,128)(2,1)S(1)}, bf16[1,32,128,1024]{3,2,1,0:T(8,128)(2,1)}, u32[]{:S(2)}) copy-start(bf16[1,32,128,1024]{3,2,1,0:T(8,128)(2,1)} %param.3) | copy-start | bytes 25165828
  24.0 13.4 %copy-start.2 = (bf16[256,640]{1,0:T(8,128)(2,1)}, bf16[256,640]{1,0:T(8,128)(2,1)S(1)}, u32[]{:S(2)}) copy-start(bf16[256,640]{1,0:T(8,128)(2,1)S(1)} %collective-permute-done.2.refs_2_) | copy-start | bytes 983044
  24.0 9.6 %collective-permute-start.3 = (bf16[256,640]{1,0:T(8,128)(2,1)S(1)}, bf16[256,640]{1,0:T(8,128)(2,1)}, u32[]{:S(2)}, u32[]{:S(2)}) collective-permute-start(bf16[256,640]{1,0:T(8,128)(2,1)S(1)} %collective-permute-done.2.refs_2_), channel_id=1, source_target_pairs={{0,2},{2,4},{4,6},{6,0},{1,3},{3,5},{5,7},{7,1},{8,10},{10,12},{12... | collective-permute-start | bytes 983048 | tf_op jit(solution)/shard_map/ppermute | solution.py:20
  35.1 11.1 %collective-permute-start.4 = (bf16[2,128,1024]{2,1,0:T(8,128)(2,1)S(1)}, bf16[2,128,1024]{2,1,0:T(8,128)(2,1)S(1)}, u32[]{:S(2)}, u32[]{:S(2)}) collective-permute-start(bf16[2,128,1024]{2,1,0:T(8,128)(2,1)S(1)} %get-tuple-element.64), channel_id=1, source_target_pairs={{0,8},{8,16},{16,24},{24,0},{1,9},{9,17},{17,25},{25,1},{2,10},{10... | collective-permute-start | bytes 1572872 | tf_op jit(solution)/shard_map/ppermute | solution.py:20
  36.3 11.3 %collective-permute-start.5 = (bf16[2,128,1024]{2,1,0:T(8,128)(2,1)S(1)}, bf16[2,128,1024]{2,1,0:T(8,128)(2,1)S(1)}, u32[]{:S(2)}, u32[]{:S(2)}) collective-permute-start(bf16[2,128,1024]{2,1,0:T(8,128)(2,1)S(1)} %get-tuple-element.65), channel_id=1, source_target_pairs={{0,24},{8,0},{16,8},{24,16},{1,25},{9,1},{17,9},{25,17},{2,26},{10... | collective-permute-start | bytes 1572872 | tf_op jit(solution)/shard_map/ppermute | solution.py:20
  37.5 15.0 %collective-permute-start.12 = (bf16[2,128,1024]{2,1,0:T(8,128)(2,1)S(1)}, bf16[2,128,1024]{2,1,0:T(8,128)(2,1)S(1)}, u32[]{:S(2)}, u32[]{:S(2)}) collective-permute-start(bf16[2,128,1024]{2,1,0:T(8,128)(2,1)S(1)} %get-tuple-element.76), channel_id=1, source_target_pairs={{0,32},{32,64},{64,96},{96,0},{1,33},{33,65},{65,97},{97,1},{2,34}... | collective-permute-start | bytes 1572872 | tf_op jit(solution)/shard_map/ppermute | solution.py:20
  37.8 14.7 %collective-permute-start.13 = (bf16[2,128,1024]{2,1,0:T(8,128)(2,1)S(1)}, bf16[2,128,1024]{2,1,0:T(8,128)(2,1)S(1)}, u32[]{:S(2)}, u32[]{:S(2)}) collective-permute-start(bf16[2,128,1024]{2,1,0:T(8,128)(2,1)S(1)} %get-tuple-element.77), channel_id=1, source_target_pairs={{0,96},{32,0},{64,32},{96,64},{1,97},{33,1},{65,33},{97,65},{2,98}... | collective-permute-start | bytes 1572872 | tf_op jit(solution)/shard_map/ppermute | solution.py:20
  49.2 8.0 %collective-permute-start.6 = (bf16[2,64,1024]{2,1,0:T(8,128)(2,1)S(1)}, bf16[2,64,1024]{2,1,0:T(8,128)(2,1)S(1)}, u32[]{:S(2)}, u32[]{:S(2)}) collective-permute-start(bf16[2,64,1024]{2,1,0:T(8,128)(2,1)S(1)} %get-tuple-element.67), channel_id=1, source_target_pairs={{0,32},{32,64},{64,96},{96,0},{1,33},{33,65},{65,97},{97,1},{2,34}... | collective-permute-start | bytes 786440 | tf_op jit(solution)/shard_map/ppermute | solution.py:20
  51.0 7.2 %collective-permute-start.7 = (bf16[2,64,1024]{2,1,0:T(8,128)(2,1)S(1)}, bf16[2,64,1024]{2,1,0:T(8,128)(2,1)S(1)}, u32[]{:S(2)}, u32[]{:S(2)}) collective-permute-start(bf16[2,64,1024]{2,1,0:T(8,128)(2,1)S(1)} %get-tuple-element.68), channel_id=1, source_target_pairs={{0,96},{32,0},{64,32},{96,64},{1,97},{33,1},{65,33},{97,65},{2,98}... | collective-permute-start | bytes 786440 | tf_op jit(solution)/shard_map/ppermute | solution.py:20
  53.0 8.6 %collective-permute-start.14 = (bf16[2,64,1024]{2,1,0:T(8,128)(2,1)S(1)}, bf16[2,64,1024]{2,1,0:T(8,128)(2,1)S(1)}, u32[]{:S(2)}, u32[]{:S(2)}) collective-permute-start(bf16[2,64,1024]{2,1,0:T(8,128)(2,1)S(1)} %get-tuple-element.79), channel_id=1, source_target_pairs={{0,8},{8,16},{16,24},{24,0},{1,9},{9,17},{17,25},{25,1},{2,10},{10... | collective-permute-start | bytes 786440 | tf_op jit(solution)/shard_map/ppermute | solution.py:20
  53.7 7.9 %collective-permute-start.15 = (bf16[2,64,1024]{2,1,0:T(8,128)(2,1)S(1)}, bf16[2,64,1024]{2,1,0:T(8,128)(2,1)S(1)}, u32[]{:S(2)}, u32[]{:S(2)}) collective-permute-start(bf16[2,64,1024]{2,1,0:T(8,128)(2,1)S(1)} %get-tuple-element.80), channel_id=1, source_target_pairs={{0,24},{8,0},{16,8},{24,16},{1,25},{9,1},{17,9},{25,17},{2,26},{10... | collective-permute-start | bytes 786440 | tf_op jit(solution)/shard_map/ppermute | solution.py:20
  55.3 22.9 %collective-permute-start.21 = (bf16[256,640]{1,0:T(8,128)(2,1)}, bf16[256,640]{1,0:T(8,128)(2,1)S(1)}, u32[]{:S(2)}, u32[]{:S(2)}) collective-permute-start(bf16[256,640]{1,0:T(8,128)(2,1)} %collective-permute-done.3.refs_4_), channel_id=1, source_target_pairs={{0,2},{2,4},{4,6},{6,0},{1,3},{3,5},{5,7},{7,1},{8,10},{10,12},{12... | collective-permute-start | bytes 983048 | tf_op jit(solution)/shard_map/ppermute | solution.py:20
  58.3 6.3 %collective-permute-start.8 = (bf16[1,64,1024]{2,1,0:T(8,128)(2,1)S(1)}, bf16[1,64,1024]{2,1,0:T(8,128)(2,1)S(1)}, u32[]{:S(2)}, u32[]{:S(2)}) collective-permute-start(bf16[1,64,1024]{2,1,0:T(8,128)(2,1)S(1)} %get-tuple-element.70), channel_id=1, source_target_pairs={{0,32},{32,64},{64,96},{96,0},{1,33},{33,65},{65,97},{97,1},{2,34}... | collective-permute-start | bytes 393224 | tf_op jit(solution)/shard_map/ppermute | solution.py:20
  60.1 5.0 %collective-permute-start.9 = (bf16[1,64,1024]{2,1,0:T(8,128)(2,1)S(1)}, bf16[1,64,1024]{2,1,0:T(8,128)(2,1)S(1)}, u32[]{:S(2)}, u32[]{:S(2)}) collective-permute-start(bf16[1,64,1024]{2,1,0:T(8,128)(2,1)S(1)} %get-tuple-element.71), channel_id=1, source_target_pairs={{0,96},{32,0},{64,32},{96,64},{1,97},{33,1},{65,33},{97,65},{2,98}... | collective-permute-start | bytes 393224 | tf_op jit(solution)/shard_map/ppermute | solution.py:20
  61.6 16.0 %copy-start.3 = (bf16[256,640]{1,0:T(8,128)(2,1)S(1)}, bf16[256,640]{1,0:T(8,128)(2,1)}, u32[]{:S(2)}) copy-start(bf16[256,640]{1,0:T(8,128)(2,1)} %copy-done.2) | copy-start | bytes 983044
  61.7 5.0 %collective-permute-start.16 = (bf16[1,64,1024]{2,1,0:T(8,128)(2,1)S(1)}, bf16[1,64,1024]{2,1,0:T(8,128)(2,1)S(1)}, u32[]{:S(2)}, u32[]{:S(2)}) collective-permute-start(bf16[1,64,1024]{2,1,0:T(8,128)(2,1)S(1)} %get-tuple-element.82), channel_id=1, source_target_pairs={{0,8},{8,16},{16,24},{24,0},{1,9},{9,17},{17,25},{25,1},{2,10},{10... | collective-permute-start | bytes 393224 | tf_op jit(solution)/shard_map/ppermute | solution.py:20
  62.3 6.2 %collective-permute-start.17 = (bf16[1,64,1024]{2,1,0:T(8,128)(2,1)S(1)}, bf16[1,64,1024]{2,1,0:T(8,128)(2,1)S(1)}, u32[]{:S(2)}, u32[]{:S(2)}) collective-permute-start(bf16[1,64,1024]{2,1,0:T(8,128)(2,1)S(1)} %get-tuple-element.83), channel_id=1, source_target_pairs={{0,24},{8,0},{16,8},{24,16},{1,25},{9,1},{17,9},{25,17},{2,26},{10... | collective-permute-start | bytes 393224 | tf_op jit(solution)/shard_map/ppermute | solution.py:20
  69.4 23.8 %all-to-all-start = ((bf16[16,128,128]{2,1,0:T(8,128)(2,1)}), bf16[16,128,128]{2,1,0:T(8,128)(2,1)S(1)}, u32[]{:S(2)}, u32[]{:S(2)}) async-start(bf16[16,128,128]{2,1,0:T(8,128)(2,1)} %pieces.1), calls=%async_computation | async-start | bytes 1048576 | tf_op jit(solution)/shard_map/all_to_all | solution.py:525
  77.2 1.9 %collective-permute-start.18 = (bf16[256,640]{1,0:T(8,128)(2,1)S(1)}, bf16[256,640]{1,0:T(8,128)(2,1)S(1)}, u32[]{:S(2)}, u32[]{:S(2)}) collective-permute-start(bf16[256,640]{1,0:T(8,128)(2,1)S(1)} %trim.1.refs_0_), channel_id=1, source_target_pairs={{0,1},{1,0},{2,3},{3,2},{4,5},{5,4},{6,7},{7,6},{8,9},{9,8},{10,11... | collective-permute-start | bytes 983048 | tf_op jit(solution)/shard_map/ppermute | solution.py:25
  77.6 1.8 %collective-permute-start.19 = (bf16[256,640]{1,0:T(8,128)(2,1)S(1)}, bf16[256,640]{1,0:T(8,128)(2,1)S(1)}, u32[]{:S(2)}, u32[]{:S(2)}) collective-permute-start(bf16[256,640]{1,0:T(8,128)(2,1)S(1)} %copy-done.3), channel_id=1, source_target_pairs={{0,1},{1,0},{2,3},{3,2},{4,5},{5,4},{6,7},{7,6},{8,9},{9,8},{10,11... | collective-permute-start | bytes 983048 | tf_op jit(solution)/shard_map/ppermute | solution.py:25
  77.8 2.7 %collective-permute-start.20 = (bf16[256,640]{1,0:T(8,128)(2,1)}, bf16[256,640]{1,0:T(8,128)(2,1)S(1)}, u32[]{:S(2)}, u32[]{:S(2)}) collective-permute-start(bf16[256,640]{1,0:T(8,128)(2,1)} %collective-permute-done.3.refs_4_), channel_id=1, source_target_pairs={{0,1},{1,0},{2,3},{3,2},{4,5},{5,4},{6,7},{7,6},{8,9},{9,8},{10,11... | collective-permute-start | bytes 983048 | tf_op jit(solution)/shard_map/ppermute | solution.py:25
  78.2 2.4 %collective-permute-start.22 = (bf16[256,640]{1,0:T(8,128)(2,1)S(1)}, bf16[256,640]{1,0:T(8,128)(2,1)S(1)}, u32[]{:S(2)}, u32[]{:S(2)}) collective-permute-start(bf16[256,640]{1,0:T(8,128)(2,1)S(1)} %collective-permute-done.21.refs_6_), channel_id=1, source_target_pairs={{0,1},{1,0},{2,3},{3,2},{4,5},{5,4},{6,7},{7,6},{8,9},{9,8},{10,11... | collective-permute-start | bytes 983048 | tf_op jit(solution)/shard_map/ppermute | solution.py:25
  94.7 14.5 %all-to-all-start.1 = ((bf16[8,128,128]{2,1,0:T(8,128)(2,1)}), bf16[8,128,128]{2,1,0:T(8,128)(2,1)S(1)}, u32[]{:S(2)}, u32[]{:S(2)}) async-start(bf16[8,128,128]{2,1,0:T(8,128)(2,1)} %copy-done.15), calls=%async_computation.1 | async-start | bytes 524288 | tf_op jit(solution)/shard_map/all_to_all | solution.py:528
  110.7 1.3 %collective-permute-start.23 = (f32[16,128]{1,0:T(8,128)S(1)}, f32[16,128]{1,0:T(8,128)S(1)}, u32[]{:S(2)}, u32[]{:S(2)}) collective-permute-start(f32[16,128]{1,0:T(8,128)S(1)} %get-tuple-element.105), channel_id=1, source_target_pairs={{0,1},{1,0},{2,3},{3,2},{4,5},{5,4},{6,7},{7,6},{8,9},{9,8},{10,11... | collective-permute-start | bytes 24584 | tf_op jit(solution)/shard_map/ppermute | solution.py:25
  112.0 3.7 %collective-permute-start.26 = (f32[16,128]{1,0:T(8,128)S(1)}, f32[16,128]{1,0:T(8,128)S(1)}, u32[]{:S(2)}, u32[]{:S(2)}) collective-permute-start(f32[16,128]{1,0:T(8,128)S(1)} %add.27), channel_id=1, source_target_pairs={{0,6},{2,0},{4,2},{6,4},{1,7},{3,1},{5,3},{7,5},{8,14},{10,8},{12,... | collective-permute-start | bytes 24584 | tf_op jit(solution)/shard_map/ppermute | solution.py:20
  113.6 4.5 %collective-permute-start.25 = (f32[16,128]{1,0:T(8,128)S(1)}, f32[16,128]{1,0:T(8,128)S(1)}, u32[]{:S(2)}, u32[]{:S(2)}) collective-permute-start(f32[16,128]{1,0:T(8,128)S(1)} %add.27), channel_id=1, source_target_pairs={{0,4},{2,6},{4,0},{6,2},{1,5},{3,7},{5,1},{7,3},{8,12},{10,14},{12... | collective-permute-start | bytes 24584 | tf_op jit(solution)/shard_map/ppermute | solution.py:20
  113.6 5.4 %collective-permute-start.24 = (f32[16,128]{1,0:T(8,128)S(1)}, f32[16,128]{1,0:T(8,128)S(1)}, u32[]{:S(2)}, u32[]{:S(2)}) collective-permute-start(f32[16,128]{1,0:T(8,128)S(1)} %add.27), channel_id=1, source_target_pairs={{0,2},{2,4},{4,6},{6,0},{1,3},{3,5},{5,7},{7,1},{8,10},{10,12},{12... | collective-permute-start | bytes 24584 | tf_op jit(solution)/shard_map/ppermute | solution.py:20
  (13 other events, 11.4 us)
where the time goes:
time: 121 us; the launch traced here: 120 us
  starting transfers between devices  42.3 us (35%)
  waiting for transfers between devices  35.7 us (30%)
  Pallas kernels  26.3 us (22%)
  local copies, waits for them, and re-layouts  14.8 us (12%)
    ppermute x22, waiting for transfers between devices, shift(): lax.ppermute(array, axis, [(i, (i + step) % size) for i in range(size)])  30.8 us
    ppermute x22, starting transfers between devices, shift(): lax.ppermute(array, axis, [(i, (i + step) % size) for i in range(size)])  28.5 us
    pallas_call x15, Pallas kernels, call(): pl.pallas_call(kernel, out_shape=out_shape, in_specs=in_specs, out_specs=...  26.3 us
    unnamed x32, local copies, waits for them, and re-layouts  14.8 us
    all_to_all x1, starting transfers between devices, local(): lax.all_to_all(pieces, ('zh',) + owner, split_axis=0, concat_axis=0, tile...  7.79 us
    all_to_all x1, starting transfers between devices, local(): lax.all_to_all(mixed, owner, split_axis=0, concat_axis=0, tiled=True)  4.79 us
    ppermute x5, waiting for transfers between devices, swap(): return lax.ppermute(array, axis, [(i, i ^ mask) for i in range(size)])  2.57 us
  transfers between devices with their start and end apart: 29, of which 17 were waited for; matrix products, arithmetic and copies ran while one was open for 0% of the time, Pallas kernels for 15%

commit v1 on v0

--- a/solution.py
+++ b/solution.py
@@ -77,7 +77,7 @@
     return last_up, last_down
 
 
-def turn_kernel(place_ref, own_ref, up_ref, down_ref, last_up_ref, last_down_ref, next_up, next_down, next_mid, next_own, sum_ref):
+def turn_kernel(which, place_ref, own_ref, up_ref, down_ref, last_up_ref, last_down_ref, next_up, next_down, next_mid, next_own, sum_ref):
     rows = own_ref.shape[1]
     half = rows // 2
     for block in range(2):
@@ -86,7 +86,7 @@
             sum_ref[block, at] = narrow(own_ref[block, at], last_up_ref[block, at], down_ref[2 + block, at])
             sum_ref[2 + block, at] = narrow(own_ref[2 + block, at], up_ref[2 + block, at], last_down_ref[block, at])
     low, high = pl.ds(0, half), pl.ds(half, half)
-    here = place_ref[0]
+    here = place_ref[which]
     ahead, across, behind = (lax.rem(here + step, 4) for step in (1, 2, 3))
     next_up[0] = sum_ref[across, low]
     next_up[1] = sum_ref[ahead, high]
@@ -98,11 +98,11 @@
     next_own[1] = sum_ref[here, high]
 
 
-def turn(place, own, up, down, last_up, last_down):
+def turn(which, place, own, up, down, last_up, last_down):
     rows, size = own.shape[1:]
     part = jax.ShapeDtypeStruct((2, rows // 2, size), own.dtype)
     return call(
-        turn_kernel,
+        functools.partial(turn_kernel, which),
         "turn",
         (part,) * 4,
         [SMEM] + [VMEM] * 5,
@@ -158,16 +158,17 @@
     return tuple(lax.rem(place_ref[which] + step, 4) for step in range(4))
 
 
-def trim_kernel(index_ref, stats_ref, out_ref):
+def trim_kernel(place_ref, table_ref, stats_ref, out_ref):
     rows = stats_ref.shape[0]
     half = rows // 2
+    slot = lax.rem(2 * place_ref[2] + place_ref[3] + 8 - table_ref[0], 4)
 
     def block(at):
         return pl.ds(at % 4 * rows, rows)
 
     for index in range(4):
 
-        @pl.when(index_ref[0] == index)
+        @pl.when(slot == index)
         def _():
             out_ref[:, block(0)] = stats_ref[:, block(index)].astype(jnp.bfloat16)
             out_ref[:, block(1)] = stats_ref[:, block(index + 1)].astype(jnp.bfloat16)
@@ -178,10 +179,10 @@
             out_ref[:, pl.ds(2 * rows, half)] = opposite.astype(jnp.bfloat16)
 
 
-def trim(index, stats):
+def trim(place, table, stats):
     rows = stats.shape[0]
     out = jax.ShapeDtypeStruct((rows, 2 * rows + rows // 2), jnp.bfloat16)
-    return call(trim_kernel, "trim", out, [SMEM, VMEM], (index, stats), flops=stats.size, moved=6 * stats.size)
+    return call(trim_kernel, "trim", out, [SMEM, SMEM, VMEM], (place, table, stats), flops=stats.size, moved=6 * stats.size)
 
 
 def send_kernel(place_ref, grads_ref, x_up, x_down, y_up, y_down, sems):
@@ -230,25 +231,29 @@
     )
 
 
-def root_kernel(where_ref, *refs):
-    given, (out_ref, slots_ref, start_ref, first_ref, second_ref, third_ref) = refs[:8], refs[8:]
+def root_kernel(place_ref, table_ref, *refs):
+    given, (out_ref, right_ref, slots_ref, rights_ref, start_ref, first_ref, second_ref, third_ref, sem) = refs[:8], refs[8:]
     size = out_ref.shape[0]
     slot = size // 4
     half = slot // 2
-    offset, zl, c = where_ref[0], where_ref[1], where_ref[2]
+    offset, zl, c = table_ref[0], place_ref[2], place_ref[3]
 
     def span(tile):
         return pl.ds(tile * slot, slot)
 
-    for tile in range(4):
-        position = lax.rem(offset + tile, 8)
-        back = lax.rem(zl + 4 - lax.div(position, 2), 4)
-        source = 2 * back + lax.rem(position + c, 2)
-        for i, ref in enumerate(given):
-
-            @pl.when(source == i)
-            def _():
-                slots_ref[tile] = ref[...]
+    for first_tile, to_ref in ((4, rights_ref), (0, slots_ref)):
+        for tile in range(4):
+            position = lax.rem(offset + first_tile + tile, 8)
+            back = lax.rem(zl + 4 - lax.div(position, 2), 4)
+            source = 2 * back + lax.rem(position + c, 2)
+            for i, ref in enumerate(given):
+
+                @pl.when(source == i)
+                def _():
+                    to_ref[tile] = ref[...]
+
+    passed = pltpu.make_async_copy(rights_ref, right_ref, sem)
+    passed.start()
 
     total = jnp.zeros((8, slot // 2), jnp.float32)
     for tile in range(4):
@@ -292,42 +297,33 @@
     for tile in range(4):
         product = jnp.dot(third_ref[span(tile), :], first_ref[...], preferred_element_type=jnp.float32)
         out_ref[span(tile), :] = product.astype(jnp.bfloat16)
-
-
-def left_inverse_root(where, slots):
+    passed.wait()
+
+
+def left_inverse_root(place, table, slots):
     rows, kept = slots[0].shape
     size = 4 * rows
-    return call(
+    matrix, side = (size, size), (4, rows, kept)
+    return pl.pallas_call(
         root_kernel,
-        "left_root",
-        jax.ShapeDtypeStruct((size, size), jnp.bfloat16),
-        [SMEM] + [VMEM] * 8,
-        (where,) + slots,
-        scratch=[pltpu.VMEM((4, rows, kept), jnp.bfloat16)] + [pltpu.VMEM((size, size), jnp.bfloat16)] * 4,
-        flops=6 * size**3,
-        moved=4 * size * size,
-    )
-
-
-def base_kernel(where_ref, *refs):
-    given, (first_ref, diagonal_ref, slots_ref) = refs[:8], refs[8:]
+        out_shape=(jax.ShapeDtypeStruct(matrix, jnp.bfloat16), jax.ShapeDtypeStruct(side, jnp.bfloat16)),
+        in_specs=[SMEM] * 2 + [VMEM] * 8,
+        out_specs=(VMEM, HBM),
+        scratch_shapes=[pltpu.VMEM(side, jnp.bfloat16)] * 2
+        + [pltpu.VMEM(matrix, jnp.bfloat16)] * 4
+        + [pltpu.SemaphoreType.DMA(())],
+        compiler_params=pltpu.CompilerParams(vmem_limit_bytes=18 * 2**20),
+        cost_estimate=pl.CostEstimate(flops=6 * size**3, bytes_accessed=4 * size * size, transcendentals=0),
+        name="left_root",
+    )(place, table, *slots)
+
+
+def base_kernel(slots_ref, first_ref, diagonal_ref):
     size = first_ref.shape[0]
     slot = size // 4
-    half = slot // 2
-    offset, zl, c = where_ref[0], where_ref[1], where_ref[2]
 
     def span(tile):
         return pl.ds(tile * slot, slot)
-
-    for tile in range(4):
-        position = lax.rem(offset + (4 + tile), 8)
-        back = lax.rem(zl + 4 - lax.div(position, 2), 4)
-        source = 2 * back + lax.rem(position + c, 2)
-        for i, ref in enumerate(given):
-
-            @pl.when(source == i)
-            def _():
-                slots_ref[tile] = ref[...]
 
     total = jnp.zeros((8, slot // 2), jnp.float32)
     for tile in range(4):
@@ -362,19 +358,14 @@
         place(tile + 2, tile, normed.T)
 
 
-def right_base(where, slots):
-    rows, kept = slots[0].shape
-    size = 4 * rows
+def right_base(slots):
+    size = 4 * slots.shape[1]
     return call(
         base_kernel,
         "right_base",
-        (
-            jax.ShapeDtypeStruct((size, size), jnp.bfloat16),
-            jax.ShapeDtypeStruct((8, size), jnp.float32),
-        ),
-        [SMEM] + [VMEM] * 8,
-        (where,) + slots,
-        scratch=[pltpu.VMEM((4, rows, kept), jnp.bfloat16)],
+        (jax.ShapeDtypeStruct((size, size), jnp.bfloat16), jax.ShapeDtypeStruct((8, size), jnp.float32)),
+        [VMEM],
+        (slots,),
         flops=4 * size * size,
         moved=4 * size * size,
     )
@@ -489,17 +480,16 @@
     rows_here = grad_partial.shape[2]
     owner = ("zl", "c")
     grads = grad_partial.reshape(2, 4, 4, rows_here, size)
-    zh, y, x, zl, c = (lax.axis_index(axis).astype(jnp.int32) for axis in FINE)
-    place = jnp.stack((x, y))
+    place = jnp.stack([lax.axis_index(axis).astype(jnp.int32) for axis in ("x", "y", "zl", "c")])
 
     x_up, x_down, y_up, y_down = pack(send_kernel, 48, place, grads)
     x_ends = ring_first(x_up, x_down, "x")
     y_ends = ring_first(y_up, y_down, "y")
 
-    place, table = after(x_up, place, owner_table)
-    near = [trim((2 * zl + c - table + 8) % 4, factor_stats[0, 0])]
+    (sent,) = after(x_up, place)
+    near = [trim(sent, owner_table, factor_stats[0, 0])]
     near.append(shift(near[0], "zl", 1))
-    x_mid, x_own, y_mid, y_own = pack(keep_kernel, 16, place, grads)
+    x_mid, x_own, y_mid, y_own = pack(keep_kernel, 16, sent, grads)
     near.append(shift(*after(x_mid, near[1]), "zl", 1))
     near.append(shift(near[2], "zl", 1))
     (x_mid,) = after(near[2], x_mid)
@@ -508,14 +498,13 @@
     far = [swap(each, "c", 1) for each in near[:3]]
     far.append(swap(*after(x_last[0], near[3]), "c", 1))
     slots = tuple(each for pair in zip(near, far) for each in pair)
-    where = jnp.stack((table[0], zl, c))
 
     x_last = ring_first(*x_last, "x")
     y_last = ring_first(*y_last, "y")
 
-    lower_up, lower_down, lower_mid, lower_own = turn(y[None], x_own, *x_ends, *x_last)
+    lower_up, lower_down, lower_mid, lower_own = turn(1, place, x_own, *x_ends, *x_last)
     lower_ends = ring_first(lower_up, lower_down, "y")
-    upper_up, upper_down, upper_mid, upper_own = turn(x[None], y_own, *y_ends, *y_last)
+    upper_up, upper_down, upper_mid, upper_own = turn(0, place, y_own, *y_ends, *y_last)
     upper_ends = ring_first(upper_up, upper_down, "x")
     lower_last = ring_first(*pass_on(lower_mid, *lower_ends), "y")
     upper_last = ring_first(*pass_on(upper_mid, *upper_ends), "x")
@@ -523,8 +512,9 @@
 
     slots = after(pieces, *slots)
     pieces = lax.all_to_all(pieces, ("zh",) + owner, split_axis=0, concat_axis=0, tiled=True)
-    mixed, energy = mix(pieces, left_inverse_root(where, slots))
-    right = right_base(where, after(mixed, *slots))
+    left_root, right_slots = left_inverse_root(place, owner_table, slots)
+    mixed, energy = mix(pieces, left_root)
+    right = right_base(*after(mixed, right_slots))
     mixed = lax.all_to_all(mixed, owner, split_axis=0, concat_axis=0, tiled=True)
     precond, totals = condition(mixed, *right, energy)
     totals = totals + swap(totals, "c", 1)

time: 121 us -> 118 us (0.975)
  waiting for transfers between devices: 35.7 us -> 46.8 us
  local copies, waits for them, and re-layouts: 14.8 us -> 6.31 us
  Pallas kernels: 26.3 us -> 23.1 us
  starting transfers between devices: 42.3 us -> 39.2 us
    pallas_call x15 -> x14, Pallas kernels: 26.3 us -> 14.5 us  [call(): pl.pallas_call(kernel, out_shape=out_shape, in_specs=in_specs, out_specs=...]
    pallas_call x0 -> x1, Pallas kernels: none -> 8.61 us  [left_inverse_root(): pl.pallas_call(root_kernel, out_shape=(jax.ShapeDtypeStruct(matrix, jnp.b...]
    unnamed x32 -> x16, local copies, waits for them, and re-layouts: 14.8 us -> 6.31 us
    ppermute x22, waiting for transfers between devices: 30.8 us -> 36.1 us  [shift(): lax.ppermute(array, axis, [(i, (i + step) % size) for i in range(size)])]
    all_to_all x1, waiting for transfers between devices: 2.2 us -> 7.01 us  [local(): lax.all_to_all(mixed, owner, split_axis=0, concat_axis=0, tiled=True)]
    ppermute x22, starting transfers between devices: 28.5 us -> 27 us  [shift(): lax.ppermute(array, axis, [(i, (i + step) % size) for i in range(size)])]
  transfers between devices with their start and end apart: 29 -> 29, of which waited for: 17 -> 18; matrix products, arithmetic and copies ran while one was open for 0% -> 0% of each run, Pallas kernels for 15% -> 13%
where the time goes in v1:
time: 118 us; the launch traced here: 116 us
  waiting for transfers between devices  46.8 us (40%)
  starting transfers between devices  39.2 us (33%)
  Pallas kernels  23.1 us (20%)
  local copies, waits for them, and re-layouts  6.31 us (5%)
    ppermute x22, waiting for transfers between devices, shift(): lax.ppermute(array, axis, [(i, (i + step) % size) for i in range(size)])  36.1 us
    ppermute x22, starting transfers between devices, shift(): lax.ppermute(array, axis, [(i, (i + step) % size) for i in range(size)])  27 us
    pallas_call x14, Pallas kernels, call(): pl.pallas_call(kernel, out_shape=out_shape, in_specs=in_specs, out_specs=...  14.5 us
    pallas_call x1, Pallas kernels, left_inverse_root(): pl.pallas_call(root_kernel, out_shape=(jax.ShapeDtypeStruct(matrix, jnp.b...  8.61 us
    all_to_all x1, waiting for transfers between devices, local(): lax.all_to_all(mixed, owner, split_axis=0, concat_axis=0, tiled=True)  7.01 us
    all_to_all x1, starting transfers between devices, local(): lax.all_to_all(pieces, ('zh',) + owner, split_axis=0, concat_axis=0, tile...  6.97 us
    unnamed x16, local copies, waits for them, and re-layouts  6.31 us
    all_to_all x1, starting transfers between devices, local(): lax.all_to_all(mixed, owner, split_axis=0, concat_axis=0, tiled=True)  3.99 us
  transfers between devices with their start and end apart: 29, of which 18 were waited for; matrix products, arithmetic and copies ran while one was open for 0% of the time, Pallas kernels for 13%

profile of v1, /device:TPU:6, one launch (start us, length us, event | category | flops | bytes accessed | tf_op | source)
XLA Modules:
  0.0 116.3 jit_solution(12021873975101547187)
XLA Ops:
  0.1 3.5 %send.1 = (bf16[4,128,1024]{2,1,0:T(8,128)(2,1)S(1)}, bf16[4,128,1024]{2,1,0:T(8,128)(2,1)S(1)}, bf16[4,128,1024]{2,1,0:T(8,128)(2,1)S(1)}, bf16[4,128,1024]{2,1,0:T(8,128)(2,1)S(1)}) custom-call(s32[4]{0:T(128)S(1)} %pad_add_fusion.place_ref, bf16[2,4,4,128,1024]{4,3,2,1,0:T(8,128)(2,1)} %bitcast.7), custom_call_target="tpu_custom_call" | custom-call | bytes 8388608 | tf_op jit(solution)/shard_map/send/pallas_call | solution.py:46
  3.6 2.3 %collective-permute-start = (bf16[4,128,1024]{2,1,0:T(8,128)(2,1)S(1)}, bf16[4,128,1024]{2,1,0:T(8,128)(2,1)S(1)}, u32[]{:S(2)}, u32[]{:S(2)}) collective-permute-start(bf16[4,128,1024]{2,1,0:T(8,128)(2,1)S(1)} %get-tuple-element.50), channel_id=1, source_target_pairs={{0,8},{8,16},{16,24},{24,0},{1,9},{9,17},{17,25},{25,1},{2,10},{10... | collective-permute-start | bytes 3145736 | tf_op jit(solution)/shard_map/ppermute | solution.py:20
  5.9 1.4 %collective-permute-start.10 = (bf16[4,128,1024]{2,1,0:T(8,128)(2,1)S(1)}, bf16[4,128,1024]{2,1,0:T(8,128)(2,1)S(1)}, u32[]{:S(2)}, u32[]{:S(2)}) collective-permute-start(bf16[4,128,1024]{2,1,0:T(8,128)(2,1)S(1)} %get-tuple-element.66), channel_id=1, source_target_pairs={{0,32},{32,64},{64,96},{96,0},{1,33},{33,65},{65,97},{97,1},{2,34}... | collective-permute-start | bytes 3145736 | tf_op jit(solution)/shard_map/ppermute | solution.py:20
  7.3 1.9 %collective-permute-start.11 = (bf16[4,128,1024]{2,1,0:T(8,128)(2,1)S(1)}, bf16[4,128,1024]{2,1,0:T(8,128)(2,1)S(1)}, u32[]{:S(2)}, u32[]{:S(2)}) collective-permute-start(bf16[4,128,1024]{2,1,0:T(8,128)(2,1)S(1)} %get-tuple-element.67), channel_id=1, source_target_pairs={{0,96},{32,0},{64,32},{96,64},{1,97},{33,1},{65,33},{97,65},{2,98}... | collective-permute-start | bytes 3145736 | tf_op jit(solution)/shard_map/ppermute | solution.py:20
  9.8 1.2 %copy-done.3 = f32[1,1,256,1024]{3,2,1,0:T(8,128)S(1)} copy-done((f32[1,1,256,1024]{3,2,1,0:T(8,128)S(1)}, f32[1,1,256,1024]{3,2,1,0:T(8,128)}, u32[]{:S(2)}) %copy-start.3) | copy-done | bytes 1048600
  11.6 1.9 %collective-permute-start.2 = (bf16[256,640]{1,0:T(8,128)(2,1)S(1)}, bf16[256,640]{1,0:T(8,128)(2,1)S(1)}, u32[]{:S(2)}, u32[]{:S(2)}) collective-permute-start(bf16[256,640]{1,0:T(8,128)(2,1)S(1)} %trim.1.refs_0_), channel_id=1, source_target_pairs={{0,2},{2,4},{4,6},{6,0},{1,3},{3,5},{5,7},{7,1},{8,10},{10,12},{12... | collective-permute-start | bytes 983048 | tf_op jit(solution)/shard_map/ppermute | solution.py:20
  13.5 1.4 %keep.1 = (bf16[4,128,1024]{2,1,0:T(8,128)(2,1)S(1)}, bf16[4,128,1024]{2,1,0:T(8,128)(2,1)S(1)}, bf16[4,128,1024]{2,1,0:T(8,128)(2,1)S(1)}, bf16[4,128,1024]{2,1,0:T(8,128)(2,1)S(1)}) custom-call(s32[4]{0:T(128)S(1)} %pad_add_fusion.place_ref, bf16[2,4,4,128,1024]{4,3,2,1,0:T(8,128)(2,1)S(1)} %bitcast.8), custom_call_target="tpu_custom_call" | custom-call | bytes 8388608 | tf_op jit(solution)/shard_map/keep/pallas_call | solution.py:46
  14.9 7.9 %collective-permute-done.2.refs_2_ = bf16[256,640]{1,0:T(8,128)(2,1)S(1)} collective-permute-done((bf16[256,640]{1,0:T(8,128)(2,1)S(1)}, bf16[256,640]{1,0:T(8,128)(2,1)S(1)}, u32[]{:S(2)}, u32[]{:S(2)}) %collective-permute-start.2) | collective-permute-done | bytes 327712 | tf_op jit(solution)/shard_map/ppermute | solution.py:20
  22.8 9.5 %collective-permute-done.3.refs_4_ = bf16[256,640]{1,0:T(8,128)(2,1)S(1)} collective-permute-done((bf16[256,640]{1,0:T(8,128)(2,1)S(1)}, bf16[256,640]{1,0:T(8,128)(2,1)S(1)}, u32[]{:S(2)}, u32[]{:S(2)}) %collective-permute-start.3) | collective-permute-done | bytes 327712 | tf_op jit(solution)/shard_map/ppermute | solution.py:20
  35.2 3.1 %collective-permute-start.13 = (bf16[2,128,1024]{2,1,0:T(8,128)(2,1)S(1)}, bf16[2,128,1024]{2,1,0:T(8,128)(2,1)S(1)}, u32[]{:S(2)}, u32[]{:S(2)}) collective-permute-start(bf16[2,128,1024]{2,1,0:T(8,128)(2,1)S(1)} %get-tuple-element.70), channel_id=1, source_target_pairs={{0,96},{32,0},{64,32},{96,64},{1,97},{33,1},{65,33},{97,65},{2,98}... | collective-permute-start | bytes 1572872 | tf_op jit(solution)/shard_map/ppermute | solution.py:20
  38.3 5.4 %collective-permute-done.4.last_up_ref = bf16[2,128,1024]{2,1,0:T(8,128)(2,1)S(1)} collective-permute-done((bf16[2,128,1024]{2,1,0:T(8,128)(2,1)S(1)}, bf16[2,128,1024]{2,1,0:T(8,128)(2,1)S(1)}, u32[]{:S(2)}, u32[]{:S(2)}) %collective-permute-start.4) | collective-permute-done | bytes 524320 | tf_op jit(solution)/shard_map/ppermute | solution.py:20
  43.8 1.3 %collective-permute-done.5.last_down_ref = bf16[2,128,1024]{2,1,0:T(8,128)(2,1)S(1)} collective-permute-done((bf16[2,128,1024]{2,1,0:T(8,128)(2,1)S(1)}, bf16[2,128,1024]{2,1,0:T(8,128)(2,1)S(1)}, u32[]{:S(2)}, u32[]{:S(2)}) %collective-permute-start.5) | collective-permute-done | bytes 524320 | tf_op jit(solution)/shard_map/ppermute | solution.py:20
  46.1 1.7 %collective-permute-start.6 = (bf16[2,64,1024]{2,1,0:T(8,128)(2,1)S(1)}, bf16[2,64,1024]{2,1,0:T(8,128)(2,1)S(1)}, u32[]{:S(2)}, u32[]{:S(2)}) collective-permute-start(bf16[2,64,1024]{2,1,0:T(8,128)(2,1)S(1)} %get-tuple-element.60), channel_id=1, source_target_pairs={{0,32},{32,64},{64,96},{96,0},{1,33},{33,65},{65,97},{97,1},{2,34}... | collective-permute-start | bytes 786440 | tf_op jit(solution)/shard_map/ppermute | solution.py:20
  47.8 1.6 %collective-permute-start.7 = (bf16[2,64,1024]{2,1,0:T(8,128)(2,1)S(1)}, bf16[2,64,1024]{2,1,0:T(8,128)(2,1)S(1)}, u32[]{:S(2)}, u32[]{:S(2)}) collective-permute-start(bf16[2,64,1024]{2,1,0:T(8,128)(2,1)S(1)} %get-tuple-element.61), channel_id=1, source_target_pairs={{0,96},{32,0},{64,32},{96,64},{1,97},{33,1},{65,33},{97,65},{2,98}... | collective-permute-start | bytes 786440 | tf_op jit(solution)/shard_map/ppermute | solution.py:20
  53.8 1.2 %collective-permute-done.7.down_ref.refs_2_ = bf16[2,64,1024]{2,1,0:T(8,128)(2,1)S(1)} collective-permute-done((bf16[2,64,1024]{2,1,0:T(8,128)(2,1)S(1)}, bf16[2,64,1024]{2,1,0:T(8,128)(2,1)S(1)}, u32[]{:S(2)}, u32[]{:S(2)}) %collective-permute-start.7) | collective-permute-done | bytes 262176 | tf_op jit(solution)/shard_map/ppermute | solution.py:20
  55.1 1.8 %collective-permute-start.8 = (bf16[1,64,1024]{2,1,0:T(8,128)(2,1)S(1)}, bf16[1,64,1024]{2,1,0:T(8,128)(2,1)S(1)}, u32[]{:S(2)}, u32[]{:S(2)}) collective-permute-start(bf16[1,64,1024]{2,1,0:T(8,128)(2,1)S(1)} %get-tuple-element.63), channel_id=1, source_target_pairs={{0,32},{32,64},{64,96},{96,0},{1,33},{33,65},{65,97},{97,1},{2,34}... | collective-permute-start | bytes 393224 | tf_op jit(solution)/shard_map/ppermute | solution.py:20
  56.9 1.5 %collective-permute-start.9 = (bf16[1,64,1024]{2,1,0:T(8,128)(2,1)S(1)}, bf16[1,64,1024]{2,1,0:T(8,128)(2,1)S(1)}, u32[]{:S(2)}, u32[]{:S(2)}) collective-permute-start(bf16[1,64,1024]{2,1,0:T(8,128)(2,1)S(1)} %get-tuple-element.64), channel_id=1, source_target_pairs={{0,96},{32,0},{64,32},{96,64},{1,97},{33,1},{65,33},{97,65},{2,98}... | collective-permute-start | bytes 393224 | tf_op jit(solution)/shard_map/ppermute | solution.py:20
  60.1 1.6 %collective-permute-start.17 = (bf16[1,64,1024]{2,1,0:T(8,128)(2,1)S(1)}, bf16[1,64,1024]{2,1,0:T(8,128)(2,1)S(1)}, u32[]{:S(2)}, u32[]{:S(2)}) collective-permute-start(bf16[1,64,1024]{2,1,0:T(8,128)(2,1)S(1)} %get-tuple-element.76), channel_id=1, source_target_pairs={{0,24},{8,0},{16,8},{24,16},{1,25},{9,1},{17,9},{25,17},{2,26},{10... | collective-permute-start | bytes 393224 | tf_op jit(solution)/shard_map/ppermute | solution.py:20
  61.9 2.7 %collective-permute-done.16.refs_8_ = bf16[1,64,1024]{2,1,0:T(8,128)(2,1)S(1)} collective-permute-done((bf16[1,64,1024]{2,1,0:T(8,128)(2,1)S(1)}, bf16[1,64,1024]{2,1,0:T(8,128)(2,1)S(1)}, u32[]{:S(2)}, u32[]{:S(2)}) %collective-permute-start.16) | collective-permute-done | bytes 131104 | tf_op jit(solution)/shard_map/ppermute | solution.py:20
  64.6 1.7 %collective-permute-done.17.refs_9_ = bf16[1,64,1024]{2,1,0:T(8,128)(2,1)S(1)} collective-permute-done((bf16[1,64,1024]{2,1,0:T(8,128)(2,1)S(1)}, bf16[1,64,1024]{2,1,0:T(8,128)(2,1)S(1)}, u32[]{:S(2)}, u32[]{:S(2)}) %collective-permute-start.17) | collective-permute-done | bytes 131104 | tf_op jit(solution)/shard_map/ppermute | solution.py:20
  67.2 7.0 %all-to-all-start = ((bf16[16,128,128]{2,1,0:T(8,128)(2,1)}), bf16[16,128,128]{2,1,0:T(8,128)(2,1)S(1)}, u32[]{:S(2)}, u32[]{:S(2)}) async-start(bf16[16,128,128]{2,1,0:T(8,128)(2,1)} %pieces.1), calls=%async_computation | async-start | bytes 1048576 | tf_op jit(solution)/shard_map/all_to_all | solution.py:514
  79.3 8.6 %left_root.1 = (bf16[1024,1024]{1,0:T(8,128)(2,1)S(1)}, bf16[4,256,640]{2,1,0:T(8,128)(2,1)S(1)}) custom-call(s32[4]{0:T(128)S(1)} %pad_add_fusion.place_ref, s32[1]{0:T(128)S(6)} %copy.4.table_ref, bf16[256,640]{1,0:T(8,128)(2,1)S(1)} %trim.1.refs_0_, bf16[256,640]{1,0:T(8,128)(2,1)S(1)} %collective-permute-done.18.refs_1_, ...), custom_call_target="tpu_custom_call" | custom-call | flops 6442450944 | bytes 4194304 | tf_op jit(solution)/shard_map/left_root/pallas_call | solution.py:307
  89.0 1.2 %all-to-all-done.pieces_ref = bf16[16,128,128]{2,1,0:T(8,128)(2,1)S(1)} async-done(((bf16[16,128,128]{2,1,0:T(8,128)(2,1)}), bf16[16,128,128]{2,1,0:T(8,128)(2,1)S(1)}, u32[]{:S(2)}, u32[]{:S(2)}) %all-to-all-start) | async-done | bytes 524320 | tf_op jit(solution)/shard_map/all_to_all | solution.py:514
  90.2 1.5 %mix.1 = (bf16[8,128,128]{2,1,0:T(8,128)(2,1)}, f32[8,128]{1,0:T(8,128)S(1)}) custom-call(bf16[16,128,128]{2,1,0:T(8,128)(2,1)S(1)} %all-to-all-done.pieces_ref, bf16[1024,1024]{1,0:T(8,128)(2,1)S(1)} %get-tuple-element.86.left_ref), custom_call_target="tpu_custom_call" | custom-call | flops 268435456 | bytes 2097152 | tf_op jit(solution)/shard_map/mix/pallas_call | solution.py:46
  91.7 4.0 %all-to-all-start.1 = ((bf16[8,128,128]{2,1,0:T(8,128)(2,1)}), bf16[8,128,128]{2,1,0:T(8,128)(2,1)S(1)}, u32[]{:S(2)}, u32[]{:S(2)}) async-start(bf16[8,128,128]{2,1,0:T(8,128)(2,1)} %get-tuple-element.87), calls=%async_computation.1 | async-start | bytes 524288 | tf_op jit(solution)/shard_map/all_to_all | solution.py:518
  95.7 1.3 %copy-done.2 = bf16[4,256,640]{2,1,0:T(8,128)(2,1)S(1)} copy-done((bf16[4,256,640]{2,1,0:T(8,128)(2,1)S(1)}, bf16[4,256,640]{2,1,0:T(8,128)(2,1)}, u32[]{:S(2)}) %copy-start.2) | copy-done | bytes 1310744
  97.0 1.4 %right_base.1 = (bf16[1024,1024]{1,0:T(8,128)(2,1)S(1)}, f32[8,1024]{1,0:T(8,128)S(1)}) custom-call(bf16[4,256,640]{2,1,0:T(8,128)(2,1)S(1)} %copy-done.2), custom_call_target="tpu_custom_call" | custom-call | flops 4194304 | bytes 4194304 | tf_op jit(solution)/shard_map/right_base/pallas_call | solution.py:46
  98.4 7.0 %all-to-all-done.1.mixed_ref = bf16[8,128,128]{2,1,0:T(8,128)(2,1)S(1)} async-done(((bf16[8,128,128]{2,1,0:T(8,128)(2,1)}), bf16[8,128,128]{2,1,0:T(8,128)(2,1)S(1)}, u32[]{:S(2)}, u32[]{:S(2)}) %all-to-all-start.1) | async-done | bytes 262176 | tf_op jit(solution)/shard_map/all_to_all | solution.py:518
  105.5 1.4 %condition.1 = (f32[128,1024]{1,0:T(8,128)S(1)}, f32[16,128]{1,0:T(8,128)S(1)}) custom-call(bf16[8,128,128]{2,1,0:T(8,128)(2,1)S(1)} %all-to-all-done.1.mixed_ref, bf16[1024,1024]{1,0:T(8,128)(2,1)S(1)} %get-tuple-element.90.first_ref, f32[8,1024]{1,0:T(8,128)S(1)} %get-tuple-element.91.diagonal_ref, f32[8,128]{1,0:T(8,128)S(1)} %get-tuple-element.92.energy_ref), custom_call_target="tpu_custom_call" | custom-call | flops 1073741824 | bytes 2097152 | tf_op jit(solution)/shard_map/condition/pallas_call | solution.py:46
  108.1 1.4 %collective-permute-start.26 = (f32[16,128]{1,0:T(8,128)S(1)}, f32[16,128]{1,0:T(8,128)S(1)}, u32[]{:S(2)}, u32[]{:S(2)}) collective-permute-start(f32[16,128]{1,0:T(8,128)S(1)} %add.12), channel_id=1, source_target_pairs={{0,6},{2,0},{4,2},{6,4},{1,7},{3,1},{5,3},{7,5},{8,14},{10,8},{12,... | collective-permute-start | bytes 24584 | tf_op jit(solution)/shard_map/ppermute | solution.py:20
  110.2 1.6 %collective-permute-done.26 = f32[16,128]{1,0:T(8,128)S(1)} collective-permute-done((f32[16,128]{1,0:T(8,128)S(1)}, f32[16,128]{1,0:T(8,128)S(1)}, u32[]{:S(2)}, u32[]{:S(2)}) %collective-permute-start.26) | collective-permute-done | bytes 8224 | tf_op jit(solution)/shard_map/ppermute | solution.py:20
  111.8 2.4 %collective-permute-done.25 = f32[16,128]{1,0:T(8,128)S(1)} collective-permute-done((f32[16,128]{1,0:T(8,128)S(1)}, f32[16,128]{1,0:T(8,128)S(1)}, u32[]{:S(2)}, u32[]{:S(2)}) %collective-permute-start.25) | collective-permute-done | bytes 8224 | tf_op jit(solution)/shard_map/ppermute | solution.py:20
  (60 shorter events, 22.0 us)
Async XLA Ops:
  0.1 13.4 %copy-start = (bf16[1,32,128,1024]{3,2,1,0:T(8,128)(2,1)S(1)}, bf16[1,32,128,1024]{3,2,1,0:T(8,128)(2,1)}, u32[]{:S(2)}) copy-start(bf16[1,32,128,1024]{3,2,1,0:T(8,128)(2,1)} %param.3) | copy-start | bytes 25165828
  3.6 28.8 %collective-permute-start = (bf16[4,128,1024]{2,1,0:T(8,128)(2,1)S(1)}, bf16[4,128,1024]{2,1,0:T(8,128)(2,1)S(1)}, u32[]{:S(2)}, u32[]{:S(2)}) collective-permute-start(bf16[4,128,1024]{2,1,0:T(8,128)(2,1)S(1)} %get-tuple-element.50), channel_id=1, source_target_pairs={{0,8},{8,16},{16,24},{24,0},{1,9},{9,17},{17,25},{25,1},{2,10},{10... | collective-permute-start | bytes 3145736 | tf_op jit(solution)/shard_map/ppermute | solution.py:20
  5.9 26.5 %collective-permute-start.1 = (bf16[4,128,1024]{2,1,0:T(8,128)(2,1)S(1)}, bf16[4,128,1024]{2,1,0:T(8,128)(2,1)S(1)}, u32[]{:S(2)}, u32[]{:S(2)}) collective-permute-start(bf16[4,128,1024]{2,1,0:T(8,128)(2,1)S(1)} %get-tuple-element.53), channel_id=1, source_target_pairs={{0,24},{8,0},{16,8},{24,16},{1,25},{9,1},{17,9},{25,17},{2,26},{10... | collective-permute-start | bytes 3145736 | tf_op jit(solution)/shard_map/ppermute | solution.py:20
  5.9 28.9 %collective-permute-start.10 = (bf16[4,128,1024]{2,1,0:T(8,128)(2,1)S(1)}, bf16[4,128,1024]{2,1,0:T(8,128)(2,1)S(1)}, u32[]{:S(2)}, u32[]{:S(2)}) collective-permute-start(bf16[4,128,1024]{2,1,0:T(8,128)(2,1)S(1)} %get-tuple-element.66), channel_id=1, source_target_pairs={{0,32},{32,64},{64,96},{96,0},{1,33},{33,65},{65,97},{97,1},{2,34}... | collective-permute-start | bytes 3145736 | tf_op jit(solution)/shard_map/ppermute | solution.py:20
  7.3 27.5 %collective-permute-start.11 = (bf16[4,128,1024]{2,1,0:T(8,128)(2,1)S(1)}, bf16[4,128,1024]{2,1,0:T(8,128)(2,1)S(1)}, u32[]{:S(2)}, u32[]{:S(2)}) collective-permute-start(bf16[4,128,1024]{2,1,0:T(8,128)(2,1)S(1)} %get-tuple-element.67), channel_id=1, source_target_pairs={{0,96},{32,0},{64,32},{96,64},{1,97},{33,1},{65,33},{97,65},{2,98}... | collective-permute-start | bytes 3145736 | tf_op jit(solution)/shard_map/ppermute | solution.py:20
  11.6 11.2 %collective-permute-start.2 = (bf16[256,640]{1,0:T(8,128)(2,1)S(1)}, bf16[256,640]{1,0:T(8,128)(2,1)S(1)}, u32[]{:S(2)}, u32[]{:S(2)}) collective-permute-start(bf16[256,640]{1,0:T(8,128)(2,1)S(1)} %trim.1.refs_0_), channel_id=1, source_target_pairs={{0,2},{2,4},{4,6},{6,0},{1,3},{3,5},{5,7},{7,1},{8,10},{10,12},{12... | collective-permute-start | bytes 983048 | tf_op jit(solution)/shard_map/ppermute | solution.py:20
  22.8 9.5 %collective-permute-start.3 = (bf16[256,640]{1,0:T(8,128)(2,1)S(1)}, bf16[256,640]{1,0:T(8,128)(2,1)S(1)}, u32[]{:S(2)}, u32[]{:S(2)}) collective-permute-start(bf16[256,640]{1,0:T(8,128)(2,1)S(1)} %collective-permute-done.2.refs_2_), channel_id=1, source_target_pairs={{0,2},{2,4},{4,6},{6,0},{1,3},{3,5},{5,7},{7,1},{8,10},{10,12},{12... | collective-permute-start | bytes 983048 | tf_op jit(solution)/shard_map/ppermute | solution.py:20
  32.4 42.4 %copy-start.4 = (bf16[256,640]{1,0:T(8,128)(2,1)}, bf16[256,640]{1,0:T(8,128)(2,1)S(1)}, u32[]{:S(2)}) copy-start(bf16[256,640]{1,0:T(8,128)(2,1)S(1)} %collective-permute-done.3.refs_4_) | copy-start | bytes 983044
  32.6 11.1 %collective-permute-start.4 = (bf16[2,128,1024]{2,1,0:T(8,128)(2,1)S(1)}, bf16[2,128,1024]{2,1,0:T(8,128)(2,1)S(1)}, u32[]{:S(2)}, u32[]{:S(2)}) collective-permute-start(bf16[2,128,1024]{2,1,0:T(8,128)(2,1)S(1)} %get-tuple-element.57), channel_id=1, source_target_pairs={{0,8},{8,16},{16,24},{24,0},{1,9},{9,17},{17,25},{25,1},{2,10},{10... | collective-permute-start | bytes 1572872 | tf_op jit(solution)/shard_map/ppermute | solution.py:20
  33.7 11.4 %collective-permute-start.5 = (bf16[2,128,1024]{2,1,0:T(8,128)(2,1)S(1)}, bf16[2,128,1024]{2,1,0:T(8,128)(2,1)S(1)}, u32[]{:S(2)}, u32[]{:S(2)}) collective-permute-start(bf16[2,128,1024]{2,1,0:T(8,128)(2,1)S(1)} %get-tuple-element.58), channel_id=1, source_target_pairs={{0,24},{8,0},{16,8},{24,16},{1,25},{9,1},{17,9},{25,17},{2,26},{10... | collective-permute-start | bytes 1572872 | tf_op jit(solution)/shard_map/ppermute | solution.py:20
  35.0 14.4 %collective-permute-start.12 = (bf16[2,128,1024]{2,1,0:T(8,128)(2,1)S(1)}, bf16[2,128,1024]{2,1,0:T(8,128)(2,1)S(1)}, u32[]{:S(2)}, u32[]{:S(2)}) collective-permute-start(bf16[2,128,1024]{2,1,0:T(8,128)(2,1)S(1)} %get-tuple-element.69), channel_id=1, source_target_pairs={{0,32},{32,64},{64,96},{96,0},{1,33},{33,65},{65,97},{97,1},{2,34}... | collective-permute-start | bytes 1572872 | tf_op jit(solution)/shard_map/ppermute | solution.py:20
  35.2 14.2 %collective-permute-start.13 = (bf16[2,128,1024]{2,1,0:T(8,128)(2,1)S(1)}, bf16[2,128,1024]{2,1,0:T(8,128)(2,1)S(1)}, u32[]{:S(2)}, u32[]{:S(2)}) collective-permute-start(bf16[2,128,1024]{2,1,0:T(8,128)(2,1)S(1)} %get-tuple-element.70), channel_id=1, source_target_pairs={{0,96},{32,0},{64,32},{96,64},{1,97},{33,1},{65,33},{97,65},{2,98}... | collective-permute-start | bytes 1572872 | tf_op jit(solution)/shard_map/ppermute | solution.py:20
  46.1 7.8 %collective-permute-start.6 = (bf16[2,64,1024]{2,1,0:T(8,128)(2,1)S(1)}, bf16[2,64,1024]{2,1,0:T(8,128)(2,1)S(1)}, u32[]{:S(2)}, u32[]{:S(2)}) collective-permute-start(bf16[2,64,1024]{2,1,0:T(8,128)(2,1)S(1)} %get-tuple-element.60), channel_id=1, source_target_pairs={{0,32},{32,64},{64,96},{96,0},{1,33},{33,65},{65,97},{97,1},{2,34}... | collective-permute-start | bytes 786440 | tf_op jit(solution)/shard_map/ppermute | solution.py:20
  47.8 7.3 %collective-permute-start.7 = (bf16[2,64,1024]{2,1,0:T(8,128)(2,1)S(1)}, bf16[2,64,1024]{2,1,0:T(8,128)(2,1)S(1)}, u32[]{:S(2)}, u32[]{:S(2)}) collective-permute-start(bf16[2,64,1024]{2,1,0:T(8,128)(2,1)S(1)} %get-tuple-element.61), channel_id=1, source_target_pairs={{0,96},{32,0},{64,32},{96,64},{1,97},{33,1},{65,33},{97,65},{2,98}... | collective-permute-start | bytes 786440 | tf_op jit(solution)/shard_map/ppermute | solution.py:20
  50.4 8.0 %collective-permute-start.14 = (bf16[2,64,1024]{2,1,0:T(8,128)(2,1)S(1)}, bf16[2,64,1024]{2,1,0:T(8,128)(2,1)S(1)}, u32[]{:S(2)}, u32[]{:S(2)}) collective-permute-start(bf16[2,64,1024]{2,1,0:T(8,128)(2,1)S(1)} %get-tuple-element.72), channel_id=1, source_target_pairs={{0,8},{8,16},{16,24},{24,0},{1,9},{9,17},{17,25},{25,1},{2,10},{10... | collective-permute-start | bytes 786440 | tf_op jit(solution)/shard_map/ppermute | solution.py:20
  51.5 8.0 %collective-permute-start.15 = (bf16[2,64,1024]{2,1,0:T(8,128)(2,1)S(1)}, bf16[2,64,1024]{2,1,0:T(8,128)(2,1)S(1)}, u32[]{:S(2)}, u32[]{:S(2)}) collective-permute-start(bf16[2,64,1024]{2,1,0:T(8,128)(2,1)S(1)} %get-tuple-element.73), channel_id=1, source_target_pairs={{0,24},{8,0},{16,8},{24,16},{1,25},{9,1},{17,9},{25,17},{2,26},{10... | collective-permute-start | bytes 786440 | tf_op jit(solution)/shard_map/ppermute | solution.py:20
  52.7 22.5 %collective-permute-start.21 = (bf16[256,640]{1,0:T(8,128)(2,1)S(1)}, bf16[256,640]{1,0:T(8,128)(2,1)S(1)}, u32[]{:S(2)}, u32[]{:S(2)}) collective-permute-start(bf16[256,640]{1,0:T(8,128)(2,1)S(1)} %collective-permute-done.3.refs_4_), channel_id=1, source_target_pairs={{0,2},{2,4},{4,6},{6,0},{1,3},{3,5},{5,7},{7,1},{8,10},{10,12},{12... | collective-permute-start | bytes 983048 | tf_op jit(solution)/shard_map/ppermute | solution.py:20
  55.1 6.6 %collective-permute-start.8 = (bf16[1,64,1024]{2,1,0:T(8,128)(2,1)S(1)}, bf16[1,64,1024]{2,1,0:T(8,128)(2,1)S(1)}, u32[]{:S(2)}, u32[]{:S(2)}) collective-permute-start(bf16[1,64,1024]{2,1,0:T(8,128)(2,1)S(1)} %get-tuple-element.63), channel_id=1, source_target_pairs={{0,32},{32,64},{64,96},{96,0},{1,33},{33,65},{65,97},{97,1},{2,34}... | collective-permute-start | bytes 393224 | tf_op jit(solution)/shard_map/ppermute | solution.py:20
  56.9 5.0 %collective-permute-start.9 = (bf16[1,64,1024]{2,1,0:T(8,128)(2,1)S(1)}, bf16[1,64,1024]{2,1,0:T(8,128)(2,1)S(1)}, u32[]{:S(2)}, u32[]{:S(2)}) collective-permute-start(bf16[1,64,1024]{2,1,0:T(8,128)(2,1)S(1)} %get-tuple-element.64), channel_id=1, source_target_pairs={{0,96},{32,0},{64,32},{96,64},{1,97},{33,1},{65,33},{97,65},{2,98}... | collective-permute-start | bytes 393224 | tf_op jit(solution)/shard_map/ppermute | solution.py:20
  59.5 5.0 %collective-permute-start.16 = (bf16[1,64,1024]{2,1,0:T(8,128)(2,1)S(1)}, bf16[1,64,1024]{2,1,0:T(8,128)(2,1)S(1)}, u32[]{:S(2)}, u32[]{:S(2)}) collective-permute-start(bf16[1,64,1024]{2,1,0:T(8,128)(2,1)S(1)} %get-tuple-element.75), channel_id=1, source_target_pairs={{0,8},{8,16},{16,24},{24,0},{1,9},{9,17},{17,25},{25,1},{2,10},{10... | collective-permute-start | bytes 393224 | tf_op jit(solution)/shard_map/ppermute | solution.py:20
  60.1 6.2 %collective-permute-start.17 = (bf16[1,64,1024]{2,1,0:T(8,128)(2,1)S(1)}, bf16[1,64,1024]{2,1,0:T(8,128)(2,1)S(1)}, u32[]{:S(2)}, u32[]{:S(2)}) collective-permute-start(bf16[1,64,1024]{2,1,0:T(8,128)(2,1)S(1)} %get-tuple-element.76), channel_id=1, source_target_pairs={{0,24},{8,0},{16,8},{24,16},{1,25},{9,1},{17,9},{25,17},{2,26},{10... | collective-permute-start | bytes 393224 | tf_op jit(solution)/shard_map/ppermute | solution.py:20
  67.2 23.0 %all-to-all-start = ((bf16[16,128,128]{2,1,0:T(8,128)(2,1)}), bf16[16,128,128]{2,1,0:T(8,128)(2,1)S(1)}, u32[]{:S(2)}, u32[]{:S(2)}) async-start(bf16[16,128,128]{2,1,0:T(8,128)(2,1)} %pieces.1), calls=%async_computation | async-start | bytes 1048576 | tf_op jit(solution)/shard_map/all_to_all | solution.py:514
  74.2 1.9 %collective-permute-start.18 = (bf16[256,640]{1,0:T(8,128)(2,1)S(1)}, bf16[256,640]{1,0:T(8,128)(2,1)S(1)}, u32[]{:S(2)}, u32[]{:S(2)}) collective-permute-start(bf16[256,640]{1,0:T(8,128)(2,1)S(1)} %trim.1.refs_0_), channel_id=1, source_target_pairs={{0,1},{1,0},{2,3},{3,2},{4,5},{5,4},{6,7},{7,6},{8,9},{9,8},{10,11... | collective-permute-start | bytes 983048 | tf_op jit(solution)/shard_map/ppermute | solution.py:25
  74.6 1.8 %collective-permute-start.19 = (bf16[256,640]{1,0:T(8,128)(2,1)S(1)}, bf16[256,640]{1,0:T(8,128)(2,1)S(1)}, u32[]{:S(2)}, u32[]{:S(2)}) collective-permute-start(bf16[256,640]{1,0:T(8,128)(2,1)S(1)} %collective-permute-done.2.refs_2_), channel_id=1, source_target_pairs={{0,1},{1,0},{2,3},{3,2},{4,5},{5,4},{6,7},{7,6},{8,9},{9,8},{10,11... | collective-permute-start | bytes 983048 | tf_op jit(solution)/shard_map/ppermute | solution.py:25
  74.8 2.1 %collective-permute-start.20 = (bf16[256,640]{1,0:T(8,128)(2,1)S(1)}, bf16[256,640]{1,0:T(8,128)(2,1)S(1)}, u32[]{:S(2)}, u32[]{:S(2)}) collective-permute-start(bf16[256,640]{1,0:T(8,128)(2,1)S(1)} %collective-permute-done.3.refs_4_), channel_id=1, source_target_pairs={{0,1},{1,0},{2,3},{3,2},{4,5},{5,4},{6,7},{7,6},{8,9},{9,8},{10,11... | collective-permute-start | bytes 983048 | tf_op jit(solution)/shard_map/ppermute | solution.py:25
  75.1 2.2 %collective-permute-start.22 = (bf16[256,640]{1,0:T(8,128)(2,1)S(1)}, bf16[256,640]{1,0:T(8,128)(2,1)S(1)}, u32[]{:S(2)}, u32[]{:S(2)}) collective-permute-start(bf16[256,640]{1,0:T(8,128)(2,1)S(1)} %collective-permute-done.21.refs_6_), channel_id=1, source_target_pairs={{0,1},{1,0},{2,3},{3,2},{4,5},{5,4},{6,7},{7,6},{8,9},{9,8},{10,11... | collective-permute-start | bytes 983048 | tf_op jit(solution)/shard_map/ppermute | solution.py:25
  91.7 13.7 %all-to-all-start.1 = ((bf16[8,128,128]{2,1,0:T(8,128)(2,1)}), bf16[8,128,128]{2,1,0:T(8,128)(2,1)S(1)}, u32[]{:S(2)}, u32[]{:S(2)}) async-start(bf16[8,128,128]{2,1,0:T(8,128)(2,1)} %get-tuple-element.87), calls=%async_computation.1 | async-start | bytes 524288 | tf_op jit(solution)/shard_map/all_to_all | solution.py:518
  95.7 1.3 %copy-start.2 = (bf16[4,256,640]{2,1,0:T(8,128)(2,1)S(1)}, bf16[4,256,640]{2,1,0:T(8,128)(2,1)}, u32[]{:S(2)}) copy-start(bf16[4,256,640]{2,1,0:T(8,128)(2,1)} %copy-done.1) | copy-start | bytes 3932164
  106.9 1.3 %collective-permute-start.23 = (f32[16,128]{1,0:T(8,128)S(1)}, f32[16,128]{1,0:T(8,128)S(1)}, u32[]{:S(2)}, u32[]{:S(2)}) collective-permute-start(f32[16,128]{1,0:T(8,128)S(1)} %get-tuple-element.93), channel_id=1, source_target_pairs={{0,1},{1,0},{2,3},{3,2},{4,5},{5,4},{6,7},{7,6},{8,9},{9,8},{10,11... | collective-permute-start | bytes 24584 | tf_op jit(solution)/shard_map/ppermute | solution.py:25
  108.1 3.7 %collective-permute-start.26 = (f32[16,128]{1,0:T(8,128)S(1)}, f32[16,128]{1,0:T(8,128)S(1)}, u32[]{:S(2)}, u32[]{:S(2)}) collective-permute-start(f32[16,128]{1,0:T(8,128)S(1)} %add.12), channel_id=1, source_target_pairs={{0,6},{2,0},{4,2},{6,4},{1,7},{3,1},{5,3},{7,5},{8,14},{10,8},{12,... | collective-permute-start | bytes 24584 | tf_op jit(solution)/shard_map/ppermute | solution.py:20
  109.6 4.6 %collective-permute-start.25 = (f32[16,128]{1,0:T(8,128)S(1)}, f32[16,128]{1,0:T(8,128)S(1)}, u32[]{:S(2)}, u32[]{:S(2)}) collective-permute-start(f32[16,128]{1,0:T(8,128)S(1)} %add.12), channel_id=1, source_target_pairs={{0,4},{2,6},{4,0},{6,2},{1,5},{3,7},{5,1},{7,3},{8,12},{10,14},{12... | collective-permute-start | bytes 24584 | tf_op jit(solution)/shard_map/ppermute | solution.py:20
  109.8 5.4 %collective-permute-start.24 = (f32[16,128]{1,0:T(8,128)S(1)}, f32[16,128]{1,0:T(8,128)S(1)}, u32[]{:S(2)}, u32[]{:S(2)}) collective-permute-start(f32[16,128]{1,0:T(8,128)S(1)} %add.12), channel_id=1, source_target_pairs={{0,2},{2,4},{4,6},{6,0},{1,3},{3,5},{5,7},{7,1},{8,10},{10,12},{12... | collective-permute-start | bytes 24584 | tf_op jit(solution)/shard_map/ppermute | solution.py:20
  (5 other events, 5.0 us)

commit v2 on v1

--- a/solution.py
+++ b/solution.py
@@ -77,30 +77,18 @@
     return last_up, last_down
 
 
-def turn_kernel(which, place_ref, own_ref, up_ref, down_ref, last_up_ref, last_down_ref, next_up, next_down, next_mid, next_own, sum_ref):
-    rows = own_ref.shape[1]
-    half = rows // 2
+def turn_kernel(which, place_ref, own_ref, up_ref, down_ref, last_up_ref, last_down_ref, far_ref, ahead_ref, behind_ref, here_ref, sum_ref):
     for block in range(2):
-        for row in range(0, rows, 32):
+        for row in range(0, own_ref.shape[1], 32):
             at = pl.ds(row, 32)
             sum_ref[block, at] = narrow(own_ref[block, at], last_up_ref[block, at], down_ref[2 + block, at])
             sum_ref[2 + block, at] = narrow(own_ref[2 + block, at], up_ref[2 + block, at], last_down_ref[block, at])
-    low, high = pl.ds(0, half), pl.ds(half, half)
-    here = place_ref[which]
-    ahead, across, behind = (lax.rem(here + step, 4) for step in (1, 2, 3))
-    next_up[0] = sum_ref[across, low]
-    next_up[1] = sum_ref[ahead, high]
-    next_down[0] = sum_ref[across, high]
-    next_down[1] = sum_ref[behind, low]
-    next_mid[0] = sum_ref[ahead, low]
-    next_mid[1] = sum_ref[behind, high]
-    next_own[0] = sum_ref[here, low]
-    next_own[1] = sum_ref[here, high]
+    for step, ref in enumerate((here_ref, ahead_ref, far_ref, behind_ref)):
+        ref[...] = sum_ref[lax.rem(place_ref[which] + step, 4)]
 
 
 def turn(which, place, own, up, down, last_up, last_down):
-    rows, size = own.shape[1:]
-    part = jax.ShapeDtypeStruct((2, rows // 2, size), own.dtype)
+    part = jax.ShapeDtypeStruct(own.shape[1:], own.dtype)
     return call(
         functools.partial(turn_kernel, which),
         "turn",
@@ -113,27 +101,27 @@
     )
 
 
+def second_stage(far, ahead, behind, here, axis):
+    return here, shift(far, axis, 2), shift(ahead, axis, 1), shift(behind, axis, -1)
+
+
 def pieces_kernel(*refs):
     out_ref = refs[-1]
-    width = out_ref.shape[2]
+    _, rows, width = out_ref.shape
     for side in range(2):
-        own, up, down, last_up, last_down = refs[5 * side : 5 * side + 5]
-        half = own.shape[1]
-        for row in range(0, half, 32):
+        terms = refs[4 * side : 4 * side + 4]
+        for row in range(0, rows, 32):
             at = pl.ds(row, 32)
-            low = narrow(own[0, at], last_up[0, at], down[1, at])
-            high = narrow(own[1, at], up[1, at], last_down[0, at])
+            total = narrow(*(ref[at] for ref in terms))
             for piece in range(8):
-                columns = slice(piece * width, (piece + 1) * width)
-                out_ref[8 * side + piece, at] = low[:, columns]
-                out_ref[8 * side + piece, pl.ds(half + row, 32)] = high[:, columns]
-
-
-def make_pieces(*parts):
-    rows, size = 2 * parts[0].shape[1], parts[0].shape[2]
+                out_ref[8 * side + piece, at] = total[:, piece * width : (piece + 1) * width]
+
+
+def make_pieces(*terms):
+    rows, size = terms[0].shape
     out = jax.ShapeDtypeStruct((16, rows, size // 8), jnp.bfloat16)
     return call(
-        pieces_kernel, "pieces", out, [VMEM] * 10, parts, flops=4 * rows * size, moved=16 * rows * size
+        pieces_kernel, "pieces", out, [VMEM] * 8, terms, flops=8 * rows * size, moved=20 * rows * size
     )
 
 
@@ -502,15 +490,12 @@
     x_last = ring_first(*x_last, "x")
     y_last = ring_first(*y_last, "y")
 
-    lower_up, lower_down, lower_mid, lower_own = turn(1, place, x_own, *x_ends, *x_last)
-    lower_ends = ring_first(lower_up, lower_down, "y")
-    upper_up, upper_down, upper_mid, upper_own = turn(0, place, y_own, *y_ends, *y_last)
-    upper_ends = ring_first(upper_up, upper_down, "x")
-    lower_last = ring_first(*pass_on(lower_mid, *lower_ends), "y")
-    upper_last = ring_first(*pass_on(upper_mid, *upper_ends), "x")
-    pieces = make_pieces(lower_own, *lower_ends, *lower_last, upper_own, *upper_ends, *upper_last)
+    lower = second_stage(*turn(1, place, x_own, *x_ends, *x_last), "y")
+    upper = second_stage(*turn(0, place, y_own, *y_ends, *y_last), "x")
+    pieces = make_pieces(*lower, *upper)
 
     slots = after(pieces, *slots)
+
     pieces = lax.all_to_all(pieces, ("zh",) + owner, split_axis=0, concat_axis=0, tiled=True)
     left_root, right_slots = left_inverse_root(place, owner_table, slots)
     mixed, energy = mix(pieces, left_root)

time: 118 us -> 120 us (1.017)
  waiting for transfers between devices: 46.8 us -> 48.8 us
    ppermute x22 -> x20, waiting for transfers between devices: 36.1 us -> 38.1 us  [shift(): lax.ppermute(array, axis, [(i, (i + step) % size) for i in range(size)])]
    all_to_all x1, starting transfers between devices: 6.97 us -> 8.96 us  [local(): lax.all_to_all(pieces, ('zh',) + owner, split_axis=0, concat_axis=0, tile...]
    ppermute x22 -> x20, starting transfers between devices: 27 us -> 25.9 us  [shift(): lax.ppermute(array, axis, [(i, (i + step) % size) for i in range(size)])]
    pallas_call x14 -> x12, Pallas kernels: 14.5 us -> 14.4 us  [call(): pl.pallas_call(kernel, out_shape=out_shape, in_specs=in_specs, out_specs=...]
  transfers between devices with their start and end apart: 29 -> 27, of which waited for: 18 -> 18; matrix products, arithmetic and copies ran while one was open for 0% -> 0% of each run, Pallas kernels for 13% -> 13%
where the time goes in v2:
time: 120 us; the launch traced here: 119 us
  waiting for transfers between devices  48.8 us (41%)
  starting transfers between devices  40.1 us (33%)
  Pallas kernels  23 us (19%)
  local copies, waits for them, and re-layouts  6.32 us (5%)
    ppermute x20, waiting for transfers between devices, shift(): lax.ppermute(array, axis, [(i, (i + step) % size) for i in range(size)])  38.1 us
    ppermute x20, starting transfers between devices, shift(): lax.ppermute(array, axis, [(i, (i + step) % size) for i in range(size)])  25.9 us
    pallas_call x12, Pallas kernels, call(): pl.pallas_call(kernel, out_shape=out_shape, in_specs=in_specs, out_specs=...  14.4 us
    all_to_all x1, starting transfers between devices, local(): lax.all_to_all(pieces, ('zh',) + owner, split_axis=0, concat_axis=0, tile...  8.96 us
    pallas_call x1, Pallas kernels, left_inverse_root(): pl.pallas_call(root_kernel, out_shape=(jax.ShapeDtypeStruct(matrix, jnp.b...  8.61 us
    all_to_all x1, waiting for transfers between devices, local(): lax.all_to_all(mixed, owner, split_axis=0, concat_axis=0, tiled=True)  7.01 us
    unnamed x16, local copies, waits for them, and re-layouts  6.32 us
    all_to_all x1, starting transfers between devices, local(): lax.all_to_all(mixed, owner, split_axis=0, concat_axis=0, tiled=True)  3.98 us
  transfers between devices with their start and end apart: 27, of which 18 were waited for; matrix products, arithmetic and copies ran while one was open for 0% of the time, Pallas kernels for 13%

profile of v2, /device:TPU:6, one launch (start us, length us, event | category | flops | bytes accessed | tf_op | source)
XLA Modules:
  0.0 119.1 jit_solution(5713454768288380842)
XLA Ops:
  0.1 3.5 %send.1 = (bf16[4,128,1024]{2,1,0:T(8,128)(2,1)S(1)}, bf16[4,128,1024]{2,1,0:T(8,128)(2,1)S(1)}, bf16[4,128,1024]{2,1,0:T(8,128)(2,1)S(1)}, bf16[4,128,1024]{2,1,0:T(8,128)(2,1)S(1)}) custom-call(s32[4]{0:T(128)S(1)} %pad_add_fusion.place_ref, bf16[2,4,4,128,1024]{4,3,2,1,0:T(8,128)(2,1)} %bitcast.7), custom_call_target="tpu_custom_call" | custom-call | bytes 8388608 | tf_op jit(solution)/shard_map/send/pallas_call | solution.py:46
  3.6 2.3 %collective-permute-start = (bf16[4,128,1024]{2,1,0:T(8,128)(2,1)S(1)}, bf16[4,128,1024]{2,1,0:T(8,128)(2,1)S(1)}, u32[]{:S(2)}, u32[]{:S(2)}) collective-permute-start(bf16[4,128,1024]{2,1,0:T(8,128)(2,1)S(1)} %get-tuple-element.46), channel_id=1, source_target_pairs={{0,8},{8,16},{16,24},{24,0},{1,9},{9,17},{17,25},{25,1},{2,10},{10... | collective-permute-start | bytes 3145736 | tf_op jit(solution)/shard_map/ppermute | solution.py:20
  5.9 1.4 %collective-permute-start.9 = (bf16[4,128,1024]{2,1,0:T(8,128)(2,1)S(1)}, bf16[4,128,1024]{2,1,0:T(8,128)(2,1)S(1)}, u32[]{:S(2)}, u32[]{:S(2)}) collective-permute-start(bf16[4,128,1024]{2,1,0:T(8,128)(2,1)S(1)} %get-tuple-element.60), channel_id=1, source_target_pairs={{0,32},{32,64},{64,96},{96,0},{1,33},{33,65},{65,97},{97,1},{2,34}... | collective-permute-start | bytes 3145736 | tf_op jit(solution)/shard_map/ppermute | solution.py:20
  7.3 1.9 %collective-permute-start.10 = (bf16[4,128,1024]{2,1,0:T(8,128)(2,1)S(1)}, bf16[4,128,1024]{2,1,0:T(8,128)(2,1)S(1)}, u32[]{:S(2)}, u32[]{:S(2)}) collective-permute-start(bf16[4,128,1024]{2,1,0:T(8,128)(2,1)S(1)} %get-tuple-element.61), channel_id=1, source_target_pairs={{0,96},{32,0},{64,32},{96,64},{1,97},{33,1},{65,33},{97,65},{2,98}... | collective-permute-start | bytes 3145736 | tf_op jit(solution)/shard_map/ppermute | solution.py:20
  9.8 1.2 %copy-done.3 = f32[1,1,256,1024]{3,2,1,0:T(8,128)S(1)} copy-done((f32[1,1,256,1024]{3,2,1,0:T(8,128)S(1)}, f32[1,1,256,1024]{3,2,1,0:T(8,128)}, u32[]{:S(2)}) %copy-start.3) | copy-done | bytes 1048600
  11.6 1.9 %collective-permute-start.2 = (bf16[256,640]{1,0:T(8,128)(2,1)S(1)}, bf16[256,640]{1,0:T(8,128)(2,1)S(1)}, u32[]{:S(2)}, u32[]{:S(2)}) collective-permute-start(bf16[256,640]{1,0:T(8,128)(2,1)S(1)} %trim.1.refs_0_), channel_id=1, source_target_pairs={{0,2},{2,4},{4,6},{6,0},{1,3},{3,5},{5,7},{7,1},{8,10},{10,12},{12... | collective-permute-start | bytes 983048 | tf_op jit(solution)/shard_map/ppermute | solution.py:20
  13.5 1.4 %keep.1 = (bf16[4,128,1024]{2,1,0:T(8,128)(2,1)S(1)}, bf16[4,128,1024]{2,1,0:T(8,128)(2,1)S(1)}, bf16[4,128,1024]{2,1,0:T(8,128)(2,1)S(1)}, bf16[4,128,1024]{2,1,0:T(8,128)(2,1)S(1)}) custom-call(s32[4]{0:T(128)S(1)} %pad_add_fusion.place_ref, bf16[2,4,4,128,1024]{4,3,2,1,0:T(8,128)(2,1)S(1)} %bitcast.8), custom_call_target="tpu_custom_call" | custom-call | bytes 8388608 | tf_op jit(solution)/shard_map/keep/pallas_call | solution.py:46
  14.9 7.9 %collective-permute-done.2.refs_2_ = bf16[256,640]{1,0:T(8,128)(2,1)S(1)} collective-permute-done((bf16[256,640]{1,0:T(8,128)(2,1)S(1)}, bf16[256,640]{1,0:T(8,128)(2,1)S(1)}, u32[]{:S(2)}, u32[]{:S(2)}) %collective-permute-start.2) | collective-permute-done | bytes 327712 | tf_op jit(solution)/shard_map/ppermute | solution.py:20
  22.8 9.5 %collective-permute-done.3.refs_4_ = bf16[256,640]{1,0:T(8,128)(2,1)S(1)} collective-permute-done((bf16[256,640]{1,0:T(8,128)(2,1)S(1)}, bf16[256,640]{1,0:T(8,128)(2,1)S(1)}, u32[]{:S(2)}, u32[]{:S(2)}) %collective-permute-start.3) | collective-permute-done | bytes 327712 | tf_op jit(solution)/shard_map/ppermute | solution.py:20
  35.4 2.9 %collective-permute-start.12 = (bf16[2,128,1024]{2,1,0:T(8,128)(2,1)S(1)}, bf16[2,128,1024]{2,1,0:T(8,128)(2,1)S(1)}, u32[]{:S(2)}, u32[]{:S(2)}) collective-permute-start(bf16[2,128,1024]{2,1,0:T(8,128)(2,1)S(1)} %get-tuple-element.64), channel_id=1, source_target_pairs={{0,96},{32,0},{64,32},{96,64},{1,97},{33,1},{65,33},{97,65},{2,98}... | collective-permute-start | bytes 1572872 | tf_op jit(solution)/shard_map/ppermute | solution.py:20
  38.3 5.4 %collective-permute-done.4.last_up_ref = bf16[2,128,1024]{2,1,0:T(8,128)(2,1)S(1)} collective-permute-done((bf16[2,128,1024]{2,1,0:T(8,128)(2,1)S(1)}, bf16[2,128,1024]{2,1,0:T(8,128)(2,1)S(1)}, u32[]{:S(2)}, u32[]{:S(2)}) %collective-permute-start.4) | collective-permute-done | bytes 524320 | tf_op jit(solution)/shard_map/ppermute | solution.py:20
  43.8 1.3 %collective-permute-done.5.last_down_ref = bf16[2,128,1024]{2,1,0:T(8,128)(2,1)S(1)} collective-permute-done((bf16[2,128,1024]{2,1,0:T(8,128)(2,1)S(1)}, bf16[2,128,1024]{2,1,0:T(8,128)(2,1)S(1)}, u32[]{:S(2)}, u32[]{:S(2)}) %collective-permute-start.5) | collective-permute-done | bytes 524320 | tf_op jit(solution)/shard_map/ppermute | solution.py:20
  46.0 3.2 %collective-permute-start.6 = (bf16[128,1024]{1,0:T(8,128)(2,1)S(1)}, bf16[128,1024]{1,0:T(8,128)(2,1)S(1)}, u32[]{:S(2)}, u32[]{:S(2)}) collective-permute-start(bf16[128,1024]{1,0:T(8,128)(2,1)S(1)} %get-tuple-element.56), channel_id=1, source_target_pairs={{0,64},{32,96},{64,0},{96,32},{1,65},{33,97},{65,1},{97,33},{2,66}... | collective-permute-start | bytes 786440 | tf_op jit(solution)/shard_map/ppermute | solution.py:20
  49.9 1.3 %collective-permute-start.19 = (bf16[256,640]{1,0:T(8,128)(2,1)S(1)}, bf16[256,640]{1,0:T(8,128)(2,1)S(1)}, u32[]{:S(2)}, u32[]{:S(2)}) collective-permute-start(bf16[256,640]{1,0:T(8,128)(2,1)S(1)} %collective-permute-done.3.refs_4_), channel_id=1, source_target_pairs={{0,2},{2,4},{4,6},{6,0},{1,3},{3,5},{5,7},{7,1},{8,10},{10,12},{12... | collective-permute-start | bytes 983048 | tf_op jit(solution)/shard_map/ppermute | solution.py:20
  51.2 2.6 %collective-permute-start.8 = (bf16[128,1024]{1,0:T(8,128)(2,1)S(1)}, bf16[128,1024]{1,0:T(8,128)(2,1)S(1)}, u32[]{:S(2)}, u32[]{:S(2)}) collective-permute-start(bf16[128,1024]{1,0:T(8,128)(2,1)S(1)} %get-tuple-element.58), channel_id=1, source_target_pairs={{0,96},{32,0},{64,32},{96,64},{1,97},{33,1},{65,33},{97,65},{2,98}... | collective-permute-start | bytes 786440 | tf_op jit(solution)/shard_map/ppermute | solution.py:20
  55.5 2.2 %collective-permute-start.14 = (bf16[128,1024]{1,0:T(8,128)(2,1)S(1)}, bf16[128,1024]{1,0:T(8,128)(2,1)S(1)}, u32[]{:S(2)}, u32[]{:S(2)}) collective-permute-start(bf16[128,1024]{1,0:T(8,128)(2,1)S(1)} %get-tuple-element.67), channel_id=1, source_target_pairs={{0,8},{8,16},{16,24},{24,0},{1,9},{9,17},{17,25},{25,1},{2,10},{10... | collective-permute-start | bytes 786440 | tf_op jit(solution)/shard_map/ppermute | solution.py:20
  59.1 6.0 %collective-permute-done.13.refs_5_ = bf16[128,1024]{1,0:T(8,128)(2,1)S(1)} collective-permute-done((bf16[128,1024]{1,0:T(8,128)(2,1)S(1)}, bf16[128,1024]{1,0:T(8,128)(2,1)S(1)}, u32[]{:S(2)}, u32[]{:S(2)}) %collective-permute-start.13) | collective-permute-done | bytes 262176 | tf_op jit(solution)/shard_map/ppermute | solution.py:20
  65.1 1.9 %collective-permute-done.15.refs_7_ = bf16[128,1024]{1,0:T(8,128)(2,1)S(1)} collective-permute-done((bf16[128,1024]{1,0:T(8,128)(2,1)S(1)}, bf16[128,1024]{1,0:T(8,128)(2,1)S(1)}, u32[]{:S(2)}, u32[]{:S(2)}) %collective-permute-start.15) | collective-permute-done | bytes 262176 | tf_op jit(solution)/shard_map/ppermute | solution.py:20
  68.1 9.0 %all-to-all-start = ((bf16[16,128,128]{2,1,0:T(8,128)(2,1)}), bf16[16,128,128]{2,1,0:T(8,128)(2,1)S(1)}, u32[]{:S(2)}, u32[]{:S(2)}) async-start(bf16[16,128,128]{2,1,0:T(8,128)(2,1)} %pieces.1), calls=%async_computation | async-start | bytes 1048576 | tf_op jit(solution)/shard_map/all_to_all | solution.py:499
  82.1 8.6 %left_root.1 = (bf16[1024,1024]{1,0:T(8,128)(2,1)S(1)}, bf16[4,256,640]{2,1,0:T(8,128)(2,1)S(1)}) custom-call(s32[4]{0:T(128)S(1)} %pad_add_fusion.place_ref, s32[1]{0:T(128)S(6)} %copy.4.table_ref, bf16[256,640]{1,0:T(8,128)(2,1)S(1)} %trim.1.refs_0_, bf16[256,640]{1,0:T(8,128)(2,1)S(1)} %collective-permute-done.16.refs_1_, ...), custom_call_target="tpu_custom_call" | custom-call | flops 6442450944 | bytes 4194304 | tf_op jit(solution)/shard_map/left_root/pallas_call | solution.py:295
  90.8 1.1 copy-done.1
  91.9 1.2 %all-to-all-done.pieces_ref = bf16[16,128,128]{2,1,0:T(8,128)(2,1)S(1)} async-done(((bf16[16,128,128]{2,1,0:T(8,128)(2,1)}), bf16[16,128,128]{2,1,0:T(8,128)(2,1)S(1)}, u32[]{:S(2)}, u32[]{:S(2)}) %all-to-all-start) | async-done | bytes 524320 | tf_op jit(solution)/shard_map/all_to_all | solution.py:499
  93.1 1.5 %mix.1 = (bf16[8,128,128]{2,1,0:T(8,128)(2,1)}, f32[8,128]{1,0:T(8,128)S(1)}) custom-call(bf16[16,128,128]{2,1,0:T(8,128)(2,1)S(1)} %all-to-all-done.pieces_ref, bf16[1024,1024]{1,0:T(8,128)(2,1)S(1)} %get-tuple-element.78.left_ref), custom_call_target="tpu_custom_call" | custom-call | flops 268435456 | bytes 2097152 | tf_op jit(solution)/shard_map/mix/pallas_call | solution.py:46
  94.6 4.0 %all-to-all-start.1 = ((bf16[8,128,128]{2,1,0:T(8,128)(2,1)}), bf16[8,128,128]{2,1,0:T(8,128)(2,1)S(1)}, u32[]{:S(2)}, u32[]{:S(2)}) async-start(bf16[8,128,128]{2,1,0:T(8,128)(2,1)} %get-tuple-element.79), calls=%async_computation.1 | async-start | bytes 524288 | tf_op jit(solution)/shard_map/all_to_all | solution.py:503
  98.6 1.3 %copy-done.2 = bf16[4,256,640]{2,1,0:T(8,128)(2,1)S(1)} copy-done((bf16[4,256,640]{2,1,0:T(8,128)(2,1)S(1)}, bf16[4,256,640]{2,1,0:T(8,128)(2,1)}, u32[]{:S(2)}) %copy-start.2) | copy-done | bytes 1310744
  99.9 1.4 %right_base.1 = (bf16[1024,1024]{1,0:T(8,128)(2,1)S(1)}, f32[8,1024]{1,0:T(8,128)S(1)}) custom-call(bf16[4,256,640]{2,1,0:T(8,128)(2,1)S(1)} %copy-done.2), custom_call_target="tpu_custom_call" | custom-call | flops 4194304 | bytes 4194304 | tf_op jit(solution)/shard_map/right_base/pallas_call | solution.py:46
  101.3 7.0 %all-to-all-done.1.mixed_ref = bf16[8,128,128]{2,1,0:T(8,128)(2,1)S(1)} async-done(((bf16[8,128,128]{2,1,0:T(8,128)(2,1)}), bf16[8,128,128]{2,1,0:T(8,128)(2,1)S(1)}, u32[]{:S(2)}, u32[]{:S(2)}) %all-to-all-start.1) | async-done | bytes 262176 | tf_op jit(solution)/shard_map/all_to_all | solution.py:503
  108.3 1.4 %condition.1 = (f32[128,1024]{1,0:T(8,128)S(1)}, f32[16,128]{1,0:T(8,128)S(1)}) custom-call(bf16[8,128,128]{2,1,0:T(8,128)(2,1)S(1)} %all-to-all-done.1.mixed_ref, bf16[1024,1024]{1,0:T(8,128)(2,1)S(1)} %get-tuple-element.82.first_ref, f32[8,1024]{1,0:T(8,128)S(1)} %get-tuple-element.83.diagonal_ref, f32[8,128]{1,0:T(8,128)S(1)} %get-tuple-element.84.energy_ref), custom_call_target="tpu_custom_call" | custom-call | flops 1073741824 | bytes 2097152 | tf_op jit(solution)/shard_map/condition/pallas_call | solution.py:46
  109.8 1.2 collective-permute-done.21
  111.0 1.4 %collective-permute-start.24 = (f32[16,128]{1,0:T(8,128)S(1)}, f32[16,128]{1,0:T(8,128)S(1)}, u32[]{:S(2)}, u32[]{:S(2)}) collective-permute-start(f32[16,128]{1,0:T(8,128)S(1)} %add.12), channel_id=1, source_target_pairs={{0,6},{2,0},{4,2},{6,4},{1,7},{3,1},{5,3},{7,5},{8,14},{10,8},{12,... | collective-permute-start | bytes 24584 | tf_op jit(solution)/shard_map/ppermute | solution.py:20
  113.0 1.6 %collective-permute-done.24 = f32[16,128]{1,0:T(8,128)S(1)} collective-permute-done((f32[16,128]{1,0:T(8,128)S(1)}, f32[16,128]{1,0:T(8,128)S(1)}, u32[]{:S(2)}, u32[]{:S(2)}) %collective-permute-start.24) | collective-permute-done | bytes 8224 | tf_op jit(solution)/shard_map/ppermute | solution.py:20
  114.6 2.4 %collective-permute-done.23 = f32[16,128]{1,0:T(8,128)S(1)} collective-permute-done((f32[16,128]{1,0:T(8,128)S(1)}, f32[16,128]{1,0:T(8,128)S(1)}, u32[]{:S(2)}, u32[]{:S(2)}) %collective-permute-start.23) | collective-permute-done | bytes 8224 | tf_op jit(solution)/shard_map/ppermute | solution.py:20
  (54 shorter events, 17.5 us)
Async XLA Ops:
  0.1 13.4 %copy-start = (bf16[1,32,128,1024]{3,2,1,0:T(8,128)(2,1)S(1)}, bf16[1,32,128,1024]{3,2,1,0:T(8,128)(2,1)}, u32[]{:S(2)}) copy-start(bf16[1,32,128,1024]{3,2,1,0:T(8,128)(2,1)} %param.3) | copy-start | bytes 25165828
  3.6 28.8 %collective-permute-start = (bf16[4,128,1024]{2,1,0:T(8,128)(2,1)S(1)}, bf16[4,128,1024]{2,1,0:T(8,128)(2,1)S(1)}, u32[]{:S(2)}, u32[]{:S(2)}) collective-permute-start(bf16[4,128,1024]{2,1,0:T(8,128)(2,1)S(1)} %get-tuple-element.46), channel_id=1, source_target_pairs={{0,8},{8,16},{16,24},{24,0},{1,9},{9,17},{17,25},{25,1},{2,10},{10... | collective-permute-start | bytes 3145736 | tf_op jit(solution)/shard_map/ppermute | solution.py:20
  5.9 26.5 %collective-permute-start.1 = (bf16[4,128,1024]{2,1,0:T(8,128)(2,1)S(1)}, bf16[4,128,1024]{2,1,0:T(8,128)(2,1)S(1)}, u32[]{:S(2)}, u32[]{:S(2)}) collective-permute-start(bf16[4,128,1024]{2,1,0:T(8,128)(2,1)S(1)} %get-tuple-element.49), channel_id=1, source_target_pairs={{0,24},{8,0},{16,8},{24,16},{1,25},{9,1},{17,9},{25,17},{2,26},{10... | collective-permute-start | bytes 3145736 | tf_op jit(solution)/shard_map/ppermute | solution.py:20
  5.9 28.9 %collective-permute-start.9 = (bf16[4,128,1024]{2,1,0:T(8,128)(2,1)S(1)}, bf16[4,128,1024]{2,1,0:T(8,128)(2,1)S(1)}, u32[]{:S(2)}, u32[]{:S(2)}) collective-permute-start(bf16[4,128,1024]{2,1,0:T(8,128)(2,1)S(1)} %get-tuple-element.60), channel_id=1, source_target_pairs={{0,32},{32,64},{64,96},{96,0},{1,33},{33,65},{65,97},{97,1},{2,34}... | collective-permute-start | bytes 3145736 | tf_op jit(solution)/shard_map/ppermute | solution.py:20
  7.3 27.5 %collective-permute-start.10 = (bf16[4,128,1024]{2,1,0:T(8,128)(2,1)S(1)}, bf16[4,128,1024]{2,1,0:T(8,128)(2,1)S(1)}, u32[]{:S(2)}, u32[]{:S(2)}) collective-permute-start(bf16[4,128,1024]{2,1,0:T(8,128)(2,1)S(1)} %get-tuple-element.61), channel_id=1, source_target_pairs={{0,96},{32,0},{64,32},{96,64},{1,97},{33,1},{65,33},{97,65},{2,98}... | collective-permute-start | bytes 3145736 | tf_op jit(solution)/shard_map/ppermute | solution.py:20
  9.8 1.2 %copy-start.3 = (f32[1,1,256,1024]{3,2,1,0:T(8,128)S(1)}, f32[1,1,256,1024]{3,2,1,0:T(8,128)}, u32[]{:S(2)}) copy-start(f32[1,1,256,1024]{3,2,1,0:T(8,128)} %param.4) | copy-start | bytes 3145732
  11.6 11.2 %collective-permute-start.2 = (bf16[256,640]{1,0:T(8,128)(2,1)S(1)}, bf16[256,640]{1,0:T(8,128)(2,1)S(1)}, u32[]{:S(2)}, u32[]{:S(2)}) collective-permute-start(bf16[256,640]{1,0:T(8,128)(2,1)S(1)} %trim.1.refs_0_), channel_id=1, source_target_pairs={{0,2},{2,4},{4,6},{6,0},{1,3},{3,5},{5,7},{7,1},{8,10},{10,12},{12... | collective-permute-start | bytes 983048 | tf_op jit(solution)/shard_map/ppermute | solution.py:20
  22.8 9.5 %collective-permute-start.3 = (bf16[256,640]{1,0:T(8,128)(2,1)S(1)}, bf16[256,640]{1,0:T(8,128)(2,1)S(1)}, u32[]{:S(2)}, u32[]{:S(2)}) collective-permute-start(bf16[256,640]{1,0:T(8,128)(2,1)S(1)} %collective-permute-done.2.refs_2_), channel_id=1, source_target_pairs={{0,2},{2,4},{4,6},{6,0},{1,3},{3,5},{5,7},{7,1},{8,10},{10,12},{12... | collective-permute-start | bytes 983048 | tf_op jit(solution)/shard_map/ppermute | solution.py:20
  32.4 45.3 %copy-start.4 = (bf16[256,640]{1,0:T(8,128)(2,1)}, bf16[256,640]{1,0:T(8,128)(2,1)S(1)}, u32[]{:S(2)}) copy-start(bf16[256,640]{1,0:T(8,128)(2,1)S(1)} %collective-permute-done.3.refs_4_) | copy-start | bytes 983044
  32.6 11.1 %collective-permute-start.4 = (bf16[2,128,1024]{2,1,0:T(8,128)(2,1)S(1)}, bf16[2,128,1024]{2,1,0:T(8,128)(2,1)S(1)}, u32[]{:S(2)}, u32[]{:S(2)}) collective-permute-start(bf16[2,128,1024]{2,1,0:T(8,128)(2,1)S(1)} %get-tuple-element.53), channel_id=1, source_target_pairs={{0,8},{8,16},{16,24},{24,0},{1,9},{9,17},{17,25},{25,1},{2,10},{10... | collective-permute-start | bytes 1572872 | tf_op jit(solution)/shard_map/ppermute | solution.py:20
  33.7 11.3 %collective-permute-start.5 = (bf16[2,128,1024]{2,1,0:T(8,128)(2,1)S(1)}, bf16[2,128,1024]{2,1,0:T(8,128)(2,1)S(1)}, u32[]{:S(2)}, u32[]{:S(2)}) collective-permute-start(bf16[2,128,1024]{2,1,0:T(8,128)(2,1)S(1)} %get-tuple-element.54), channel_id=1, source_target_pairs={{0,24},{8,0},{16,8},{24,16},{1,25},{9,1},{17,9},{25,17},{2,26},{10... | collective-permute-start | bytes 1572872 | tf_op jit(solution)/shard_map/ppermute | solution.py:20
  35.0 16.2 %collective-permute-start.11 = (bf16[2,128,1024]{2,1,0:T(8,128)(2,1)S(1)}, bf16[2,128,1024]{2,1,0:T(8,128)(2,1)S(1)}, u32[]{:S(2)}, u32[]{:S(2)}) collective-permute-start(bf16[2,128,1024]{2,1,0:T(8,128)(2,1)S(1)} %get-tuple-element.63), channel_id=1, source_target_pairs={{0,32},{32,64},{64,96},{96,0},{1,33},{33,65},{65,97},{97,1},{2,34}... | collective-permute-start | bytes 1572872 | tf_op jit(solution)/shard_map/ppermute | solution.py:20
  35.4 18.4 %collective-permute-start.12 = (bf16[2,128,1024]{2,1,0:T(8,128)(2,1)S(1)}, bf16[2,128,1024]{2,1,0:T(8,128)(2,1)S(1)}, u32[]{:S(2)}, u32[]{:S(2)}) collective-permute-start(bf16[2,128,1024]{2,1,0:T(8,128)(2,1)S(1)} %get-tuple-element.64), channel_id=1, source_target_pairs={{0,96},{32,0},{64,32},{96,64},{1,97},{33,1},{65,33},{97,65},{2,98}... | collective-permute-start | bytes 1572872 | tf_op jit(solution)/shard_map/ppermute | solution.py:20
  46.0 9.5 %collective-permute-start.6 = (bf16[128,1024]{1,0:T(8,128)(2,1)S(1)}, bf16[128,1024]{1,0:T(8,128)(2,1)S(1)}, u32[]{:S(2)}, u32[]{:S(2)}) collective-permute-start(bf16[128,1024]{1,0:T(8,128)(2,1)S(1)} %get-tuple-element.56), channel_id=1, source_target_pairs={{0,64},{32,96},{64,0},{96,32},{1,65},{33,97},{65,1},{97,33},{2,66}... | collective-permute-start | bytes 786440 | tf_op jit(solution)/shard_map/ppermute | solution.py:20
  49.2 9.1 %collective-permute-start.7 = (bf16[128,1024]{1,0:T(8,128)(2,1)S(1)}, bf16[128,1024]{1,0:T(8,128)(2,1)S(1)}, u32[]{:S(2)}, u32[]{:S(2)}) collective-permute-start(bf16[128,1024]{1,0:T(8,128)(2,1)S(1)} %get-tuple-element.57), channel_id=1, source_target_pairs={{0,32},{32,64},{64,96},{96,0},{1,33},{33,65},{65,97},{97,1},{2,34}... | collective-permute-start | bytes 786440 | tf_op jit(solution)/shard_map/ppermute | solution.py:20
  49.9 28.1 %collective-permute-start.19 = (bf16[256,640]{1,0:T(8,128)(2,1)S(1)}, bf16[256,640]{1,0:T(8,128)(2,1)S(1)}, u32[]{:S(2)}, u32[]{:S(2)}) collective-permute-start(bf16[256,640]{1,0:T(8,128)(2,1)S(1)} %collective-permute-done.3.refs_4_), channel_id=1, source_target_pairs={{0,2},{2,4},{4,6},{6,0},{1,3},{3,5},{5,7},{7,1},{8,10},{10,12},{12... | collective-permute-start | bytes 983048 | tf_op jit(solution)/shard_map/ppermute | solution.py:20
  51.2 7.9 %collective-permute-start.8 = (bf16[128,1024]{1,0:T(8,128)(2,1)S(1)}, bf16[128,1024]{1,0:T(8,128)(2,1)S(1)}, u32[]{:S(2)}, u32[]{:S(2)}) collective-permute-start(bf16[128,1024]{1,0:T(8,128)(2,1)S(1)} %get-tuple-element.58), channel_id=1, source_target_pairs={{0,96},{32,0},{64,32},{96,64},{1,97},{33,1},{65,33},{97,65},{2,98}... | collective-permute-start | bytes 786440 | tf_op jit(solution)/shard_map/ppermute | solution.py:20
  54.7 10.4 %collective-permute-start.13 = (bf16[128,1024]{1,0:T(8,128)(2,1)S(1)}, bf16[128,1024]{1,0:T(8,128)(2,1)S(1)}, u32[]{:S(2)}, u32[]{:S(2)}) collective-permute-start(bf16[128,1024]{1,0:T(8,128)(2,1)S(1)} %get-tuple-element.66), channel_id=1, source_target_pairs={{0,16},{8,24},{16,0},{24,8},{1,17},{9,25},{17,1},{25,9},{2,18},{10... | collective-permute-start | bytes 786440 | tf_op jit(solution)/shard_map/ppermute | solution.py:20
  55.5 9.6 %collective-permute-start.14 = (bf16[128,1024]{1,0:T(8,128)(2,1)S(1)}, bf16[128,1024]{1,0:T(8,128)(2,1)S(1)}, u32[]{:S(2)}, u32[]{:S(2)}) collective-permute-start(bf16[128,1024]{1,0:T(8,128)(2,1)S(1)} %get-tuple-element.67), channel_id=1, source_target_pairs={{0,8},{8,16},{16,24},{24,0},{1,9},{9,17},{17,25},{25,1},{2,10},{10... | collective-permute-start | bytes 786440 | tf_op jit(solution)/shard_map/ppermute | solution.py:20
  58.3 8.8 %collective-permute-start.15 = (bf16[128,1024]{1,0:T(8,128)(2,1)S(1)}, bf16[128,1024]{1,0:T(8,128)(2,1)S(1)}, u32[]{:S(2)}, u32[]{:S(2)}) collective-permute-start(bf16[128,1024]{1,0:T(8,128)(2,1)S(1)} %get-tuple-element.68), channel_id=1, source_target_pairs={{0,24},{8,0},{16,8},{24,16},{1,25},{9,1},{17,9},{25,17},{2,26},{10... | collective-permute-start | bytes 786440 | tf_op jit(solution)/shard_map/ppermute | solution.py:20
  68.1 25.0 %all-to-all-start = ((bf16[16,128,128]{2,1,0:T(8,128)(2,1)}), bf16[16,128,128]{2,1,0:T(8,128)(2,1)S(1)}, u32[]{:S(2)}, u32[]{:S(2)}) async-start(bf16[16,128,128]{2,1,0:T(8,128)(2,1)} %pieces.1), calls=%async_computation | async-start | bytes 1048576 | tf_op jit(solution)/shard_map/all_to_all | solution.py:499
  77.1 1.8 %collective-permute-start.16 = (bf16[256,640]{1,0:T(8,128)(2,1)S(1)}, bf16[256,640]{1,0:T(8,128)(2,1)S(1)}, u32[]{:S(2)}, u32[]{:S(2)}) collective-permute-start(bf16[256,640]{1,0:T(8,128)(2,1)S(1)} %trim.1.refs_0_), channel_id=1, source_target_pairs={{0,1},{1,0},{2,3},{3,2},{4,5},{5,4},{6,7},{7,6},{8,9},{9,8},{10,11... | collective-permute-start | bytes 983048 | tf_op jit(solution)/shard_map/ppermute | solution.py:25
  77.5 1.8 %collective-permute-start.17 = (bf16[256,640]{1,0:T(8,128)(2,1)S(1)}, bf16[256,640]{1,0:T(8,128)(2,1)S(1)}, u32[]{:S(2)}, u32[]{:S(2)}) collective-permute-start(bf16[256,640]{1,0:T(8,128)(2,1)S(1)} %collective-permute-done.2.refs_2_), channel_id=1, source_target_pairs={{0,1},{1,0},{2,3},{3,2},{4,5},{5,4},{6,7},{7,6},{8,9},{9,8},{10,11... | collective-permute-start | bytes 983048 | tf_op jit(solution)/shard_map/ppermute | solution.py:25
  77.7 2.1 %collective-permute-start.18 = (bf16[256,640]{1,0:T(8,128)(2,1)S(1)}, bf16[256,640]{1,0:T(8,128)(2,1)S(1)}, u32[]{:S(2)}, u32[]{:S(2)}) collective-permute-start(bf16[256,640]{1,0:T(8,128)(2,1)S(1)} %collective-permute-done.3.refs_4_), channel_id=1, source_target_pairs={{0,1},{1,0},{2,3},{3,2},{4,5},{5,4},{6,7},{7,6},{8,9},{9,8},{10,11... | collective-permute-start | bytes 983048 | tf_op jit(solution)/shard_map/ppermute | solution.py:25
  78.0 2.2 %collective-permute-start.20 = (bf16[256,640]{1,0:T(8,128)(2,1)S(1)}, bf16[256,640]{1,0:T(8,128)(2,1)S(1)}, u32[]{:S(2)}, u32[]{:S(2)}) collective-permute-start(bf16[256,640]{1,0:T(8,128)(2,1)S(1)} %collective-permute-done.19.refs_6_), channel_id=1, source_target_pairs={{0,1},{1,0},{2,3},{3,2},{4,5},{5,4},{6,7},{7,6},{8,9},{9,8},{10,11... | collective-permute-start | bytes 983048 | tf_op jit(solution)/shard_map/ppermute | solution.py:25
  90.7 1.1 copy-start.1
  94.6 13.7 %all-to-all-start.1 = ((bf16[8,128,128]{2,1,0:T(8,128)(2,1)}), bf16[8,128,128]{2,1,0:T(8,128)(2,1)S(1)}, u32[]{:S(2)}, u32[]{:S(2)}) async-start(bf16[8,128,128]{2,1,0:T(8,128)(2,1)} %get-tuple-element.79), calls=%async_computation.1 | async-start | bytes 524288 | tf_op jit(solution)/shard_map/all_to_all | solution.py:503
  98.5 1.3 %copy-start.2 = (bf16[4,256,640]{2,1,0:T(8,128)(2,1)S(1)}, bf16[4,256,640]{2,1,0:T(8,128)(2,1)}, u32[]{:S(2)}) copy-start(bf16[4,256,640]{2,1,0:T(8,128)(2,1)} %copy-done.1) | copy-start | bytes 3932164
  109.7 1.3 %collective-permute-start.21 = (f32[16,128]{1,0:T(8,128)S(1)}, f32[16,128]{1,0:T(8,128)S(1)}, u32[]{:S(2)}, u32[]{:S(2)}) collective-permute-start(f32[16,128]{1,0:T(8,128)S(1)} %get-tuple-element.85), channel_id=1, source_target_pairs={{0,1},{1,0},{2,3},{3,2},{4,5},{5,4},{6,7},{7,6},{8,9},{9,8},{10,11... | collective-permute-start | bytes 24584 | tf_op jit(solution)/shard_map/ppermute | solution.py:25
  111.0 3.7 %collective-permute-start.24 = (f32[16,128]{1,0:T(8,128)S(1)}, f32[16,128]{1,0:T(8,128)S(1)}, u32[]{:S(2)}, u32[]{:S(2)}) collective-permute-start(f32[16,128]{1,0:T(8,128)S(1)} %add.12), channel_id=1, source_target_pairs={{0,6},{2,0},{4,2},{6,4},{1,7},{3,1},{5,3},{7,5},{8,14},{10,8},{12,... | collective-permute-start | bytes 24584 | tf_op jit(solution)/shard_map/ppermute | solution.py:20
  112.4 4.6 %collective-permute-start.23 = (f32[16,128]{1,0:T(8,128)S(1)}, f32[16,128]{1,0:T(8,128)S(1)}, u32[]{:S(2)}, u32[]{:S(2)}) collective-permute-start(f32[16,128]{1,0:T(8,128)S(1)} %add.12), channel_id=1, source_target_pairs={{0,4},{2,6},{4,0},{6,2},{1,5},{3,7},{5,1},{7,3},{8,12},{10,14},{12... | collective-permute-start | bytes 24584 | tf_op jit(solution)/shard_map/ppermute | solution.py:20
  112.6 5.4 %collective-permute-start.22 = (f32[16,128]{1,0:T(8,128)S(1)}, f32[16,128]{1,0:T(8,128)S(1)}, u32[]{:S(2)}, u32[]{:S(2)}) collective-permute-start(f32[16,128]{1,0:T(8,128)S(1)} %add.12), channel_id=1, source_target_pairs={{0,2},{2,4},{4,6},{6,0},{1,3},{3,5},{5,7},{7,1},{8,10},{10,12},{12... | collective-permute-start | bytes 24584 | tf_op jit(solution)/shard_map/ppermute | solution.py:20
  (3 other events, 2.7 us)

commit v3 on v1

--- a/solution.py
+++ b/solution.py
@@ -77,7 +77,7 @@
     return last_up, last_down
 
 
-def turn_kernel(which, place_ref, own_ref, up_ref, down_ref, last_up_ref, last_down_ref, next_up, next_down, next_mid, next_own, sum_ref):
+def turn_kernel(place_ref, own_ref, up_ref, down_ref, last_up_ref, last_down_ref, next_up, next_down, next_mid, next_own, sum_ref):
     rows = own_ref.shape[1]
     half = rows // 2
     for block in range(2):
@@ -86,7 +86,7 @@
             sum_ref[block, at] = narrow(own_ref[block, at], last_up_ref[block, at], down_ref[2 + block, at])
             sum_ref[2 + block, at] = narrow(own_ref[2 + block, at], up_ref[2 + block, at], last_down_ref[block, at])
     low, high = pl.ds(0, half), pl.ds(half, half)
-    here = place_ref[which]
+    here = place_ref[0]
     ahead, across, behind = (lax.rem(here + step, 4) for step in (1, 2, 3))
     next_up[0] = sum_ref[across, low]
     next_up[1] = sum_ref[ahead, high]
@@ -98,11 +98,11 @@
     next_own[1] = sum_ref[here, high]
 
 
-def turn(which, place, own, up, down, last_up, last_down):
+def turn(place, own, up, down, last_up, last_down):
     rows, size = own.shape[1:]
     part = jax.ShapeDtypeStruct((2, rows // 2, size), own.dtype)
     return call(
-        functools.partial(turn_kernel, which),
+        turn_kernel,
         "turn",
         (part,) * 4,
         [SMEM] + [VMEM] * 5,
@@ -431,8 +431,12 @@
         precond = 1.5 * wide_ref[:, at] - 0.5 * product
         out_ref[:, at] = precond
         total = total + lanes(precond * precond)
-    totals_ref[:8] = energy_ref[...]
-    totals_ref[8:] = total
+    row_ids = lax.broadcasted_iota(jnp.int32, energy_ref.shape, 0)
+    grad_sums = jnp.sum(energy_ref[...], axis=0, keepdims=True)
+    cond_sums = jnp.sum(total, axis=0, keepdims=True)
+    sums = jnp.where(row_ids == 0, grad_sums, jnp.where(row_ids == 1, cond_sums, 0.0))
+    for piece in range(count):
+        totals_ref[piece] = sums
 
 
 def condition(mixed, first, diagonal, energy):
@@ -441,7 +445,7 @@
     return call(
         condition_kernel,
         "condition",
-        (jax.ShapeDtypeStruct(slab, jnp.float32), jax.ShapeDtypeStruct((16, 128), jnp.float32)),
+        (jax.ShapeDtypeStruct(slab, jnp.float32), jax.ShapeDtypeStruct((8, 8, 128), jnp.float32)),
         [VMEM] * 4,
         (mixed, first, diagonal, energy),
         scratch=[pltpu.VMEM(slab, jnp.float32), pltpu.VMEM(slab, jnp.bfloat16), pltpu.VMEM(slab, jnp.bfloat16)],
@@ -451,8 +455,9 @@
 
 
 def finish_kernel(count, totals_ref, precond_ref, out_ref):
-    grad_mean = jnp.sum(totals_ref[:8]) / count
-    cond_mean = jnp.sum(totals_ref[8:]) / count
+    totals = sum(totals_ref[piece] for piece in range(totals_ref.shape[0]))
+    grad_mean = jnp.sum(totals[:1]) / count
+    cond_mean = jnp.sum(totals[1:2]) / count
     factor = jnp.sqrt(grad_mean / (cond_mean + 1e-06))
     for row in range(0, out_ref.shape[0], 32):
         at = pl.ds(row, 32)
@@ -480,7 +485,8 @@
     rows_here = grad_partial.shape[2]
     owner = ("zl", "c")
     grads = grad_partial.reshape(2, 4, 4, rows_here, size)
-    place = jnp.stack([lax.axis_index(axis).astype(jnp.int32) for axis in ("x", "y", "zl", "c")])
+    x, y, zl, c = (lax.axis_index(axis).astype(jnp.int32) for axis in ("x", "y", "zl", "c"))
+    place = jnp.stack((x, y, zl, c))
 
     x_up, x_down, y_up, y_down = pack(send_kernel, 48, place, grads)
     x_ends = ring_first(x_up, x_down, "x")
@@ -502,9 +508,9 @@
     x_last = ring_first(*x_last, "x")
     y_last = ring_first(*y_last, "y")
 
-    lower_up, lower_down, lower_mid, lower_own = turn(1, place, x_own, *x_ends, *x_last)
+    lower_up, lower_down, lower_mid, lower_own = turn(y[None], x_own, *x_ends, *x_last)
     lower_ends = ring_first(lower_up, lower_down, "y")
-    upper_up, upper_down, upper_mid, upper_own = turn(0, place, y_own, *y_ends, *y_last)
+    upper_up, upper_down, upper_mid, upper_own = turn(x[None], y_own, *y_ends, *y_last)
     upper_ends = ring_first(upper_up, upper_down, "x")
     lower_last = ring_first(*pass_on(lower_mid, *lower_ends), "y")
     upper_last = ring_first(*pass_on(upper_mid, *upper_ends), "x")
@@ -517,8 +523,7 @@
     right = right_base(*after(mixed, right_slots))
     mixed = lax.all_to_all(mixed, owner, split_axis=0, concat_axis=0, tiled=True)
     precond, totals = condition(mixed, *right, energy)
-    totals = totals + swap(totals, "c", 1)
-    totals = totals + shift(totals, "zl", 1) + shift(totals, "zl", 2) + shift(totals, "zl", 3)
+    totals = lax.all_to_all(totals, owner, split_axis=0, concat_axis=0, tiled=True)
     return finish(totals, precond, float(size * size))[None]
 
 

time: 118 us -> 118 us (level)
  blocking collectives: 0 us -> 8.26 us
  waiting for transfers between devices: 46.8 us -> 42.3 us
  starting transfers between devices: 39.2 us -> 36 us
    all_to_all x0 -> x1, blocking collectives: none -> 8.26 us  [local(): lax.all_to_all(totals, owner, split_axis=0, concat_axis=0, tiled=True)]
    ppermute x22 -> x19, waiting for transfers between devices: 36.1 us -> 32.8 us  [shift(): lax.ppermute(array, axis, [(i, (i + step) % size) for i in range(size)])]
    ppermute x22 -> x19, starting transfers between devices: 27 us -> 24.8 us  [shift(): lax.ppermute(array, axis, [(i, (i + step) % size) for i in range(size)])]
    ppermute x5 -> x4, waiting for transfers between devices: 2.43 us -> 1.28 us  [swap(): return lax.ppermute(array, axis, [(i, i ^ mask) for i in range(size)])]
  transfers between devices with their start and end apart: 29 -> 25, of which waited for: 18 -> 14; matrix products, arithmetic and copies ran while one was open for 0% -> 0% of each run, Pallas kernels for 13% -> 13%
where the time goes in v3:
time: 118 us; the launch traced here: 116 us
  waiting for transfers between devices  42.3 us (36%)
  starting transfers between devices  36 us (31%)
  Pallas kernels  22.1 us (19%)
  blocking collectives  8.26 us (7%)
  local copies, waits for them, and re-layouts  6.32 us (5%)
    ppermute x19, waiting for transfers between devices, shift(): lax.ppermute(array, axis, [(i, (i + step) % size) for i in range(size)])  32.8 us
    ppermute x19, starting transfers between devices, shift(): lax.ppermute(array, axis, [(i, (i + step) % size) for i in range(size)])  24.8 us
    pallas_call x14, Pallas kernels, call(): pl.pallas_call(kernel, out_shape=out_shape, in_specs=in_specs, out_specs=...  13.5 us
    pallas_call x1, Pallas kernels, left_inverse_root(): pl.pallas_call(root_kernel, out_shape=(jax.ShapeDtypeStruct(matrix, jnp.b...  8.61 us
    all_to_all x1, blocking collectives, local(): lax.all_to_all(totals, owner, split_axis=0, concat_axis=0, tiled=True)  8.26 us
    all_to_all x1, waiting for transfers between devices, local(): lax.all_to_all(mixed, owner, split_axis=0, concat_axis=0, tiled=True)  7.01 us
    unnamed x16, local copies, waits for them, and re-layouts  6.32 us
    all_to_all x1, starting transfers between devices, local(): lax.all_to_all(pieces, ('zh',) + owner, split_axis=0, concat_axis=0, tile...  6.11 us
  transfers between devices with their start and end apart: 25, of which 14 were waited for; matrix products, arithmetic and copies ran while one was open for 0% of the time, Pallas kernels for 13%

profile of v3, /device:TPU:6, one launch (start us, length us, event | category | flops | bytes accessed | tf_op | source)
XLA Modules:
  0.0 115.8 jit_solution(17023645917275544218)
XLA Ops:
  0.1 3.5 %send.1 = (bf16[4,128,1024]{2,1,0:T(8,128)(2,1)S(1)}, bf16[4,128,1024]{2,1,0:T(8,128)(2,1)S(1)}, bf16[4,128,1024]{2,1,0:T(8,128)(2,1)S(1)}, bf16[4,128,1024]{2,1,0:T(8,128)(2,1)S(1)}) custom-call(s32[4]{0:T(128)S(1)} %pad_add_fusion.place_ref, bf16[2,4,4,128,1024]{4,3,2,1,0:T(8,128)(2,1)} %bitcast.7), custom_call_target="tpu_custom_call" | custom-call | bytes 8388608 | tf_op jit(solution)/shard_map/send/pallas_call | solution.py:46
  3.6 2.3 %collective-permute-start = (bf16[4,128,1024]{2,1,0:T(8,128)(2,1)S(1)}, bf16[4,128,1024]{2,1,0:T(8,128)(2,1)S(1)}, u32[]{:S(2)}, u32[]{:S(2)}) collective-permute-start(bf16[4,128,1024]{2,1,0:T(8,128)(2,1)S(1)} %get-tuple-element.50), channel_id=1, source_target_pairs={{0,8},{8,16},{16,24},{24,0},{1,9},{9,17},{17,25},{25,1},{2,10},{10... | collective-permute-start | bytes 3145736 | tf_op jit(solution)/shard_map/ppermute | solution.py:20
  5.9 1.4 %collective-permute-start.10 = (bf16[4,128,1024]{2,1,0:T(8,128)(2,1)S(1)}, bf16[4,128,1024]{2,1,0:T(8,128)(2,1)S(1)}, u32[]{:S(2)}, u32[]{:S(2)}) collective-permute-start(bf16[4,128,1024]{2,1,0:T(8,128)(2,1)S(1)} %get-tuple-element.66), channel_id=1, source_target_pairs={{0,32},{32,64},{64,96},{96,0},{1,33},{33,65},{65,97},{97,1},{2,34}... | collective-permute-start | bytes 3145736 | tf_op jit(solution)/shard_map/ppermute | solution.py:20
  7.3 1.9 %collective-permute-start.11 = (bf16[4,128,1024]{2,1,0:T(8,128)(2,1)S(1)}, bf16[4,128,1024]{2,1,0:T(8,128)(2,1)S(1)}, u32[]{:S(2)}, u32[]{:S(2)}) collective-permute-start(bf16[4,128,1024]{2,1,0:T(8,128)(2,1)S(1)} %get-tuple-element.67), channel_id=1, source_target_pairs={{0,96},{32,0},{64,32},{96,64},{1,97},{33,1},{65,33},{97,65},{2,98}... | collective-permute-start | bytes 3145736 | tf_op jit(solution)/shard_map/ppermute | solution.py:20
  9.8 1.2 %copy-done.3 = f32[1,1,256,1024]{3,2,1,0:T(8,128)S(1)} copy-done((f32[1,1,256,1024]{3,2,1,0:T(8,128)S(1)}, f32[1,1,256,1024]{3,2,1,0:T(8,128)}, u32[]{:S(2)}) %copy-start.3) | copy-done | bytes 1048600
  11.7 1.7 %collective-permute-start.2 = (bf16[256,640]{1,0:T(8,128)(2,1)S(1)}, bf16[256,640]{1,0:T(8,128)(2,1)S(1)}, u32[]{:S(2)}, u32[]{:S(2)}) collective-permute-start(bf16[256,640]{1,0:T(8,128)(2,1)S(1)} %trim.1.refs_0_), channel_id=1, source_target_pairs={{0,2},{2,4},{4,6},{6,0},{1,3},{3,5},{5,7},{7,1},{8,10},{10,12},{12... | collective-permute-start | bytes 983048 | tf_op jit(solution)/shard_map/ppermute | solution.py:20
  13.4 1.4 %keep.1 = (bf16[4,128,1024]{2,1,0:T(8,128)(2,1)S(1)}, bf16[4,128,1024]{2,1,0:T(8,128)(2,1)S(1)}, bf16[4,128,1024]{2,1,0:T(8,128)(2,1)S(1)}, bf16[4,128,1024]{2,1,0:T(8,128)(2,1)S(1)}) custom-call(s32[4]{0:T(128)S(1)} %pad_add_fusion.place_ref, bf16[2,4,4,128,1024]{4,3,2,1,0:T(8,128)(2,1)S(1)} %bitcast.8), custom_call_target="tpu_custom_call" | custom-call | bytes 8388608 | tf_op jit(solution)/shard_map/keep/pallas_call | solution.py:46
  14.9 8.0 %collective-permute-done.2.refs_2_ = bf16[256,640]{1,0:T(8,128)(2,1)S(1)} collective-permute-done((bf16[256,640]{1,0:T(8,128)(2,1)S(1)}, bf16[256,640]{1,0:T(8,128)(2,1)S(1)}, u32[]{:S(2)}, u32[]{:S(2)}) %collective-permute-start.2) | collective-permute-done | bytes 327712 | tf_op jit(solution)/shard_map/ppermute | solution.py:20
  22.8 9.6 %collective-permute-done.3.refs_4_ = bf16[256,640]{1,0:T(8,128)(2,1)S(1)} collective-permute-done((bf16[256,640]{1,0:T(8,128)(2,1)S(1)}, bf16[256,640]{1,0:T(8,128)(2,1)S(1)}, u32[]{:S(2)}, u32[]{:S(2)}) %collective-permute-start.3) | collective-permute-done | bytes 327712 | tf_op jit(solution)/shard_map/ppermute | solution.py:20
  33.7 1.1 collective-permute-start.5
  35.2 3.2 %collective-permute-start.13 = (bf16[2,128,1024]{2,1,0:T(8,128)(2,1)S(1)}, bf16[2,128,1024]{2,1,0:T(8,128)(2,1)S(1)}, u32[]{:S(2)}, u32[]{:S(2)}) collective-permute-start(bf16[2,128,1024]{2,1,0:T(8,128)(2,1)S(1)} %get-tuple-element.70), channel_id=1, source_target_pairs={{0,96},{32,0},{64,32},{96,64},{1,97},{33,1},{65,33},{97,65},{2,98}... | collective-permute-start | bytes 1572872 | tf_op jit(solution)/shard_map/ppermute | solution.py:20
  38.4 5.5 %collective-permute-done.4.last_up_ref = bf16[2,128,1024]{2,1,0:T(8,128)(2,1)S(1)} collective-permute-done((bf16[2,128,1024]{2,1,0:T(8,128)(2,1)S(1)}, bf16[2,128,1024]{2,1,0:T(8,128)(2,1)S(1)}, u32[]{:S(2)}, u32[]{:S(2)}) %collective-permute-start.4) | collective-permute-done | bytes 524320 | tf_op jit(solution)/shard_map/ppermute | solution.py:20
  43.9 1.3 %collective-permute-done.5.last_down_ref = bf16[2,128,1024]{2,1,0:T(8,128)(2,1)S(1)} collective-permute-done((bf16[2,128,1024]{2,1,0:T(8,128)(2,1)S(1)}, bf16[2,128,1024]{2,1,0:T(8,128)(2,1)S(1)}, u32[]{:S(2)}, u32[]{:S(2)}) %collective-permute-start.5) | collective-permute-done | bytes 524320 | tf_op jit(solution)/shard_map/ppermute | solution.py:20
  45.6 1.4 %collective-permute-start.6 = (bf16[2,64,1024]{2,1,0:T(8,128)(2,1)S(1)}, bf16[2,64,1024]{2,1,0:T(8,128)(2,1)S(1)}, u32[]{:S(2)}, u32[]{:S(2)}) collective-permute-start(bf16[2,64,1024]{2,1,0:T(8,128)(2,1)S(1)} %get-tuple-element.60), channel_id=1, source_target_pairs={{0,32},{32,64},{64,96},{96,0},{1,33},{33,65},{65,97},{97,1},{2,34}... | collective-permute-start | bytes 786440 | tf_op jit(solution)/shard_map/ppermute | solution.py:20
  47.0 1.9 %collective-permute-start.7 = (bf16[2,64,1024]{2,1,0:T(8,128)(2,1)S(1)}, bf16[2,64,1024]{2,1,0:T(8,128)(2,1)S(1)}, u32[]{:S(2)}, u32[]{:S(2)}) collective-permute-start(bf16[2,64,1024]{2,1,0:T(8,128)(2,1)S(1)} %get-tuple-element.61), channel_id=1, source_target_pairs={{0,96},{32,0},{64,32},{96,64},{1,97},{33,1},{65,33},{97,65},{2,98}... | collective-permute-start | bytes 786440 | tf_op jit(solution)/shard_map/ppermute | solution.py:20
  49.4 2.3 %collective-permute-start.14 = (bf16[2,64,1024]{2,1,0:T(8,128)(2,1)S(1)}, bf16[2,64,1024]{2,1,0:T(8,128)(2,1)S(1)}, u32[]{:S(2)}, u32[]{:S(2)}) collective-permute-start(bf16[2,64,1024]{2,1,0:T(8,128)(2,1)S(1)} %get-tuple-element.72), channel_id=1, source_target_pairs={{0,8},{8,16},{16,24},{24,0},{1,9},{9,17},{17,25},{25,1},{2,10},{10... | collective-permute-start | bytes 786440 | tf_op jit(solution)/shard_map/ppermute | solution.py:20
  55.3 2.4 %collective-permute-start.9 = (bf16[1,64,1024]{2,1,0:T(8,128)(2,1)S(1)}, bf16[1,64,1024]{2,1,0:T(8,128)(2,1)S(1)}, u32[]{:S(2)}, u32[]{:S(2)}) collective-permute-start(bf16[1,64,1024]{2,1,0:T(8,128)(2,1)S(1)} %get-tuple-element.64), channel_id=1, source_target_pairs={{0,96},{32,0},{64,32},{96,64},{1,97},{33,1},{65,33},{97,65},{2,98}... | collective-permute-start | bytes 393224 | tf_op jit(solution)/shard_map/ppermute | solution.py:20
  57.6 2.7 %collective-permute-done.15.down_ref.refs_7_ = bf16[2,64,1024]{2,1,0:T(8,128)(2,1)S(1)} collective-permute-done((bf16[2,64,1024]{2,1,0:T(8,128)(2,1)S(1)}, bf16[2,64,1024]{2,1,0:T(8,128)(2,1)S(1)}, u32[]{:S(2)}, u32[]{:S(2)}) %collective-permute-start.15) | collective-permute-done | bytes 262176 | tf_op jit(solution)/shard_map/ppermute | solution.py:20
  60.5 2.0 %collective-permute-start.17 = (bf16[1,64,1024]{2,1,0:T(8,128)(2,1)S(1)}, bf16[1,64,1024]{2,1,0:T(8,128)(2,1)S(1)}, u32[]{:S(2)}, u32[]{:S(2)}) collective-permute-start(bf16[1,64,1024]{2,1,0:T(8,128)(2,1)S(1)} %get-tuple-element.76), channel_id=1, source_target_pairs={{0,24},{8,0},{16,8},{24,16},{1,25},{9,1},{17,9},{25,17},{2,26},{10... | collective-permute-start | bytes 393224 | tf_op jit(solution)/shard_map/ppermute | solution.py:20
  62.5 2.9 %collective-permute-done.16.refs_8_ = bf16[1,64,1024]{2,1,0:T(8,128)(2,1)S(1)} collective-permute-done((bf16[1,64,1024]{2,1,0:T(8,128)(2,1)S(1)}, bf16[1,64,1024]{2,1,0:T(8,128)(2,1)S(1)}, u32[]{:S(2)}, u32[]{:S(2)}) %collective-permute-start.16) | collective-permute-done | bytes 131104 | tf_op jit(solution)/shard_map/ppermute | solution.py:20
  65.4 1.3 %collective-permute-done.17.refs_9_ = bf16[1,64,1024]{2,1,0:T(8,128)(2,1)S(1)} collective-permute-done((bf16[1,64,1024]{2,1,0:T(8,128)(2,1)S(1)}, bf16[1,64,1024]{2,1,0:T(8,128)(2,1)S(1)}, u32[]{:S(2)}, u32[]{:S(2)}) %collective-permute-start.17) | collective-permute-done | bytes 131104 | tf_op jit(solution)/shard_map/ppermute | solution.py:20
  67.7 6.1 %all-to-all-start = ((bf16[16,128,128]{2,1,0:T(8,128)(2,1)}), bf16[16,128,128]{2,1,0:T(8,128)(2,1)S(1)}, u32[]{:S(2)}, u32[]{:S(2)}) async-start(bf16[16,128,128]{2,1,0:T(8,128)(2,1)} %pieces.1), calls=%async_computation | async-start | bytes 1048576 | tf_op jit(solution)/shard_map/all_to_all | solution.py:520
  78.9 8.6 %left_root.1 = (bf16[1024,1024]{1,0:T(8,128)(2,1)S(1)}, bf16[4,256,640]{2,1,0:T(8,128)(2,1)S(1)}) custom-call(s32[4]{0:T(128)S(1)} %pad_add_fusion.place_ref, s32[1]{0:T(128)S(6)} %copy.4.table_ref, bf16[256,640]{1,0:T(8,128)(2,1)S(1)} %trim.1.refs_0_, bf16[256,640]{1,0:T(8,128)(2,1)S(1)} %collective-permute-done.18.refs_1_, ...), custom_call_target="tpu_custom_call" | custom-call | flops 6442450944 | bytes 4194304 | tf_op jit(solution)/shard_map/left_root/pallas_call | solution.py:307
  87.5 1.1 copy-done.1
  88.6 1.2 %all-to-all-done.pieces_ref = bf16[16,128,128]{2,1,0:T(8,128)(2,1)S(1)} async-done(((bf16[16,128,128]{2,1,0:T(8,128)(2,1)}), bf16[16,128,128]{2,1,0:T(8,128)(2,1)S(1)}, u32[]{:S(2)}, u32[]{:S(2)}) %all-to-all-start) | async-done | bytes 524320 | tf_op jit(solution)/shard_map/all_to_all | solution.py:520
  89.9 1.5 %mix.1 = (bf16[8,128,128]{2,1,0:T(8,128)(2,1)}, f32[8,128]{1,0:T(8,128)S(1)}) custom-call(bf16[16,128,128]{2,1,0:T(8,128)(2,1)S(1)} %all-to-all-done.pieces_ref, bf16[1024,1024]{1,0:T(8,128)(2,1)S(1)} %get-tuple-element.86.left_ref), custom_call_target="tpu_custom_call" | custom-call | flops 268435456 | bytes 2097152 | tf_op jit(solution)/shard_map/mix/pallas_call | solution.py:46
  91.3 4.0 %all-to-all-start.1 = ((bf16[8,128,128]{2,1,0:T(8,128)(2,1)}), bf16[8,128,128]{2,1,0:T(8,128)(2,1)S(1)}, u32[]{:S(2)}, u32[]{:S(2)}) async-start(bf16[8,128,128]{2,1,0:T(8,128)(2,1)} %get-tuple-element.87), calls=%async_computation.1 | async-start | bytes 524288 | tf_op jit(solution)/shard_map/all_to_all | solution.py:524
  95.3 1.3 %copy-done.2 = bf16[4,256,640]{2,1,0:T(8,128)(2,1)S(1)} copy-done((bf16[4,256,640]{2,1,0:T(8,128)(2,1)S(1)}, bf16[4,256,640]{2,1,0:T(8,128)(2,1)}, u32[]{:S(2)}) %copy-start.2) | copy-done | bytes 1310744
  96.6 1.4 %right_base.1 = (bf16[1024,1024]{1,0:T(8,128)(2,1)S(1)}, f32[8,1024]{1,0:T(8,128)S(1)}) custom-call(bf16[4,256,640]{2,1,0:T(8,128)(2,1)S(1)} %copy-done.2), custom_call_target="tpu_custom_call" | custom-call | flops 4194304 | bytes 4194304 | tf_op jit(solution)/shard_map/right_base/pallas_call | solution.py:46
  98.1 7.0 %all-to-all-done.1.mixed_ref = bf16[8,128,128]{2,1,0:T(8,128)(2,1)S(1)} async-done(((bf16[8,128,128]{2,1,0:T(8,128)(2,1)}), bf16[8,128,128]{2,1,0:T(8,128)(2,1)S(1)}, u32[]{:S(2)}, u32[]{:S(2)}) %all-to-all-start.1) | async-done | bytes 262176 | tf_op jit(solution)/shard_map/all_to_all | solution.py:524
  105.1 1.4 %condition.1 = (f32[128,1024]{1,0:T(8,128)S(1)}, f32[8,8,128]{2,1,0:T(8,128)S(1)}) custom-call(bf16[8,128,128]{2,1,0:T(8,128)(2,1)S(1)} %all-to-all-done.1.mixed_ref, bf16[1024,1024]{1,0:T(8,128)(2,1)S(1)} %get-tuple-element.90.first_ref, f32[8,1024]{1,0:T(8,128)S(1)} %get-tuple-element.91.diagonal_ref, f32[8,128]{1,0:T(8,128)S(1)} %get-tuple-element.92.energy_ref), custom_call_target="tpu_custom_call" | custom-call | flops 1073741824 | bytes 2097152 | tf_op jit(solution)/shard_map/condition/pallas_call | solution.py:46
  106.5 8.3 %all_to_all.15.totals_ref = f32[8,8,128]{2,1,0:T(8,128)S(1)} all-to-all(f32[8,8,128]{2,1,0:T(8,128)S(1)} %get-tuple-element.93), channel_id=1, replica_groups=mesh['zh'=2,'y'=4,'x'=4,'zl'=4,'c'=2] {'zl','c'}, dimensions={0} | all-to-all | bytes 65536 | tf_op jit(solution)/shard_map/all_to_all | solution.py:526
  (51 shorter events, 14.2 us)
Async XLA Ops:
  0.1 13.3 %copy-start = (bf16[1,32,128,1024]{3,2,1,0:T(8,128)(2,1)S(1)}, bf16[1,32,128,1024]{3,2,1,0:T(8,128)(2,1)}, u32[]{:S(2)}) copy-start(bf16[1,32,128,1024]{3,2,1,0:T(8,128)(2,1)} %param.3) | copy-start | bytes 25165828
  3.6 28.8 %collective-permute-start = (bf16[4,128,1024]{2,1,0:T(8,128)(2,1)S(1)}, bf16[4,128,1024]{2,1,0:T(8,128)(2,1)S(1)}, u32[]{:S(2)}, u32[]{:S(2)}) collective-permute-start(bf16[4,128,1024]{2,1,0:T(8,128)(2,1)S(1)} %get-tuple-element.50), channel_id=1, source_target_pairs={{0,8},{8,16},{16,24},{24,0},{1,9},{9,17},{17,25},{25,1},{2,10},{10... | collective-permute-start | bytes 3145736 | tf_op jit(solution)/shard_map/ppermute | solution.py:20
  5.9 26.6 %collective-permute-start.1 = (bf16[4,128,1024]{2,1,0:T(8,128)(2,1)S(1)}, bf16[4,128,1024]{2,1,0:T(8,128)(2,1)S(1)}, u32[]{:S(2)}, u32[]{:S(2)}) collective-permute-start(bf16[4,128,1024]{2,1,0:T(8,128)(2,1)S(1)} %get-tuple-element.53), channel_id=1, source_target_pairs={{0,24},{8,0},{16,8},{24,16},{1,25},{9,1},{17,9},{25,17},{2,26},{10... | collective-permute-start | bytes 3145736 | tf_op jit(solution)/shard_map/ppermute | solution.py:20
  5.9 28.9 %collective-permute-start.10 = (bf16[4,128,1024]{2,1,0:T(8,128)(2,1)S(1)}, bf16[4,128,1024]{2,1,0:T(8,128)(2,1)S(1)}, u32[]{:S(2)}, u32[]{:S(2)}) collective-permute-start(bf16[4,128,1024]{2,1,0:T(8,128)(2,1)S(1)} %get-tuple-element.66), channel_id=1, source_target_pairs={{0,32},{32,64},{64,96},{96,0},{1,33},{33,65},{65,97},{97,1},{2,34}... | collective-permute-start | bytes 3145736 | tf_op jit(solution)/shard_map/ppermute | solution.py:20
  7.3 27.5 %collective-permute-start.11 = (bf16[4,128,1024]{2,1,0:T(8,128)(2,1)S(1)}, bf16[4,128,1024]{2,1,0:T(8,128)(2,1)S(1)}, u32[]{:S(2)}, u32[]{:S(2)}) collective-permute-start(bf16[4,128,1024]{2,1,0:T(8,128)(2,1)S(1)} %get-tuple-element.67), channel_id=1, source_target_pairs={{0,96},{32,0},{64,32},{96,64},{1,97},{33,1},{65,33},{97,65},{2,98}... | collective-permute-start | bytes 3145736 | tf_op jit(solution)/shard_map/ppermute | solution.py:20
  9.8 1.2 %copy-start.3 = (f32[1,1,256,1024]{3,2,1,0:T(8,128)S(1)}, f32[1,1,256,1024]{3,2,1,0:T(8,128)}, u32[]{:S(2)}) copy-start(f32[1,1,256,1024]{3,2,1,0:T(8,128)} %param.4) | copy-start | bytes 3145732
  11.7 11.2 %collective-permute-start.2 = (bf16[256,640]{1,0:T(8,128)(2,1)S(1)}, bf16[256,640]{1,0:T(8,128)(2,1)S(1)}, u32[]{:S(2)}, u32[]{:S(2)}) collective-permute-start(bf16[256,640]{1,0:T(8,128)(2,1)S(1)} %trim.1.refs_0_), channel_id=1, source_target_pairs={{0,2},{2,4},{4,6},{6,0},{1,3},{3,5},{5,7},{7,1},{8,10},{10,12},{12... | collective-permute-start | bytes 983048 | tf_op jit(solution)/shard_map/ppermute | solution.py:20
  22.8 9.6 %collective-permute-start.3 = (bf16[256,640]{1,0:T(8,128)(2,1)S(1)}, bf16[256,640]{1,0:T(8,128)(2,1)S(1)}, u32[]{:S(2)}, u32[]{:S(2)}) collective-permute-start(bf16[256,640]{1,0:T(8,128)(2,1)S(1)} %collective-permute-done.2.refs_2_), channel_id=1, source_target_pairs={{0,2},{2,4},{4,6},{6,0},{1,3},{3,5},{5,7},{7,1},{8,10},{10,12},{12... | collective-permute-start | bytes 983048 | tf_op jit(solution)/shard_map/ppermute | solution.py:20
  32.4 42.0 %copy-start.4 = (bf16[256,640]{1,0:T(8,128)(2,1)}, bf16[256,640]{1,0:T(8,128)(2,1)S(1)}, u32[]{:S(2)}) copy-start(bf16[256,640]{1,0:T(8,128)(2,1)S(1)} %collective-permute-done.3.refs_4_) | copy-start | bytes 983044
  32.7 11.2 %collective-permute-start.4 = (bf16[2,128,1024]{2,1,0:T(8,128)(2,1)S(1)}, bf16[2,128,1024]{2,1,0:T(8,128)(2,1)S(1)}, u32[]{:S(2)}, u32[]{:S(2)}) collective-permute-start(bf16[2,128,1024]{2,1,0:T(8,128)(2,1)S(1)} %get-tuple-element.57), channel_id=1, source_target_pairs={{0,8},{8,16},{16,24},{24,0},{1,9},{9,17},{17,25},{25,1},{2,10},{10... | collective-permute-start | bytes 1572872 | tf_op jit(solution)/shard_map/ppermute | solution.py:20
  33.7 11.4 %collective-permute-start.5 = (bf16[2,128,1024]{2,1,0:T(8,128)(2,1)S(1)}, bf16[2,128,1024]{2,1,0:T(8,128)(2,1)S(1)}, u32[]{:S(2)}, u32[]{:S(2)}) collective-permute-start(bf16[2,128,1024]{2,1,0:T(8,128)(2,1)S(1)} %get-tuple-element.58), channel_id=1, source_target_pairs={{0,24},{8,0},{16,8},{24,16},{1,25},{9,1},{17,9},{25,17},{2,26},{10... | collective-permute-start | bytes 1572872 | tf_op jit(solution)/shard_map/ppermute | solution.py:20
  35.0 13.9 %collective-permute-start.12 = (bf16[2,128,1024]{2,1,0:T(8,128)(2,1)S(1)}, bf16[2,128,1024]{2,1,0:T(8,128)(2,1)S(1)}, u32[]{:S(2)}, u32[]{:S(2)}) collective-permute-start(bf16[2,128,1024]{2,1,0:T(8,128)(2,1)S(1)} %get-tuple-element.69), channel_id=1, source_target_pairs={{0,32},{32,64},{64,96},{96,0},{1,33},{33,65},{65,97},{97,1},{2,34}... | collective-permute-start | bytes 1572872 | tf_op jit(solution)/shard_map/ppermute | solution.py:20
  35.2 13.7 %collective-permute-start.13 = (bf16[2,128,1024]{2,1,0:T(8,128)(2,1)S(1)}, bf16[2,128,1024]{2,1,0:T(8,128)(2,1)S(1)}, u32[]{:S(2)}, u32[]{:S(2)}) collective-permute-start(bf16[2,128,1024]{2,1,0:T(8,128)(2,1)S(1)} %get-tuple-element.70), channel_id=1, source_target_pairs={{0,96},{32,0},{64,32},{96,64},{1,97},{33,1},{65,33},{97,65},{2,98}... | collective-permute-start | bytes 1572872 | tf_op jit(solution)/shard_map/ppermute | solution.py:20
  45.6 7.7 %collective-permute-start.6 = (bf16[2,64,1024]{2,1,0:T(8,128)(2,1)S(1)}, bf16[2,64,1024]{2,1,0:T(8,128)(2,1)S(1)}, u32[]{:S(2)}, u32[]{:S(2)}) collective-permute-start(bf16[2,64,1024]{2,1,0:T(8,128)(2,1)S(1)} %get-tuple-element.60), channel_id=1, source_target_pairs={{0,32},{32,64},{64,96},{96,0},{1,33},{33,65},{65,97},{97,1},{2,34}... | collective-permute-start | bytes 786440 | tf_op jit(solution)/shard_map/ppermute | solution.py:20
  47.0 7.2 %collective-permute-start.7 = (bf16[2,64,1024]{2,1,0:T(8,128)(2,1)S(1)}, bf16[2,64,1024]{2,1,0:T(8,128)(2,1)S(1)}, u32[]{:S(2)}, u32[]{:S(2)}) collective-permute-start(bf16[2,64,1024]{2,1,0:T(8,128)(2,1)S(1)} %get-tuple-element.61), channel_id=1, source_target_pairs={{0,96},{32,0},{64,32},{96,64},{1,97},{33,1},{65,33},{97,65},{2,98}... | collective-permute-start | bytes 786440 | tf_op jit(solution)/shard_map/ppermute | solution.py:20
  49.4 8.2 %collective-permute-start.14 = (bf16[2,64,1024]{2,1,0:T(8,128)(2,1)S(1)}, bf16[2,64,1024]{2,1,0:T(8,128)(2,1)S(1)}, u32[]{:S(2)}, u32[]{:S(2)}) collective-permute-start(bf16[2,64,1024]{2,1,0:T(8,128)(2,1)S(1)} %get-tuple-element.72), channel_id=1, source_target_pairs={{0,8},{8,16},{16,24},{24,0},{1,9},{9,17},{17,25},{25,1},{2,10},{10... | collective-permute-start | bytes 786440 | tf_op jit(solution)/shard_map/ppermute | solution.py:20
  51.7 8.6 %collective-permute-start.15 = (bf16[2,64,1024]{2,1,0:T(8,128)(2,1)S(1)}, bf16[2,64,1024]{2,1,0:T(8,128)(2,1)S(1)}, u32[]{:S(2)}, u32[]{:S(2)}) collective-permute-start(bf16[2,64,1024]{2,1,0:T(8,128)(2,1)S(1)} %get-tuple-element.73), channel_id=1, source_target_pairs={{0,24},{8,0},{16,8},{24,16},{1,25},{9,1},{17,9},{25,17},{2,26},{10... | collective-permute-start | bytes 786440 | tf_op jit(solution)/shard_map/ppermute | solution.py:20
  51.7 23.1 %collective-permute-start.21 = (bf16[256,640]{1,0:T(8,128)(2,1)S(1)}, bf16[256,640]{1,0:T(8,128)(2,1)S(1)}, u32[]{:S(2)}, u32[]{:S(2)}) collective-permute-start(bf16[256,640]{1,0:T(8,128)(2,1)S(1)} %collective-permute-done.3.refs_4_), channel_id=1, source_target_pairs={{0,2},{2,4},{4,6},{6,0},{1,3},{3,5},{5,7},{7,1},{8,10},{10,12},{12... | collective-permute-start | bytes 983048 | tf_op jit(solution)/shard_map/ppermute | solution.py:20
  54.3 8.2 %collective-permute-start.8 = (bf16[1,64,1024]{2,1,0:T(8,128)(2,1)S(1)}, bf16[1,64,1024]{2,1,0:T(8,128)(2,1)S(1)}, u32[]{:S(2)}, u32[]{:S(2)}) collective-permute-start(bf16[1,64,1024]{2,1,0:T(8,128)(2,1)S(1)} %get-tuple-element.63), channel_id=1, source_target_pairs={{0,32},{32,64},{64,96},{96,0},{1,33},{33,65},{65,97},{97,1},{2,34}... | collective-permute-start | bytes 393224 | tf_op jit(solution)/shard_map/ppermute | solution.py:20
  55.3 7.2 %collective-permute-start.9 = (bf16[1,64,1024]{2,1,0:T(8,128)(2,1)S(1)}, bf16[1,64,1024]{2,1,0:T(8,128)(2,1)S(1)}, u32[]{:S(2)}, u32[]{:S(2)}) collective-permute-start(bf16[1,64,1024]{2,1,0:T(8,128)(2,1)S(1)} %get-tuple-element.64), channel_id=1, source_target_pairs={{0,96},{32,0},{64,32},{96,64},{1,97},{33,1},{65,33},{97,65},{2,98}... | collective-permute-start | bytes 393224 | tf_op jit(solution)/shard_map/ppermute | solution.py:20
  60.4 5.0 %collective-permute-start.16 = (bf16[1,64,1024]{2,1,0:T(8,128)(2,1)S(1)}, bf16[1,64,1024]{2,1,0:T(8,128)(2,1)S(1)}, u32[]{:S(2)}, u32[]{:S(2)}) collective-permute-start(bf16[1,64,1024]{2,1,0:T(8,128)(2,1)S(1)} %get-tuple-element.75), channel_id=1, source_target_pairs={{0,8},{8,16},{16,24},{24,0},{1,9},{9,17},{17,25},{25,1},{2,10},{10... | collective-permute-start | bytes 393224 | tf_op jit(solution)/shard_map/ppermute | solution.py:20
  60.5 6.3 %collective-permute-start.17 = (bf16[1,64,1024]{2,1,0:T(8,128)(2,1)S(1)}, bf16[1,64,1024]{2,1,0:T(8,128)(2,1)S(1)}, u32[]{:S(2)}, u32[]{:S(2)}) collective-permute-start(bf16[1,64,1024]{2,1,0:T(8,128)(2,1)S(1)} %get-tuple-element.76), channel_id=1, source_target_pairs={{0,24},{8,0},{16,8},{24,16},{1,25},{9,1},{17,9},{25,17},{2,26},{10... | collective-permute-start | bytes 393224 | tf_op jit(solution)/shard_map/ppermute | solution.py:20
  67.7 22.1 %all-to-all-start = ((bf16[16,128,128]{2,1,0:T(8,128)(2,1)}), bf16[16,128,128]{2,1,0:T(8,128)(2,1)S(1)}, u32[]{:S(2)}, u32[]{:S(2)}) async-start(bf16[16,128,128]{2,1,0:T(8,128)(2,1)} %pieces.1), calls=%async_computation | async-start | bytes 1048576 | tf_op jit(solution)/shard_map/all_to_all | solution.py:520
  73.8 1.8 %collective-permute-start.18 = (bf16[256,640]{1,0:T(8,128)(2,1)S(1)}, bf16[256,640]{1,0:T(8,128)(2,1)S(1)}, u32[]{:S(2)}, u32[]{:S(2)}) collective-permute-start(bf16[256,640]{1,0:T(8,128)(2,1)S(1)} %trim.1.refs_0_), channel_id=1, source_target_pairs={{0,1},{1,0},{2,3},{3,2},{4,5},{5,4},{6,7},{7,6},{8,9},{9,8},{10,11... | collective-permute-start | bytes 983048 | tf_op jit(solution)/shard_map/ppermute | solution.py:25
  74.2 1.8 %collective-permute-start.19 = (bf16[256,640]{1,0:T(8,128)(2,1)S(1)}, bf16[256,640]{1,0:T(8,128)(2,1)S(1)}, u32[]{:S(2)}, u32[]{:S(2)}) collective-permute-start(bf16[256,640]{1,0:T(8,128)(2,1)S(1)} %collective-permute-done.2.refs_2_), channel_id=1, source_target_pairs={{0,1},{1,0},{2,3},{3,2},{4,5},{5,4},{6,7},{7,6},{8,9},{9,8},{10,11... | collective-permute-start | bytes 983048 | tf_op jit(solution)/shard_map/ppermute | solution.py:25
  74.4 2.1 %collective-permute-start.20 = (bf16[256,640]{1,0:T(8,128)(2,1)S(1)}, bf16[256,640]{1,0:T(8,128)(2,1)S(1)}, u32[]{:S(2)}, u32[]{:S(2)}) collective-permute-start(bf16[256,640]{1,0:T(8,128)(2,1)S(1)} %collective-permute-done.3.refs_4_), channel_id=1, source_target_pairs={{0,1},{1,0},{2,3},{3,2},{4,5},{5,4},{6,7},{7,6},{8,9},{9,8},{10,11... | collective-permute-start | bytes 983048 | tf_op jit(solution)/shard_map/ppermute | solution.py:25
  74.8 2.2 %collective-permute-start.22 = (bf16[256,640]{1,0:T(8,128)(2,1)S(1)}, bf16[256,640]{1,0:T(8,128)(2,1)S(1)}, u32[]{:S(2)}, u32[]{:S(2)}) collective-permute-start(bf16[256,640]{1,0:T(8,128)(2,1)S(1)} %collective-permute-done.21.refs_6_), channel_id=1, source_target_pairs={{0,1},{1,0},{2,3},{3,2},{4,5},{5,4},{6,7},{7,6},{8,9},{9,8},{10,11... | collective-permute-start | bytes 983048 | tf_op jit(solution)/shard_map/ppermute | solution.py:25
  77.0 1.0 copy-start.5
  77.9 1.0 copy-start.7
  87.5 1.1 copy-start.1
  91.3 13.7 %all-to-all-start.1 = ((bf16[8,128,128]{2,1,0:T(8,128)(2,1)}), bf16[8,128,128]{2,1,0:T(8,128)(2,1)S(1)}, u32[]{:S(2)}, u32[]{:S(2)}) async-start(bf16[8,128,128]{2,1,0:T(8,128)(2,1)} %get-tuple-element.87), calls=%async_computation.1 | async-start | bytes 524288 | tf_op jit(solution)/shard_map/all_to_all | solution.py:524
  95.3 1.3 %copy-start.2 = (bf16[4,256,640]{2,1,0:T(8,128)(2,1)S(1)}, bf16[4,256,640]{2,1,0:T(8,128)(2,1)}, u32[]{:S(2)}) copy-start(bf16[4,256,640]{2,1,0:T(8,128)(2,1)} %copy-done.1) | copy-start | bytes 3932164
  (1 other events, 0.7 us)

commit v4 on v3

--- a/solution.py
+++ b/solution.py
@@ -377,8 +377,9 @@
     return sum(total[:, at : at + 128] for at in range(0, columns, 128))
 
 
-def mix_kernel(pieces_ref, left_ref, out_ref, energy_ref, grad_ref):
-    count, rows, _ = out_ref.shape
+def mix_kernel(zl_ref, pieces_ref, left_ref, *refs):
+    out_refs, (energy_ref, grad_ref, held_ref) = refs[:4], refs[4:]
+    count, rows = pieces_ref.shape[0] // 2, pieces_ref.shape[1]
     energy = jnp.zeros(energy_ref.shape, jnp.float32)
     for piece in range(count):
         grad = narrow(pieces_ref[piece], pieces_ref[count + piece])
@@ -390,28 +391,51 @@
         product = jnp.dot(
             left_ref[pl.ds(piece * rows, 2 * rows), :], grad_ref[...], preferred_element_type=jnp.float32
         ).astype(jnp.bfloat16)
-        out_ref[piece] = product[:rows]
-        out_ref[piece + 1] = product[rows:]
-
-
-def mix(pieces, left_root):
+        held_ref[piece // 2, 0] = product[:rows]
+        held_ref[piece // 2, 1] = product[rows:]
+    for step, out_ref in enumerate(out_refs):
+        out_ref[...] = held_ref[lax.rem(zl_ref[0] + step, 4)]
+
+
+def mix(zl, pieces, left_root):
     _, rows, width = pieces.shape
+    out = jax.ShapeDtypeStruct((2, rows, width), jnp.bfloat16)
     return call(
         mix_kernel,
         "mix",
-        (jax.ShapeDtypeStruct((8, rows, width), jnp.bfloat16), jax.ShapeDtypeStruct((8, 128), jnp.float32)),
-        [VMEM] * 2,
-        (pieces, left_root),
-        scratch=[pltpu.VMEM((8 * rows, width), jnp.bfloat16)],
+        (out,) * 4 + (jax.ShapeDtypeStruct((8, 128), jnp.float32),),
+        [SMEM] + [VMEM] * 2,
+        (zl, pieces, left_root),
+        scratch=[pltpu.VMEM((8 * rows, width), jnp.bfloat16), pltpu.VMEM((4,) + out.shape, jnp.bfloat16)],
         flops=2 * left_root.size * width,
         moved=2 * left_root.size,
     )
 
 
-def condition_kernel(mixed_ref, first_ref, diagonal_ref, energy_ref, out_ref, totals_ref, wide_ref, even_ref, odd_ref):
-    count, _, width = mixed_ref.shape
+def split_kernel(c_ref, *refs):
+    got, out_ref = refs[:4], refs[4]
+    for step, ref in enumerate(got):
+        out_ref[step] = ref[1 - c_ref[0]]
+
+
+def exchange(c, mixed, dep):
+    got = after(dep, mixed[0]) + tuple(shift(each, "zl", step) for step, each in enumerate(mixed) if step)
+    give = jax.ShapeDtypeStruct((4,) + mixed[0].shape[1:], mixed[0].dtype)
+    give = call(split_kernel, "split", give, [SMEM] + [VMEM] * 4, (c,) + got, moved=4 * give.size)
+    return got + (swap(give, "c", 1),)
+
+
+def condition_kernel(zl_ref, c_ref, *refs):
+    got, other_ref, refs = refs[:4], refs[4], refs[5:]
+    first_ref, diagonal_ref, energy_ref, out_ref, totals_ref, wide_ref, even_ref, odd_ref, held_ref = refs
+    count, _, width = held_ref.shape
+    zl, c = zl_ref[0], c_ref[0]
+    for step, ref in enumerate(got):
+        chip = lax.rem(zl + (4 - step), 4)
+        held_ref[2 * chip + c] = ref[c]
+        held_ref[2 * chip + 1 - c] = other_ref[step]
     for piece in range(count):
-        odd_ref[:, pl.ds(piece * width, width)] = mixed_ref[piece]
+        odd_ref[:, pl.ds(piece * width, width)] = held_ref[piece]
 
     def products(slab_ref):
         for column in range(0, out_ref.shape[1], 2 * width):
@@ -439,16 +463,16 @@
         totals_ref[piece] = sums
 
 
-def condition(mixed, first, diagonal, energy):
-    _, rows, width = mixed.shape
+def condition(zl, c, mixed, first, diagonal, energy):
+    _, rows, width = mixed[0].shape
     slab = (rows, 8 * width)
     return call(
         condition_kernel,
         "condition",
         (jax.ShapeDtypeStruct(slab, jnp.float32), jax.ShapeDtypeStruct((8, 8, 128), jnp.float32)),
-        [VMEM] * 4,
-        (mixed, first, diagonal, energy),
-        scratch=[pltpu.VMEM(slab, jnp.float32), pltpu.VMEM(slab, jnp.bfloat16), pltpu.VMEM(slab, jnp.bfloat16)],
+        [SMEM] * 2 + [VMEM] * 8,
+        (zl, c) + mixed + (first, diagonal, energy),
+        scratch=[pltpu.VMEM(slab, jnp.float32), pltpu.VMEM(slab, jnp.bfloat16), pltpu.VMEM(slab, jnp.bfloat16), pltpu.VMEM((8, rows, width), jnp.bfloat16)],
         flops=8 * rows * first.size,
         moved=2 * first.size,
     )
@@ -519,10 +543,10 @@
     slots = after(pieces, *slots)
     pieces = lax.all_to_all(pieces, ("zh",) + owner, split_axis=0, concat_axis=0, tiled=True)
     left_root, right_slots = left_inverse_root(place, owner_table, slots)
-    mixed, energy = mix(pieces, left_root)
-    right = right_base(*after(mixed, right_slots))
-    mixed = lax.all_to_all(mixed, owner, split_axis=0, concat_axis=0, tiled=True)
-    precond, totals = condition(mixed, *right, energy)
+    *mixed, energy = mix(zl[None], pieces, left_root)
+    right = right_base(*after(mixed[0], right_slots))
+    mixed = exchange(c[None], tuple(mixed), right[0])
+    precond, totals = condition(zl[None], c[None], mixed, *right, energy)
     totals = lax.all_to_all(totals, owner, split_axis=0, concat_axis=0, tiled=True)
     return finish(totals, precond, float(size * size))[None]
 

time: 118 us -> 115 us (0.975)
  waiting for transfers between devices: 42.3 us -> 38.6 us
  starting transfers between devices: 36 us -> 38.4 us
  local copies, waits for them, and re-layouts: 6.32 us -> 5.01 us
    all_to_all x1 -> x0, waiting for transfers between devices: 7.01 us -> none  [local(): lax.all_to_all(mixed, owner, split_axis=0, concat_axis=0, tiled=True)]
    ppermute x19 -> x22, starting transfers between devices: 24.8 us -> 29.9 us  [shift(): lax.ppermute(array, axis, [(i, (i + step) % size) for i in range(size)])]
    all_to_all x1 -> x0, starting transfers between devices: 3.98 us -> none  [local(): lax.all_to_all(mixed, owner, split_axis=0, concat_axis=0, tiled=True)]
    ppermute x19 -> x22, waiting for transfers between devices: 32.8 us -> 35 us  [shift(): lax.ppermute(array, axis, [(i, (i + step) % size) for i in range(size)])]
    unnamed x16, local copies, waits for them, and re-layouts: 6.32 us -> 5.01 us
    ppermute x4 -> x5, waiting for transfers between devices: 1.28 us -> 2.42 us  [swap(): return lax.ppermute(array, axis, [(i, i ^ mask) for i in range(size)])]
    pallas_call x14 -> x15, Pallas kernels: 13.5 us -> 12.8 us  [call(): pl.pallas_call(kernel, out_shape=out_shape, in_specs=in_specs, out_specs=...]
  transfers between devices with their start and end apart: 25 -> 28, of which waited for: 14 -> 15; matrix products, arithmetic and copies ran while one was open for 0% -> 0% of each run, Pallas kernels for 13% -> 13%
where the time goes in v4:
time: 115 us; the launch traced here: 113 us
  waiting for transfers between devices  38.6 us (34%)
  starting transfers between devices  38.4 us (33%)
  Pallas kernels  21.4 us (19%)
  blocking collectives  9.12 us (8%)
  local copies, waits for them, and re-layouts  5.01 us (4%)
    ppermute x22, waiting for transfers between devices, shift(): lax.ppermute(array, axis, [(i, (i + step) % size) for i in range(size)])  35 us
    ppermute x22, starting transfers between devices, shift(): lax.ppermute(array, axis, [(i, (i + step) % size) for i in range(size)])  29.9 us
    pallas_call x15, Pallas kernels, call(): pl.pallas_call(kernel, out_shape=out_shape, in_specs=in_specs, out_specs=...  12.8 us
    all_to_all x1, blocking collectives, local(): lax.all_to_all(totals, owner, split_axis=0, concat_axis=0, tiled=True)  9.12 us
    pallas_call x1, Pallas kernels, left_inverse_root(): pl.pallas_call(root_kernel, out_shape=(jax.ShapeDtypeStruct(matrix, jnp.b...  8.61 us
    all_to_all x1, starting transfers between devices, local(): lax.all_to_all(pieces, ('zh',) + owner, split_axis=0, concat_axis=0, tile...  7.08 us
    unnamed x16, local copies, waits for them, and re-layouts  5.01 us
    ppermute x5, waiting for transfers between devices, swap(): return lax.ppermute(array, axis, [(i, i ^ mask) for i in range(size)])  2.42 us
  transfers between devices with their start and end apart: 28, of which 15 were waited for; matrix products, arithmetic and copies ran while one was open for 0% of the time, Pallas kernels for 13%

profile of v4, /device:TPU:6, one launch (start us, length us, event | category | flops | bytes accessed | tf_op | source)
XLA Modules:
  0.0 113.4 jit_solution(12655968363549814077)
XLA Ops:
  0.1 3.5 %send.1 = (bf16[4,128,1024]{2,1,0:T(8,128)(2,1)S(1)}, bf16[4,128,1024]{2,1,0:T(8,128)(2,1)S(1)}, bf16[4,128,1024]{2,1,0:T(8,128)(2,1)S(1)}, bf16[4,128,1024]{2,1,0:T(8,128)(2,1)S(1)}) custom-call(s32[4]{0:T(128)S(1)} %pad_add_fusion.place_ref, bf16[2,4,4,128,1024]{4,3,2,1,0:T(8,128)(2,1)} %bitcast.7), custom_call_target="tpu_custom_call" | custom-call | bytes 8388608 | tf_op jit(solution)/shard_map/send/pallas_call | solution.py:46
  3.6 2.3 %collective-permute-start = (bf16[4,128,1024]{2,1,0:T(8,128)(2,1)S(1)}, bf16[4,128,1024]{2,1,0:T(8,128)(2,1)S(1)}, u32[]{:S(2)}, u32[]{:S(2)}) collective-permute-start(bf16[4,128,1024]{2,1,0:T(8,128)(2,1)S(1)} %get-tuple-element.54), channel_id=1, source_target_pairs={{0,8},{8,16},{16,24},{24,0},{1,9},{9,17},{17,25},{25,1},{2,10},{10... | collective-permute-start | bytes 3145736 | tf_op jit(solution)/shard_map/ppermute | solution.py:20
  5.9 1.4 %collective-permute-start.10 = (bf16[4,128,1024]{2,1,0:T(8,128)(2,1)S(1)}, bf16[4,128,1024]{2,1,0:T(8,128)(2,1)S(1)}, u32[]{:S(2)}, u32[]{:S(2)}) collective-permute-start(bf16[4,128,1024]{2,1,0:T(8,128)(2,1)S(1)} %get-tuple-element.70), channel_id=1, source_target_pairs={{0,32},{32,64},{64,96},{96,0},{1,33},{33,65},{65,97},{97,1},{2,34}... | collective-permute-start | bytes 3145736 | tf_op jit(solution)/shard_map/ppermute | solution.py:20
  7.3 1.9 %collective-permute-start.11 = (bf16[4,128,1024]{2,1,0:T(8,128)(2,1)S(1)}, bf16[4,128,1024]{2,1,0:T(8,128)(2,1)S(1)}, u32[]{:S(2)}, u32[]{:S(2)}) collective-permute-start(bf16[4,128,1024]{2,1,0:T(8,128)(2,1)S(1)} %get-tuple-element.71), channel_id=1, source_target_pairs={{0,96},{32,0},{64,32},{96,64},{1,97},{33,1},{65,33},{97,65},{2,98}... | collective-permute-start | bytes 3145736 | tf_op jit(solution)/shard_map/ppermute | solution.py:20
  9.8 1.2 %copy-done.3 = f32[1,1,256,1024]{3,2,1,0:T(8,128)S(1)} copy-done((f32[1,1,256,1024]{3,2,1,0:T(8,128)S(1)}, f32[1,1,256,1024]{3,2,1,0:T(8,128)}, u32[]{:S(2)}) %copy-start.3) | copy-done | bytes 1048600
  11.6 1.9 %collective-permute-start.2 = (bf16[256,640]{1,0:T(8,128)(2,1)S(1)}, bf16[256,640]{1,0:T(8,128)(2,1)S(1)}, u32[]{:S(2)}, u32[]{:S(2)}) collective-permute-start(bf16[256,640]{1,0:T(8,128)(2,1)S(1)} %trim.1.refs_0_), channel_id=1, source_target_pairs={{0,2},{2,4},{4,6},{6,0},{1,3},{3,5},{5,7},{7,1},{8,10},{10,12},{12... | collective-permute-start | bytes 983048 | tf_op jit(solution)/shard_map/ppermute | solution.py:20
  13.5 1.4 %keep.1 = (bf16[4,128,1024]{2,1,0:T(8,128)(2,1)S(1)}, bf16[4,128,1024]{2,1,0:T(8,128)(2,1)S(1)}, bf16[4,128,1024]{2,1,0:T(8,128)(2,1)S(1)}, bf16[4,128,1024]{2,1,0:T(8,128)(2,1)S(1)}) custom-call(s32[4]{0:T(128)S(1)} %pad_add_fusion.place_ref, bf16[2,4,4,128,1024]{4,3,2,1,0:T(8,128)(2,1)S(1)} %bitcast.8), custom_call_target="tpu_custom_call" | custom-call | bytes 8388608 | tf_op jit(solution)/shard_map/keep/pallas_call | solution.py:46
  14.9 7.8 %collective-permute-done.2.refs_2_ = bf16[256,640]{1,0:T(8,128)(2,1)S(1)} collective-permute-done((bf16[256,640]{1,0:T(8,128)(2,1)S(1)}, bf16[256,640]{1,0:T(8,128)(2,1)S(1)}, u32[]{:S(2)}, u32[]{:S(2)}) %collective-permute-start.2) | collective-permute-done | bytes 327712 | tf_op jit(solution)/shard_map/ppermute | solution.py:20
  22.8 9.5 %collective-permute-done.3.refs_4_ = bf16[256,640]{1,0:T(8,128)(2,1)S(1)} collective-permute-done((bf16[256,640]{1,0:T(8,128)(2,1)S(1)}, bf16[256,640]{1,0:T(8,128)(2,1)S(1)}, u32[]{:S(2)}, u32[]{:S(2)}) %collective-permute-start.3) | collective-permute-done | bytes 327712 | tf_op jit(solution)/shard_map/ppermute | solution.py:20
  32.5 1.2 %collective-permute-start.4 = (bf16[2,128,1024]{2,1,0:T(8,128)(2,1)S(1)}, bf16[2,128,1024]{2,1,0:T(8,128)(2,1)S(1)}, u32[]{:S(2)}, u32[]{:S(2)}) collective-permute-start(bf16[2,128,1024]{2,1,0:T(8,128)(2,1)S(1)} %get-tuple-element.61), channel_id=1, source_target_pairs={{0,8},{8,16},{16,24},{24,0},{1,9},{9,17},{17,25},{25,1},{2,10},{10... | collective-permute-start | bytes 1572872 | tf_op jit(solution)/shard_map/ppermute | solution.py:20
  35.2 3.0 %collective-permute-start.13 = (bf16[2,128,1024]{2,1,0:T(8,128)(2,1)S(1)}, bf16[2,128,1024]{2,1,0:T(8,128)(2,1)S(1)}, u32[]{:S(2)}, u32[]{:S(2)}) collective-permute-start(bf16[2,128,1024]{2,1,0:T(8,128)(2,1)S(1)} %get-tuple-element.74), channel_id=1, source_target_pairs={{0,96},{32,0},{64,32},{96,64},{1,97},{33,1},{65,33},{97,65},{2,98}... | collective-permute-start | bytes 1572872 | tf_op jit(solution)/shard_map/ppermute | solution.py:20
  38.2 5.4 %collective-permute-done.4.last_up_ref = bf16[2,128,1024]{2,1,0:T(8,128)(2,1)S(1)} collective-permute-done((bf16[2,128,1024]{2,1,0:T(8,128)(2,1)S(1)}, bf16[2,128,1024]{2,1,0:T(8,128)(2,1)S(1)}, u32[]{:S(2)}, u32[]{:S(2)}) %collective-permute-start.4) | collective-permute-done | bytes 524320 | tf_op jit(solution)/shard_map/ppermute | solution.py:20
  43.6 1.3 %collective-permute-done.5.last_down_ref = bf16[2,128,1024]{2,1,0:T(8,128)(2,1)S(1)} collective-permute-done((bf16[2,128,1024]{2,1,0:T(8,128)(2,1)S(1)}, bf16[2,128,1024]{2,1,0:T(8,128)(2,1)S(1)}, u32[]{:S(2)}, u32[]{:S(2)}) %collective-permute-start.5) | collective-permute-done | bytes 524320 | tf_op jit(solution)/shard_map/ppermute | solution.py:20
  45.4 1.7 %collective-permute-start.6 = (bf16[2,64,1024]{2,1,0:T(8,128)(2,1)S(1)}, bf16[2,64,1024]{2,1,0:T(8,128)(2,1)S(1)}, u32[]{:S(2)}, u32[]{:S(2)}) collective-permute-start(bf16[2,64,1024]{2,1,0:T(8,128)(2,1)S(1)} %get-tuple-element.64), channel_id=1, source_target_pairs={{0,32},{32,64},{64,96},{96,0},{1,33},{33,65},{65,97},{97,1},{2,34}... | collective-permute-start | bytes 786440 | tf_op jit(solution)/shard_map/ppermute | solution.py:20
  47.1 1.6 %collective-permute-start.7 = (bf16[2,64,1024]{2,1,0:T(8,128)(2,1)S(1)}, bf16[2,64,1024]{2,1,0:T(8,128)(2,1)S(1)}, u32[]{:S(2)}, u32[]{:S(2)}) collective-permute-start(bf16[2,64,1024]{2,1,0:T(8,128)(2,1)S(1)} %get-tuple-element.65), channel_id=1, source_target_pairs={{0,96},{32,0},{64,32},{96,64},{1,97},{33,1},{65,33},{97,65},{2,98}... | collective-permute-start | bytes 786440 | tf_op jit(solution)/shard_map/ppermute | solution.py:20
  49.2 2.2 %collective-permute-start.14 = (bf16[2,64,1024]{2,1,0:T(8,128)(2,1)S(1)}, bf16[2,64,1024]{2,1,0:T(8,128)(2,1)S(1)}, u32[]{:S(2)}, u32[]{:S(2)}) collective-permute-start(bf16[2,64,1024]{2,1,0:T(8,128)(2,1)S(1)} %get-tuple-element.76), channel_id=1, source_target_pairs={{0,8},{8,16},{16,24},{24,0},{1,9},{9,17},{17,25},{25,1},{2,10},{10... | collective-permute-start | bytes 786440 | tf_op jit(solution)/shard_map/ppermute | solution.py:20
  51.5 1.3 %collective-permute-start.21 = (bf16[256,640]{1,0:T(8,128)(2,1)S(1)}, bf16[256,640]{1,0:T(8,128)(2,1)S(1)}, u32[]{:S(2)}, u32[]{:S(2)}) collective-permute-start(bf16[256,640]{1,0:T(8,128)(2,1)S(1)} %collective-permute-done.3.refs_4_), channel_id=1, source_target_pairs={{0,2},{2,4},{4,6},{6,0},{1,3},{3,5},{5,7},{7,1},{8,10},{10,12},{12... | collective-permute-start | bytes 983048 | tf_op jit(solution)/shard_map/ppermute | solution.py:20
  53.0 1.3 %collective-permute-done.7.down_ref.refs_2_ = bf16[2,64,1024]{2,1,0:T(8,128)(2,1)S(1)} collective-permute-done((bf16[2,64,1024]{2,1,0:T(8,128)(2,1)S(1)}, bf16[2,64,1024]{2,1,0:T(8,128)(2,1)S(1)}, u32[]{:S(2)}, u32[]{:S(2)}) %collective-permute-start.7) | collective-permute-done | bytes 262176 | tf_op jit(solution)/shard_map/ppermute | solution.py:20
  55.5 2.2 %collective-permute-start.9 = (bf16[1,64,1024]{2,1,0:T(8,128)(2,1)S(1)}, bf16[1,64,1024]{2,1,0:T(8,128)(2,1)S(1)}, u32[]{:S(2)}, u32[]{:S(2)}) collective-permute-start(bf16[1,64,1024]{2,1,0:T(8,128)(2,1)S(1)} %get-tuple-element.68), channel_id=1, source_target_pairs={{0,96},{32,0},{64,32},{96,64},{1,97},{33,1},{65,33},{97,65},{2,98}... | collective-permute-start | bytes 393224 | tf_op jit(solution)/shard_map/ppermute | solution.py:20
  57.7 2.1 %collective-permute-done.15.down_ref.refs_7_ = bf16[2,64,1024]{2,1,0:T(8,128)(2,1)S(1)} collective-permute-done((bf16[2,64,1024]{2,1,0:T(8,128)(2,1)S(1)}, bf16[2,64,1024]{2,1,0:T(8,128)(2,1)S(1)}, u32[]{:S(2)}, u32[]{:S(2)}) %collective-permute-start.15) | collective-permute-done | bytes 262176 | tf_op jit(solution)/shard_map/ppermute | solution.py:20
  60.0 2.0 %collective-permute-start.17 = (bf16[1,64,1024]{2,1,0:T(8,128)(2,1)S(1)}, bf16[1,64,1024]{2,1,0:T(8,128)(2,1)S(1)}, u32[]{:S(2)}, u32[]{:S(2)}) collective-permute-start(bf16[1,64,1024]{2,1,0:T(8,128)(2,1)S(1)} %get-tuple-element.80), channel_id=1, source_target_pairs={{0,24},{8,0},{16,8},{24,16},{1,25},{9,1},{17,9},{25,17},{2,26},{10... | collective-permute-start | bytes 393224 | tf_op jit(solution)/shard_map/ppermute | solution.py:20
  62.0 2.9 %collective-permute-done.16.refs_8_ = bf16[1,64,1024]{2,1,0:T(8,128)(2,1)S(1)} collective-permute-done((bf16[1,64,1024]{2,1,0:T(8,128)(2,1)S(1)}, bf16[1,64,1024]{2,1,0:T(8,128)(2,1)S(1)}, u32[]{:S(2)}, u32[]{:S(2)}) %collective-permute-start.16) | collective-permute-done | bytes 131104 | tf_op jit(solution)/shard_map/ppermute | solution.py:20
  65.0 1.3 %collective-permute-done.17.refs_9_ = bf16[1,64,1024]{2,1,0:T(8,128)(2,1)S(1)} collective-permute-done((bf16[1,64,1024]{2,1,0:T(8,128)(2,1)S(1)}, bf16[1,64,1024]{2,1,0:T(8,128)(2,1)S(1)}, u32[]{:S(2)}, u32[]{:S(2)}) %collective-permute-start.17) | collective-permute-done | bytes 131104 | tf_op jit(solution)/shard_map/ppermute | solution.py:20
  67.2 7.1 %all-to-all-start = ((bf16[16,128,128]{2,1,0:T(8,128)(2,1)}), bf16[16,128,128]{2,1,0:T(8,128)(2,1)S(1)}, u32[]{:S(2)}, u32[]{:S(2)}) async-start(bf16[16,128,128]{2,1,0:T(8,128)(2,1)} %pieces.1), calls=%async_computation | async-start | bytes 1048576 | tf_op jit(solution)/shard_map/all_to_all | solution.py:544
  79.4 8.6 %left_root.1 = (bf16[1024,1024]{1,0:T(8,128)(2,1)S(1)}, bf16[4,256,640]{2,1,0:T(8,128)(2,1)S(1)}) custom-call(s32[4]{0:T(128)S(1)} %pad_add_fusion.place_ref, s32[1]{0:T(128)S(6)} %copy.4.table_ref, bf16[256,640]{1,0:T(8,128)(2,1)S(1)} %trim.1.refs_0_, bf16[256,640]{1,0:T(8,128)(2,1)S(1)} %collective-permute-done.18.refs_1_, ...), custom_call_target="tpu_custom_call" | custom-call | flops 6442450944 | bytes 4194304 | tf_op jit(solution)/shard_map/left_root/pallas_call | solution.py:307
  89.1 1.2 %all-to-all-done.pieces_ref = bf16[16,128,128]{2,1,0:T(8,128)(2,1)S(1)} async-done(((bf16[16,128,128]{2,1,0:T(8,128)(2,1)}), bf16[16,128,128]{2,1,0:T(8,128)(2,1)S(1)}, u32[]{:S(2)}, u32[]{:S(2)}) %all-to-all-start) | async-done | bytes 524320 | tf_op jit(solution)/shard_map/all_to_all | solution.py:544
  91.9 2.6 %collective-permute-start.24 = (bf16[2,128,128]{2,1,0:T(8,128)(2,1)S(1)}, bf16[2,128,128]{2,1,0:T(8,128)(2,1)S(1)}, u32[]{:S(2)}, u32[]{:S(2)}) collective-permute-start(bf16[2,128,128]{2,1,0:T(8,128)(2,1)S(1)} %get-tuple-element.97), channel_id=1, source_target_pairs={{0,4},{2,6},{4,0},{6,2},{1,5},{3,7},{5,1},{7,3},{8,12},{10,14},{12... | collective-permute-start | bytes 196616 | tf_op jit(solution)/shard_map/ppermute | solution.py:20
  94.5 1.4 %collective-permute-start.25 = (bf16[2,128,128]{2,1,0:T(8,128)(2,1)S(1)}, bf16[2,128,128]{2,1,0:T(8,128)(2,1)S(1)}, u32[]{:S(2)}, u32[]{:S(2)}) collective-permute-start(bf16[2,128,128]{2,1,0:T(8,128)(2,1)S(1)} %get-tuple-element.98), channel_id=1, source_target_pairs={{0,6},{2,0},{4,2},{6,4},{1,7},{3,1},{5,3},{7,5},{8,14},{10,8},{12,... | collective-permute-start | bytes 196616 | tf_op jit(solution)/shard_map/ppermute | solution.py:20
  95.9 1.4 %right_base.1 = (bf16[1024,1024]{1,0:T(8,128)(2,1)S(1)}, f32[8,1024]{1,0:T(8,128)S(1)}) custom-call(bf16[4,256,640]{2,1,0:T(8,128)(2,1)S(1)} %copy-done.2), custom_call_target="tpu_custom_call" | custom-call | flops 4194304 | bytes 4194304 | tf_op jit(solution)/shard_map/right_base/pallas_call | solution.py:46
  97.4 3.0 %collective-permute-done.24.refs_2_ = bf16[2,128,128]{2,1,0:T(8,128)(2,1)S(1)} collective-permute-done((bf16[2,128,128]{2,1,0:T(8,128)(2,1)S(1)}, bf16[2,128,128]{2,1,0:T(8,128)(2,1)S(1)}, u32[]{:S(2)}, u32[]{:S(2)}) %collective-permute-start.24) | collective-permute-done | bytes 65568 | tf_op jit(solution)/shard_map/ppermute | solution.py:20
  101.8 1.4 %condition.1 = (f32[128,1024]{1,0:T(8,128)S(1)}, f32[8,8,128]{2,1,0:T(8,128)S(1)}) custom-call(s32[1]{0:T(128)} %bitcast.zl_ref, s32[1]{0:T(128)} %bitcast.1.c_ref, bf16[2,128,128]{2,1,0:T(8,128)(2,1)S(1)} %get-tuple-element.95.refs_0_, bf16[2,128,128]{2,1,0:T(8,128)(2,1)S(1)} %collective-permute-done.23.refs_1_, ...), custom_call_target="tpu_custom_call" | custom-call | flops 1073741824 | bytes 2097152 | tf_op jit(solution)/shard_map/condition/pallas_call | solution.py:46
  103.2 9.1 %all_to_all.10.totals_ref = f32[8,8,128]{2,1,0:T(8,128)S(1)} all-to-all(f32[8,8,128]{2,1,0:T(8,128)S(1)} %get-tuple-element.101), channel_id=1, replica_groups=mesh['zh'=2,'y'=4,'x'=4,'zl'=4,'c'=2] {'zl','c'}, dimensions={0} | all-to-all | bytes 65536 | tf_op jit(solution)/shard_map/all_to_all | solution.py:550
  (58 shorter events, 16.2 us)
Async XLA Ops:
  0.1 13.4 %copy-start = (bf16[1,32,128,1024]{3,2,1,0:T(8,128)(2,1)S(1)}, bf16[1,32,128,1024]{3,2,1,0:T(8,128)(2,1)}, u32[]{:S(2)}) copy-start(bf16[1,32,128,1024]{3,2,1,0:T(8,128)(2,1)} %param.3) | copy-start | bytes 25165828
  3.6 28.7 %collective-permute-start = (bf16[4,128,1024]{2,1,0:T(8,128)(2,1)S(1)}, bf16[4,128,1024]{2,1,0:T(8,128)(2,1)S(1)}, u32[]{:S(2)}, u32[]{:S(2)}) collective-permute-start(bf16[4,128,1024]{2,1,0:T(8,128)(2,1)S(1)} %get-tuple-element.54), channel_id=1, source_target_pairs={{0,8},{8,16},{16,24},{24,0},{1,9},{9,17},{17,25},{25,1},{2,10},{10... | collective-permute-start | bytes 3145736 | tf_op jit(solution)/shard_map/ppermute | solution.py:20
  5.9 26.4 %collective-permute-start.1 = (bf16[4,128,1024]{2,1,0:T(8,128)(2,1)S(1)}, bf16[4,128,1024]{2,1,0:T(8,128)(2,1)S(1)}, u32[]{:S(2)}, u32[]{:S(2)}) collective-permute-start(bf16[4,128,1024]{2,1,0:T(8,128)(2,1)S(1)} %get-tuple-element.57), channel_id=1, source_target_pairs={{0,24},{8,0},{16,8},{24,16},{1,25},{9,1},{17,9},{25,17},{2,26},{10... | collective-permute-start | bytes 3145736 | tf_op jit(solution)/shard_map/ppermute | solution.py:20
  5.9 28.7 %collective-permute-start.10 = (bf16[4,128,1024]{2,1,0:T(8,128)(2,1)S(1)}, bf16[4,128,1024]{2,1,0:T(8,128)(2,1)S(1)}, u32[]{:S(2)}, u32[]{:S(2)}) collective-permute-start(bf16[4,128,1024]{2,1,0:T(8,128)(2,1)S(1)} %get-tuple-element.70), channel_id=1, source_target_pairs={{0,32},{32,64},{64,96},{96,0},{1,33},{33,65},{65,97},{97,1},{2,34}... | collective-permute-start | bytes 3145736 | tf_op jit(solution)/shard_map/ppermute | solution.py:20
  7.3 27.4 %collective-permute-start.11 = (bf16[4,128,1024]{2,1,0:T(8,128)(2,1)S(1)}, bf16[4,128,1024]{2,1,0:T(8,128)(2,1)S(1)}, u32[]{:S(2)}, u32[]{:S(2)}) collective-permute-start(bf16[4,128,1024]{2,1,0:T(8,128)(2,1)S(1)} %get-tuple-element.71), channel_id=1, source_target_pairs={{0,96},{32,0},{64,32},{96,64},{1,97},{33,1},{65,33},{97,65},{2,98}... | collective-permute-start | bytes 3145736 | tf_op jit(solution)/shard_map/ppermute | solution.py:20
  9.8 1.2 %copy-start.3 = (f32[1,1,256,1024]{3,2,1,0:T(8,128)S(1)}, f32[1,1,256,1024]{3,2,1,0:T(8,128)}, u32[]{:S(2)}) copy-start(f32[1,1,256,1024]{3,2,1,0:T(8,128)} %param.4) | copy-start | bytes 3145732
  11.6 11.2 %collective-permute-start.2 = (bf16[256,640]{1,0:T(8,128)(2,1)S(1)}, bf16[256,640]{1,0:T(8,128)(2,1)S(1)}, u32[]{:S(2)}, u32[]{:S(2)}) collective-permute-start(bf16[256,640]{1,0:T(8,128)(2,1)S(1)} %trim.1.refs_0_), channel_id=1, source_target_pairs={{0,2},{2,4},{4,6},{6,0},{1,3},{3,5},{5,7},{7,1},{8,10},{10,12},{12... | collective-permute-start | bytes 983048 | tf_op jit(solution)/shard_map/ppermute | solution.py:20
  22.8 9.5 %collective-permute-start.3 = (bf16[256,640]{1,0:T(8,128)(2,1)S(1)}, bf16[256,640]{1,0:T(8,128)(2,1)S(1)}, u32[]{:S(2)}, u32[]{:S(2)}) collective-permute-start(bf16[256,640]{1,0:T(8,128)(2,1)S(1)} %collective-permute-done.2.refs_2_), channel_id=1, source_target_pairs={{0,2},{2,4},{4,6},{6,0},{1,3},{3,5},{5,7},{7,1},{8,10},{10,12},{12... | collective-permute-start | bytes 983048 | tf_op jit(solution)/shard_map/ppermute | solution.py:20
  32.3 42.7 %copy-start.4 = (bf16[256,640]{1,0:T(8,128)(2,1)}, bf16[256,640]{1,0:T(8,128)(2,1)S(1)}, u32[]{:S(2)}) copy-start(bf16[256,640]{1,0:T(8,128)(2,1)S(1)} %collective-permute-done.3.refs_4_) | copy-start | bytes 983044
  32.5 11.1 %collective-permute-start.4 = (bf16[2,128,1024]{2,1,0:T(8,128)(2,1)S(1)}, bf16[2,128,1024]{2,1,0:T(8,128)(2,1)S(1)}, u32[]{:S(2)}, u32[]{:S(2)}) collective-permute-start(bf16[2,128,1024]{2,1,0:T(8,128)(2,1)S(1)} %get-tuple-element.61), channel_id=1, source_target_pairs={{0,8},{8,16},{16,24},{24,0},{1,9},{9,17},{17,25},{25,1},{2,10},{10... | collective-permute-start | bytes 1572872 | tf_op jit(solution)/shard_map/ppermute | solution.py:20
  33.7 11.2 %collective-permute-start.5 = (bf16[2,128,1024]{2,1,0:T(8,128)(2,1)S(1)}, bf16[2,128,1024]{2,1,0:T(8,128)(2,1)S(1)}, u32[]{:S(2)}, u32[]{:S(2)}) collective-permute-start(bf16[2,128,1024]{2,1,0:T(8,128)(2,1)S(1)} %get-tuple-element.62), channel_id=1, source_target_pairs={{0,24},{8,0},{16,8},{24,16},{1,25},{9,1},{17,9},{25,17},{2,26},{10... | collective-permute-start | bytes 1572872 | tf_op jit(solution)/shard_map/ppermute | solution.py:20
  34.9 13.9 %collective-permute-start.12 = (bf16[2,128,1024]{2,1,0:T(8,128)(2,1)S(1)}, bf16[2,128,1024]{2,1,0:T(8,128)(2,1)S(1)}, u32[]{:S(2)}, u32[]{:S(2)}) collective-permute-start(bf16[2,128,1024]{2,1,0:T(8,128)(2,1)S(1)} %get-tuple-element.73), channel_id=1, source_target_pairs={{0,32},{32,64},{64,96},{96,0},{1,33},{33,65},{65,97},{97,1},{2,34}... | collective-permute-start | bytes 1572872 | tf_op jit(solution)/shard_map/ppermute | solution.py:20
  35.2 13.6 %collective-permute-start.13 = (bf16[2,128,1024]{2,1,0:T(8,128)(2,1)S(1)}, bf16[2,128,1024]{2,1,0:T(8,128)(2,1)S(1)}, u32[]{:S(2)}, u32[]{:S(2)}) collective-permute-start(bf16[2,128,1024]{2,1,0:T(8,128)(2,1)S(1)} %get-tuple-element.74), channel_id=1, source_target_pairs={{0,96},{32,0},{64,32},{96,64},{1,97},{33,1},{65,33},{97,65},{2,98}... | collective-permute-start | bytes 1572872 | tf_op jit(solution)/shard_map/ppermute | solution.py:20
  45.4 7.7 %collective-permute-start.6 = (bf16[2,64,1024]{2,1,0:T(8,128)(2,1)S(1)}, bf16[2,64,1024]{2,1,0:T(8,128)(2,1)S(1)}, u32[]{:S(2)}, u32[]{:S(2)}) collective-permute-start(bf16[2,64,1024]{2,1,0:T(8,128)(2,1)S(1)} %get-tuple-element.64), channel_id=1, source_target_pairs={{0,32},{32,64},{64,96},{96,0},{1,33},{33,65},{65,97},{97,1},{2,34}... | collective-permute-start | bytes 786440 | tf_op jit(solution)/shard_map/ppermute | solution.py:20
  47.1 7.2 %collective-permute-start.7 = (bf16[2,64,1024]{2,1,0:T(8,128)(2,1)S(1)}, bf16[2,64,1024]{2,1,0:T(8,128)(2,1)S(1)}, u32[]{:S(2)}, u32[]{:S(2)}) collective-permute-start(bf16[2,64,1024]{2,1,0:T(8,128)(2,1)S(1)} %get-tuple-element.65), channel_id=1, source_target_pairs={{0,96},{32,0},{64,32},{96,64},{1,97},{33,1},{65,33},{97,65},{2,98}... | collective-permute-start | bytes 786440 | tf_op jit(solution)/shard_map/ppermute | solution.py:20
  49.2 8.5 %collective-permute-start.14 = (bf16[2,64,1024]{2,1,0:T(8,128)(2,1)S(1)}, bf16[2,64,1024]{2,1,0:T(8,128)(2,1)S(1)}, u32[]{:S(2)}, u32[]{:S(2)}) collective-permute-start(bf16[2,64,1024]{2,1,0:T(8,128)(2,1)S(1)} %get-tuple-element.76), channel_id=1, source_target_pairs={{0,8},{8,16},{16,24},{24,0},{1,9},{9,17},{17,25},{25,1},{2,10},{10... | collective-permute-start | bytes 786440 | tf_op jit(solution)/shard_map/ppermute | solution.py:20
  51.5 8.4 %collective-permute-start.15 = (bf16[2,64,1024]{2,1,0:T(8,128)(2,1)S(1)}, bf16[2,64,1024]{2,1,0:T(8,128)(2,1)S(1)}, u32[]{:S(2)}, u32[]{:S(2)}) collective-permute-start(bf16[2,64,1024]{2,1,0:T(8,128)(2,1)S(1)} %get-tuple-element.77), channel_id=1, source_target_pairs={{0,24},{8,0},{16,8},{24,16},{1,25},{9,1},{17,9},{25,17},{2,26},{10... | collective-permute-start | bytes 786440 | tf_op jit(solution)/shard_map/ppermute | solution.py:20
  51.5 23.7 %collective-permute-start.21 = (bf16[256,640]{1,0:T(8,128)(2,1)S(1)}, bf16[256,640]{1,0:T(8,128)(2,1)S(1)}, u32[]{:S(2)}, u32[]{:S(2)}) collective-permute-start(bf16[256,640]{1,0:T(8,128)(2,1)S(1)} %collective-permute-done.3.refs_4_), channel_id=1, source_target_pairs={{0,2},{2,4},{4,6},{6,0},{1,3},{3,5},{5,7},{7,1},{8,10},{10,12},{12... | collective-permute-start | bytes 983048 | tf_op jit(solution)/shard_map/ppermute | solution.py:20
  54.4 7.6 %collective-permute-start.8 = (bf16[1,64,1024]{2,1,0:T(8,128)(2,1)S(1)}, bf16[1,64,1024]{2,1,0:T(8,128)(2,1)S(1)}, u32[]{:S(2)}, u32[]{:S(2)}) collective-permute-start(bf16[1,64,1024]{2,1,0:T(8,128)(2,1)S(1)} %get-tuple-element.67), channel_id=1, source_target_pairs={{0,32},{32,64},{64,96},{96,0},{1,33},{33,65},{65,97},{97,1},{2,34}... | collective-permute-start | bytes 393224 | tf_op jit(solution)/shard_map/ppermute | solution.py:20
  55.5 6.5 %collective-permute-start.9 = (bf16[1,64,1024]{2,1,0:T(8,128)(2,1)S(1)}, bf16[1,64,1024]{2,1,0:T(8,128)(2,1)S(1)}, u32[]{:S(2)}, u32[]{:S(2)}) collective-permute-start(bf16[1,64,1024]{2,1,0:T(8,128)(2,1)S(1)} %get-tuple-element.68), channel_id=1, source_target_pairs={{0,96},{32,0},{64,32},{96,64},{1,97},{33,1},{65,33},{97,65},{2,98}... | collective-permute-start | bytes 393224 | tf_op jit(solution)/shard_map/ppermute | solution.py:20
  59.9 5.0 %collective-permute-start.16 = (bf16[1,64,1024]{2,1,0:T(8,128)(2,1)S(1)}, bf16[1,64,1024]{2,1,0:T(8,128)(2,1)S(1)}, u32[]{:S(2)}, u32[]{:S(2)}) collective-permute-start(bf16[1,64,1024]{2,1,0:T(8,128)(2,1)S(1)} %get-tuple-element.79), channel_id=1, source_target_pairs={{0,8},{8,16},{16,24},{24,0},{1,9},{9,17},{17,25},{25,1},{2,10},{10... | collective-permute-start | bytes 393224 | tf_op jit(solution)/shard_map/ppermute | solution.py:20
  60.0 6.3 %collective-permute-start.17 = (bf16[1,64,1024]{2,1,0:T(8,128)(2,1)S(1)}, bf16[1,64,1024]{2,1,0:T(8,128)(2,1)S(1)}, u32[]{:S(2)}, u32[]{:S(2)}) collective-permute-start(bf16[1,64,1024]{2,1,0:T(8,128)(2,1)S(1)} %get-tuple-element.80), channel_id=1, source_target_pairs={{0,24},{8,0},{16,8},{24,16},{1,25},{9,1},{17,9},{25,17},{2,26},{10... | collective-permute-start | bytes 393224 | tf_op jit(solution)/shard_map/ppermute | solution.py:20
  67.2 23.1 %all-to-all-start = ((bf16[16,128,128]{2,1,0:T(8,128)(2,1)}), bf16[16,128,128]{2,1,0:T(8,128)(2,1)S(1)}, u32[]{:S(2)}, u32[]{:S(2)}) async-start(bf16[16,128,128]{2,1,0:T(8,128)(2,1)} %pieces.1), calls=%async_computation | async-start | bytes 1048576 | tf_op jit(solution)/shard_map/all_to_all | solution.py:544
  74.3 1.9 %collective-permute-start.18 = (bf16[256,640]{1,0:T(8,128)(2,1)S(1)}, bf16[256,640]{1,0:T(8,128)(2,1)S(1)}, u32[]{:S(2)}, u32[]{:S(2)}) collective-permute-start(bf16[256,640]{1,0:T(8,128)(2,1)S(1)} %trim.1.refs_0_), channel_id=1, source_target_pairs={{0,1},{1,0},{2,3},{3,2},{4,5},{5,4},{6,7},{7,6},{8,9},{9,8},{10,11... | collective-permute-start | bytes 983048 | tf_op jit(solution)/shard_map/ppermute | solution.py:25
  74.7 1.8 %collective-permute-start.19 = (bf16[256,640]{1,0:T(8,128)(2,1)S(1)}, bf16[256,640]{1,0:T(8,128)(2,1)S(1)}, u32[]{:S(2)}, u32[]{:S(2)}) collective-permute-start(bf16[256,640]{1,0:T(8,128)(2,1)S(1)} %collective-permute-done.2.refs_2_), channel_id=1, source_target_pairs={{0,1},{1,0},{2,3},{3,2},{4,5},{5,4},{6,7},{7,6},{8,9},{9,8},{10,11... | collective-permute-start | bytes 983048 | tf_op jit(solution)/shard_map/ppermute | solution.py:25
  74.9 2.1 %collective-permute-start.20 = (bf16[256,640]{1,0:T(8,128)(2,1)S(1)}, bf16[256,640]{1,0:T(8,128)(2,1)S(1)}, u32[]{:S(2)}, u32[]{:S(2)}) collective-permute-start(bf16[256,640]{1,0:T(8,128)(2,1)S(1)} %collective-permute-done.3.refs_4_), channel_id=1, source_target_pairs={{0,1},{1,0},{2,3},{3,2},{4,5},{5,4},{6,7},{7,6},{8,9},{9,8},{10,11... | collective-permute-start | bytes 983048 | tf_op jit(solution)/shard_map/ppermute | solution.py:25
  75.2 2.2 %collective-permute-start.22 = (bf16[256,640]{1,0:T(8,128)(2,1)S(1)}, bf16[256,640]{1,0:T(8,128)(2,1)S(1)}, u32[]{:S(2)}, u32[]{:S(2)}) collective-permute-start(bf16[256,640]{1,0:T(8,128)(2,1)S(1)} %collective-permute-done.21.refs_6_), channel_id=1, source_target_pairs={{0,1},{1,0},{2,3},{3,2},{4,5},{5,4},{6,7},{7,6},{8,9},{9,8},{10,11... | collective-permute-start | bytes 983048 | tf_op jit(solution)/shard_map/ppermute | solution.py:25
  90.3 5.6 %copy-start.2 = (bf16[4,256,640]{2,1,0:T(8,128)(2,1)S(1)}, bf16[4,256,640]{2,1,0:T(8,128)(2,1)}, u32[]{:S(2)}) copy-start(bf16[4,256,640]{2,1,0:T(8,128)(2,1)} %copy-done.1) | copy-start | bytes 3932164
  91.2 6.2 %collective-permute-start.23 = (bf16[2,128,128]{2,1,0:T(8,128)(2,1)S(1)}, bf16[2,128,128]{2,1,0:T(8,128)(2,1)S(1)}, u32[]{:S(2)}, u32[]{:S(2)}) collective-permute-start(bf16[2,128,128]{2,1,0:T(8,128)(2,1)S(1)} %get-tuple-element.96), channel_id=1, source_target_pairs={{0,2},{2,4},{4,6},{6,0},{1,3},{3,5},{5,7},{7,1},{8,10},{10,12},{12... | collective-permute-start | bytes 196616 | tf_op jit(solution)/shard_map/ppermute | solution.py:20
  91.9 8.5 %collective-permute-start.24 = (bf16[2,128,128]{2,1,0:T(8,128)(2,1)S(1)}, bf16[2,128,128]{2,1,0:T(8,128)(2,1)S(1)}, u32[]{:S(2)}, u32[]{:S(2)}) collective-permute-start(bf16[2,128,128]{2,1,0:T(8,128)(2,1)S(1)} %get-tuple-element.97), channel_id=1, source_target_pairs={{0,4},{2,6},{4,0},{6,2},{1,5},{3,7},{5,1},{7,3},{8,12},{10,14},{12... | collective-permute-start | bytes 196616 | tf_op jit(solution)/shard_map/ppermute | solution.py:20
  94.5 5.9 %collective-permute-start.25 = (bf16[2,128,128]{2,1,0:T(8,128)(2,1)S(1)}, bf16[2,128,128]{2,1,0:T(8,128)(2,1)S(1)}, u32[]{:S(2)}, u32[]{:S(2)}) collective-permute-start(bf16[2,128,128]{2,1,0:T(8,128)(2,1)S(1)} %get-tuple-element.98), channel_id=1, source_target_pairs={{0,6},{2,0},{4,2},{6,4},{1,7},{3,1},{5,3},{7,5},{8,14},{10,8},{12,... | collective-permute-start | bytes 196616 | tf_op jit(solution)/shard_map/ppermute | solution.py:20
  100.4 1.4 %collective-permute-start.26 = (bf16[4,128,128]{2,1,0:T(8,128)(2,1)S(1)}, bf16[4,128,128]{2,1,0:T(8,128)(2,1)S(1)}, u32[]{:S(2)}, u32[]{:S(2)}) collective-permute-start(bf16[4,128,128]{2,1,0:T(8,128)(2,1)S(1)} %split.1), channel_id=1, source_target_pairs={{0,1},{1,0},{2,3},{3,2},{4,5},{5,4},{6,7},{7,6},{8,9},{9,8},{10,11... | collective-permute-start | bytes 393224 | tf_op jit(solution)/shard_map/ppermute | solution.py:25
  (4 other events, 3.8 us)

commit v5 on v4

--- a/solution.py
+++ b/solution.py
@@ -531,6 +531,8 @@
 
     x_last = ring_first(*x_last, "x")
     y_last = ring_first(*y_last, "y")
+    for each in (near[3], *far[:3]):
+        (y_own,) = after(each, y_own)
 
     lower_up, lower_down, lower_mid, lower_own = turn(y[None], x_own, *x_ends, *x_last)
     lower_ends = ring_first(lower_up, lower_down, "y")

time: 115 us -> 118 us (1.026)
  local copies, waits for them, and re-layouts: 5.01 us -> 7.22 us
  waiting for transfers between devices: 38.6 us -> 40.2 us
    unnamed x16 -> x28, local copies, waits for them, and re-layouts: 5.01 us -> 7.22 us
    ppermute x5, waiting for transfers between devices: 2.42 us -> 4.22 us  [swap(): return lax.ppermute(array, axis, [(i, i ^ mask) for i in range(size)])]
    all_to_all x1, waiting for transfers between devices: 1.22 us -> 0.01 us  [local(): lax.all_to_all(pieces, ('zh',) + owner, split_axis=0, concat_axis=0, tile...]
  transfers between devices with their start and end apart: 28 -> 28, of which waited for: 15 -> 14; matrix products, arithmetic and copies ran while one was open for 0% -> 0% of each run, Pallas kernels for 13% -> 12%
where the time goes in v5:
time: 118 us
  waiting for transfers between devices  40.2 us (34%)
  starting transfers between devices  38.2 us (32%)
  Pallas kernels  21.4 us (18%)
  blocking collectives  9.5 us (8%)
  local copies, waits for them, and re-layouts  7.22 us (6%)
    ppermute x22, waiting for transfers between devices, shift(): lax.ppermute(array, axis, [(i, (i + step) % size) for i in range(size)])  36 us
    ppermute x22, starting transfers between devices, shift(): lax.ppermute(array, axis, [(i, (i + step) % size) for i in range(size)])  29.3 us
    pallas_call x15, Pallas kernels, call(): pl.pallas_call(kernel, out_shape=out_shape, in_specs=in_specs, out_specs=...  12.8 us
    all_to_all x1, blocking collectives, local(): lax.all_to_all(totals, owner, split_axis=0, concat_axis=0, tiled=True)  9.5 us
    pallas_call x1, Pallas kernels, left_inverse_root(): pl.pallas_call(root_kernel, out_shape=(jax.ShapeDtypeStruct(matrix, jnp.b...  8.61 us
    all_to_all x1, starting transfers between devices, local(): lax.all_to_all(pieces, ('zh',) + owner, split_axis=0, concat_axis=0, tile...  7.82 us
    unnamed x28, local copies, waits for them, and re-layouts  7.22 us
    ppermute x5, waiting for transfers between devices, swap(): return lax.ppermute(array, axis, [(i, i ^ mask) for i in range(size)])  4.22 us
  transfers between devices with their start and end apart: 28, of which 14 were waited for; matrix products, arithmetic and copies ran while one was open for 0% of the time, Pallas kernels for 12%

profile of v5, /device:TPU:6, one launch (start us, length us, event | category | flops | bytes accessed | tf_op | source)
XLA Modules:
  0.0 117.6 jit_solution(13860509554389412562)
XLA Ops:
  0.1 3.5 %send.1 = (bf16[4,128,1024]{2,1,0:T(8,128)(2,1)S(1)}, bf16[4,128,1024]{2,1,0:T(8,128)(2,1)S(1)}, bf16[4,128,1024]{2,1,0:T(8,128)(2,1)S(1)}, bf16[4,128,1024]{2,1,0:T(8,128)(2,1)S(1)}) custom-call(s32[4]{0:T(128)S(1)} %pad_add_fusion.place_ref, bf16[2,4,4,128,1024]{4,3,2,1,0:T(8,128)(2,1)} %bitcast.7), custom_call_target="tpu_custom_call" | custom-call | bytes 8388608 | tf_op jit(solution)/shard_map/send/pallas_call | solution.py:46
  3.6 2.3 %collective-permute-start = (bf16[4,128,1024]{2,1,0:T(8,128)(2,1)S(1)}, bf16[4,128,1024]{2,1,0:T(8,128)(2,1)S(1)}, u32[]{:S(2)}, u32[]{:S(2)}) collective-permute-start(bf16[4,128,1024]{2,1,0:T(8,128)(2,1)S(1)} %get-tuple-element.58), channel_id=1, source_target_pairs={{0,8},{8,16},{16,24},{24,0},{1,9},{9,17},{17,25},{25,1},{2,10},{10... | collective-permute-start | bytes 3145736 | tf_op jit(solution)/shard_map/ppermute | solution.py:20
  5.9 1.4 %collective-permute-start.14 = (bf16[4,128,1024]{2,1,0:T(8,128)(2,1)S(1)}, bf16[4,128,1024]{2,1,0:T(8,128)(2,1)S(1)}, u32[]{:S(2)}, u32[]{:S(2)}) collective-permute-start(bf16[4,128,1024]{2,1,0:T(8,128)(2,1)S(1)} %get-tuple-element.78), channel_id=1, source_target_pairs={{0,32},{32,64},{64,96},{96,0},{1,33},{33,65},{65,97},{97,1},{2,34}... | collective-permute-start | bytes 3145736 | tf_op jit(solution)/shard_map/ppermute | solution.py:20
  7.3 1.9 %collective-permute-start.15 = (bf16[4,128,1024]{2,1,0:T(8,128)(2,1)S(1)}, bf16[4,128,1024]{2,1,0:T(8,128)(2,1)S(1)}, u32[]{:S(2)}, u32[]{:S(2)}) collective-permute-start(bf16[4,128,1024]{2,1,0:T(8,128)(2,1)S(1)} %get-tuple-element.79), channel_id=1, source_target_pairs={{0,96},{32,0},{64,32},{96,64},{1,97},{33,1},{65,33},{97,65},{2,98}... | collective-permute-start | bytes 3145736 | tf_op jit(solution)/shard_map/ppermute | solution.py:20
  9.8 1.2 %copy-done.3 = f32[1,1,256,1024]{3,2,1,0:T(8,128)S(1)} copy-done((f32[1,1,256,1024]{3,2,1,0:T(8,128)S(1)}, f32[1,1,256,1024]{3,2,1,0:T(8,128)}, u32[]{:S(2)}) %copy-start.3) | copy-done | bytes 1048600
  11.7 1.7 %collective-permute-start.2 = (bf16[256,640]{1,0:T(8,128)(2,1)S(1)}, bf16[256,640]{1,0:T(8,128)(2,1)S(1)}, u32[]{:S(2)}, u32[]{:S(2)}) collective-permute-start(bf16[256,640]{1,0:T(8,128)(2,1)S(1)} %trim.1.refs_0_), channel_id=1, source_target_pairs={{0,2},{2,4},{4,6},{6,0},{1,3},{3,5},{5,7},{7,1},{8,10},{10,12},{12... | collective-permute-start | bytes 983048 | tf_op jit(solution)/shard_map/ppermute | solution.py:20
  13.4 1.4 %keep.1 = (bf16[4,128,1024]{2,1,0:T(8,128)(2,1)S(1)}, bf16[4,128,1024]{2,1,0:T(8,128)(2,1)S(1)}, bf16[4,128,1024]{2,1,0:T(8,128)(2,1)S(1)}, bf16[4,128,1024]{2,1,0:T(8,128)(2,1)S(1)}) custom-call(s32[4]{0:T(128)S(1)} %pad_add_fusion.place_ref, bf16[2,4,4,128,1024]{4,3,2,1,0:T(8,128)(2,1)S(1)} %bitcast.8), custom_call_target="tpu_custom_call" | custom-call | bytes 8388608 | tf_op jit(solution)/shard_map/keep/pallas_call | solution.py:46
  14.9 8.0 %collective-permute-done.2.refs_2_ = bf16[256,640]{1,0:T(8,128)(2,1)S(1)} collective-permute-done((bf16[256,640]{1,0:T(8,128)(2,1)S(1)}, bf16[256,640]{1,0:T(8,128)(2,1)S(1)}, u32[]{:S(2)}, u32[]{:S(2)}) %collective-permute-start.2) | collective-permute-done | bytes 327712 | tf_op jit(solution)/shard_map/ppermute | solution.py:20
  22.8 9.6 %collective-permute-done.3.refs_4_ = bf16[256,640]{1,0:T(8,128)(2,1)S(1)} collective-permute-done((bf16[256,640]{1,0:T(8,128)(2,1)S(1)}, bf16[256,640]{1,0:T(8,128)(2,1)S(1)}, u32[]{:S(2)}, u32[]{:S(2)}) %collective-permute-start.3) | collective-permute-done | bytes 327712 | tf_op jit(solution)/shard_map/ppermute | solution.py:20
  36.2 2.7 %collective-permute-start.17 = (bf16[2,128,1024]{2,1,0:T(8,128)(2,1)S(1)}, bf16[2,128,1024]{2,1,0:T(8,128)(2,1)S(1)}, u32[]{:S(2)}, u32[]{:S(2)}) collective-permute-start(bf16[2,128,1024]{2,1,0:T(8,128)(2,1)S(1)} %get-tuple-element.82), channel_id=1, source_target_pairs={{0,96},{32,0},{64,32},{96,64},{1,97},{33,1},{65,33},{97,65},{2,98}... | collective-permute-start | bytes 1572872 | tf_op jit(solution)/shard_map/ppermute | solution.py:20
  38.9 5.6 %collective-permute-done.13.refs_6_ = bf16[256,640]{1,0:T(8,128)(2,1)S(1)} collective-permute-done((bf16[256,640]{1,0:T(8,128)(2,1)S(1)}, bf16[256,640]{1,0:T(8,128)(2,1)S(1)}, u32[]{:S(2)}, u32[]{:S(2)}) %collective-permute-start.13) | collective-permute-done | bytes 327712 | tf_op jit(solution)/shard_map/ppermute | solution.py:20
  44.5 1.6 %collective-permute-done.10.refs_5_ = bf16[256,640]{1,0:T(8,128)(2,1)S(1)} collective-permute-done((bf16[256,640]{1,0:T(8,128)(2,1)S(1)}, bf16[256,640]{1,0:T(8,128)(2,1)S(1)}, u32[]{:S(2)}, u32[]{:S(2)}) %collective-permute-start.10) | collective-permute-done | bytes 327712 | tf_op jit(solution)/shard_map/ppermute | solution.py:25
  46.1 1.1 collective-permute-done.4.last_up_ref
  47.2 1.9 %collective-permute-done.5.last_down_ref = bf16[2,128,1024]{2,1,0:T(8,128)(2,1)S(1)} collective-permute-done((bf16[2,128,1024]{2,1,0:T(8,128)(2,1)S(1)}, bf16[2,128,1024]{2,1,0:T(8,128)(2,1)S(1)}, u32[]{:S(2)}, u32[]{:S(2)}) %collective-permute-start.5) | collective-permute-done | bytes 524320 | tf_op jit(solution)/shard_map/ppermute | solution.py:20
  50.5 2.4 %collective-permute-start.7 = (bf16[2,64,1024]{2,1,0:T(8,128)(2,1)S(1)}, bf16[2,64,1024]{2,1,0:T(8,128)(2,1)S(1)}, u32[]{:S(2)}, u32[]{:S(2)}) collective-permute-start(bf16[2,64,1024]{2,1,0:T(8,128)(2,1)S(1)} %get-tuple-element.69), channel_id=1, source_target_pairs={{0,96},{32,0},{64,32},{96,64},{1,97},{33,1},{65,33},{97,65},{2,98}... | collective-permute-start | bytes 786440 | tf_op jit(solution)/shard_map/ppermute | solution.py:20
  53.7 1.7 %collective-permute-start.19 = (bf16[2,64,1024]{2,1,0:T(8,128)(2,1)S(1)}, bf16[2,64,1024]{2,1,0:T(8,128)(2,1)S(1)}, u32[]{:S(2)}, u32[]{:S(2)}) collective-permute-start(bf16[2,64,1024]{2,1,0:T(8,128)(2,1)S(1)} %get-tuple-element.85), channel_id=1, source_target_pairs={{0,24},{8,0},{16,8},{24,16},{1,25},{9,1},{17,9},{25,17},{2,26},{10... | collective-permute-start | bytes 786440 | tf_op jit(solution)/shard_map/ppermute | solution.py:20
  55.5 2.6 %collective-permute-done.6.up_ref.refs_1_ = bf16[2,64,1024]{2,1,0:T(8,128)(2,1)S(1)} collective-permute-done((bf16[2,64,1024]{2,1,0:T(8,128)(2,1)S(1)}, bf16[2,64,1024]{2,1,0:T(8,128)(2,1)S(1)}, u32[]{:S(2)}, u32[]{:S(2)}) %collective-permute-start.6) | collective-permute-done | bytes 262176 | tf_op jit(solution)/shard_map/ppermute | solution.py:20
  59.1 2.3 %collective-permute-start.9 = (bf16[1,64,1024]{2,1,0:T(8,128)(2,1)S(1)}, bf16[1,64,1024]{2,1,0:T(8,128)(2,1)S(1)}, u32[]{:S(2)}, u32[]{:S(2)}) collective-permute-start(bf16[1,64,1024]{2,1,0:T(8,128)(2,1)S(1)} %get-tuple-element.72), channel_id=1, source_target_pairs={{0,96},{32,0},{64,32},{96,64},{1,97},{33,1},{65,33},{97,65},{2,98}... | collective-permute-start | bytes 393224 | tf_op jit(solution)/shard_map/ppermute | solution.py:20
  62.2 1.6 %collective-permute-start.21 = (bf16[1,64,1024]{2,1,0:T(8,128)(2,1)S(1)}, bf16[1,64,1024]{2,1,0:T(8,128)(2,1)S(1)}, u32[]{:S(2)}, u32[]{:S(2)}) collective-permute-start(bf16[1,64,1024]{2,1,0:T(8,128)(2,1)S(1)} %get-tuple-element.88), channel_id=1, source_target_pairs={{0,24},{8,0},{16,8},{24,16},{1,25},{9,1},{17,9},{25,17},{2,26},{10... | collective-permute-start | bytes 393224 | tf_op jit(solution)/shard_map/ppermute | solution.py:20
  64.4 2.3 %collective-permute-done.20.refs_8_ = bf16[1,64,1024]{2,1,0:T(8,128)(2,1)S(1)} collective-permute-done((bf16[1,64,1024]{2,1,0:T(8,128)(2,1)S(1)}, bf16[1,64,1024]{2,1,0:T(8,128)(2,1)S(1)}, u32[]{:S(2)}, u32[]{:S(2)}) %collective-permute-start.20) | collective-permute-done | bytes 131104 | tf_op jit(solution)/shard_map/ppermute | solution.py:20
  66.7 1.7 %collective-permute-done.21.refs_9_ = bf16[1,64,1024]{2,1,0:T(8,128)(2,1)S(1)} collective-permute-done((bf16[1,64,1024]{2,1,0:T(8,128)(2,1)S(1)}, bf16[1,64,1024]{2,1,0:T(8,128)(2,1)S(1)}, u32[]{:S(2)}, u32[]{:S(2)}) %collective-permute-start.21) | collective-permute-done | bytes 131104 | tf_op jit(solution)/shard_map/ppermute | solution.py:20
  69.3 7.8 %all-to-all-start = ((bf16[16,128,128]{2,1,0:T(8,128)(2,1)}), bf16[16,128,128]{2,1,0:T(8,128)(2,1)S(1)}, u32[]{:S(2)}, u32[]{:S(2)}) async-start(bf16[16,128,128]{2,1,0:T(8,128)(2,1)} %pieces.1), calls=%async_computation | async-start | bytes 1048576 | tf_op jit(solution)/shard_map/all_to_all | solution.py:546
  77.7 1.3 %collective-permute-done.22.refs_7_ = bf16[256,640]{1,0:T(8,128)(2,1)S(1)} collective-permute-done((bf16[256,640]{1,0:T(8,128)(2,1)S(1)}, bf16[256,640]{1,0:T(8,128)(2,1)S(1)}, u32[]{:S(2)}, u32[]{:S(2)}) %collective-permute-start.22) | collective-permute-done | bytes 327712 | tf_op jit(solution)/shard_map/ppermute | solution.py:25
  83.8 8.6 %left_root.1 = (bf16[1024,1024]{1,0:T(8,128)(2,1)S(1)}, bf16[4,256,640]{2,1,0:T(8,128)(2,1)S(1)}) custom-call(s32[4]{0:T(128)S(1)} %pad_add_fusion.place_ref, s32[1]{0:T(128)S(6)} %copy.4.table_ref, bf16[256,640]{1,0:T(8,128)(2,1)S(1)} %trim.1.refs_0_, bf16[256,640]{1,0:T(8,128)(2,1)S(1)} %copy-done.7, bf16[256,640]{1,0:T(8,128)(2,1)S(1)} %collective-permute-done.2.refs_2_, ...), custom_call_target="tpu_custom_call" | custom-call | flops 6442450944 | bytes 4194304 | tf_op jit(solution)/shard_map/left_root/pallas_call | solution.py:307
  94.4 2.0 %collective-permute-start.23 = (bf16[2,128,128]{2,1,0:T(8,128)(2,1)S(1)}, bf16[2,128,128]{2,1,0:T(8,128)(2,1)S(1)}, u32[]{:S(2)}, u32[]{:S(2)}) collective-permute-start(bf16[2,128,128]{2,1,0:T(8,128)(2,1)S(1)} %get-tuple-element.104), channel_id=1, source_target_pairs={{0,2},{2,4},{4,6},{6,0},{1,3},{3,5},{5,7},{7,1},{8,10},{10,12},{12... | collective-permute-start | bytes 196616 | tf_op jit(solution)/shard_map/ppermute | solution.py:20
  96.3 2.4 %collective-permute-start.24 = (bf16[2,128,128]{2,1,0:T(8,128)(2,1)S(1)}, bf16[2,128,128]{2,1,0:T(8,128)(2,1)S(1)}, u32[]{:S(2)}, u32[]{:S(2)}) collective-permute-start(bf16[2,128,128]{2,1,0:T(8,128)(2,1)S(1)} %get-tuple-element.105), channel_id=1, source_target_pairs={{0,4},{2,6},{4,0},{6,2},{1,5},{3,7},{5,1},{7,3},{8,12},{10,14},{12... | collective-permute-start | bytes 196616 | tf_op jit(solution)/shard_map/ppermute | solution.py:20
  98.7 1.5 %collective-permute-start.25 = (bf16[2,128,128]{2,1,0:T(8,128)(2,1)S(1)}, bf16[2,128,128]{2,1,0:T(8,128)(2,1)S(1)}, u32[]{:S(2)}, u32[]{:S(2)}) collective-permute-start(bf16[2,128,128]{2,1,0:T(8,128)(2,1)S(1)} %get-tuple-element.106), channel_id=1, source_target_pairs={{0,6},{2,0},{4,2},{6,4},{1,7},{3,1},{5,3},{7,5},{8,14},{10,8},{12,... | collective-permute-start | bytes 196616 | tf_op jit(solution)/shard_map/ppermute | solution.py:20
  100.2 1.4 %right_base.1 = (bf16[1024,1024]{1,0:T(8,128)(2,1)S(1)}, f32[8,1024]{1,0:T(8,128)S(1)}) custom-call(bf16[4,256,640]{2,1,0:T(8,128)(2,1)S(1)} %copy-done.2), custom_call_target="tpu_custom_call" | custom-call | flops 4194304 | bytes 4194304 | tf_op jit(solution)/shard_map/right_base/pallas_call | solution.py:46
  101.6 2.5 %collective-permute-done.24.refs_2_ = bf16[2,128,128]{2,1,0:T(8,128)(2,1)S(1)} collective-permute-done((bf16[2,128,128]{2,1,0:T(8,128)(2,1)S(1)}, bf16[2,128,128]{2,1,0:T(8,128)(2,1)S(1)}, u32[]{:S(2)}, u32[]{:S(2)}) %collective-permute-start.24) | collective-permute-done | bytes 65568 | tf_op jit(solution)/shard_map/ppermute | solution.py:20
  104.3 1.3 %collective-permute-done.26.refs_4_ = bf16[4,128,128]{2,1,0:T(8,128)(2,1)S(1)} collective-permute-done((bf16[4,128,128]{2,1,0:T(8,128)(2,1)S(1)}, bf16[4,128,128]{2,1,0:T(8,128)(2,1)S(1)}, u32[]{:S(2)}, u32[]{:S(2)}) %collective-permute-start.26) | collective-permute-done | bytes 131104 | tf_op jit(solution)/shard_map/ppermute | solution.py:25
  105.6 1.4 %condition.1 = (f32[128,1024]{1,0:T(8,128)S(1)}, f32[8,8,128]{2,1,0:T(8,128)S(1)}) custom-call(s32[1]{0:T(128)} %bitcast.zl_ref, s32[1]{0:T(128)} %bitcast.1.c_ref, bf16[2,128,128]{2,1,0:T(8,128)(2,1)S(1)} %get-tuple-element.103.refs_0_, bf16[2,128,128]{2,1,0:T(8,128)(2,1)S(1)} %collective-permute-done.23.refs_1_, ...), custom_call_target="tpu_custom_call" | custom-call | flops 1073741824 | bytes 2097152 | tf_op jit(solution)/shard_map/condition/pallas_call | solution.py:46
  107.0 9.5 %all_to_all.10.totals_ref = f32[8,8,128]{2,1,0:T(8,128)S(1)} all-to-all(f32[8,8,128]{2,1,0:T(8,128)S(1)} %get-tuple-element.109), channel_id=1, replica_groups=mesh['zh'=2,'y'=4,'x'=4,'zl'=4,'c'=2] {'zl','c'}, dimensions={0} | all-to-all | bytes 65536 | tf_op jit(solution)/shard_map/all_to_all | solution.py:552
  (70 shorter events, 18.5 us)
Async XLA Ops:
  0.1 13.3 %copy-start = (bf16[1,32,128,1024]{3,2,1,0:T(8,128)(2,1)S(1)}, bf16[1,32,128,1024]{3,2,1,0:T(8,128)(2,1)}, u32[]{:S(2)}) copy-start(bf16[1,32,128,1024]{3,2,1,0:T(8,128)(2,1)} %param.3) | copy-start | bytes 25165828
  3.6 28.8 %collective-permute-start = (bf16[4,128,1024]{2,1,0:T(8,128)(2,1)S(1)}, bf16[4,128,1024]{2,1,0:T(8,128)(2,1)S(1)}, u32[]{:S(2)}, u32[]{:S(2)}) collective-permute-start(bf16[4,128,1024]{2,1,0:T(8,128)(2,1)S(1)} %get-tuple-element.58), channel_id=1, source_target_pairs={{0,8},{8,16},{16,24},{24,0},{1,9},{9,17},{17,25},{25,1},{2,10},{10... | collective-permute-start | bytes 3145736 | tf_op jit(solution)/shard_map/ppermute | solution.py:20
  5.9 27.1 %collective-permute-start.1 = (bf16[4,128,1024]{2,1,0:T(8,128)(2,1)S(1)}, bf16[4,128,1024]{2,1,0:T(8,128)(2,1)S(1)}, u32[]{:S(2)}, u32[]{:S(2)}) collective-permute-start(bf16[4,128,1024]{2,1,0:T(8,128)(2,1)S(1)} %get-tuple-element.61), channel_id=1, source_target_pairs={{0,24},{8,0},{16,8},{24,16},{1,25},{9,1},{17,9},{25,17},{2,26},{10... | collective-permute-start | bytes 3145736 | tf_op jit(solution)/shard_map/ppermute | solution.py:20
  5.9 27.3 %collective-permute-start.14 = (bf16[4,128,1024]{2,1,0:T(8,128)(2,1)S(1)}, bf16[4,128,1024]{2,1,0:T(8,128)(2,1)S(1)}, u32[]{:S(2)}, u32[]{:S(2)}) collective-permute-start(bf16[4,128,1024]{2,1,0:T(8,128)(2,1)S(1)} %get-tuple-element.78), channel_id=1, source_target_pairs={{0,32},{32,64},{64,96},{96,0},{1,33},{33,65},{65,97},{97,1},{2,34}... | collective-permute-start | bytes 3145736 | tf_op jit(solution)/shard_map/ppermute | solution.py:20
  7.3 27.0 %collective-permute-start.15 = (bf16[4,128,1024]{2,1,0:T(8,128)(2,1)S(1)}, bf16[4,128,1024]{2,1,0:T(8,128)(2,1)S(1)}, u32[]{:S(2)}, u32[]{:S(2)}) collective-permute-start(bf16[4,128,1024]{2,1,0:T(8,128)(2,1)S(1)} %get-tuple-element.79), channel_id=1, source_target_pairs={{0,96},{32,0},{64,32},{96,64},{1,97},{33,1},{65,33},{97,65},{2,98}... | collective-permute-start | bytes 3145736 | tf_op jit(solution)/shard_map/ppermute | solution.py:20
  11.7 11.2 %collective-permute-start.2 = (bf16[256,640]{1,0:T(8,128)(2,1)S(1)}, bf16[256,640]{1,0:T(8,128)(2,1)S(1)}, u32[]{:S(2)}, u32[]{:S(2)}) collective-permute-start(bf16[256,640]{1,0:T(8,128)(2,1)S(1)} %trim.1.refs_0_), channel_id=1, source_target_pairs={{0,2},{2,4},{4,6},{6,0},{1,3},{3,5},{5,7},{7,1},{8,10},{10,12},{12... | collective-permute-start | bytes 983048 | tf_op jit(solution)/shard_map/ppermute | solution.py:20
  22.8 9.6 %collective-permute-start.3 = (bf16[256,640]{1,0:T(8,128)(2,1)S(1)}, bf16[256,640]{1,0:T(8,128)(2,1)S(1)}, u32[]{:S(2)}, u32[]{:S(2)}) collective-permute-start(bf16[256,640]{1,0:T(8,128)(2,1)S(1)} %collective-permute-done.2.refs_2_), channel_id=1, source_target_pairs={{0,2},{2,4},{4,6},{6,0},{1,3},{3,5},{5,7},{7,1},{8,10},{10,12},{12... | collective-permute-start | bytes 983048 | tf_op jit(solution)/shard_map/ppermute | solution.py:20
  32.4 3.1 %collective-permute-start.12 = (bf16[256,640]{1,0:T(8,128)(2,1)S(1)}, bf16[256,640]{1,0:T(8,128)(2,1)S(1)}, u32[]{:S(2)}, u32[]{:S(2)}) collective-permute-start(bf16[256,640]{1,0:T(8,128)(2,1)S(1)} %trim.1.refs_0_), channel_id=1, source_target_pairs={{0,1},{1,0},{2,3},{3,2},{4,5},{5,4},{6,7},{7,6},{8,9},{9,8},{10,11... | collective-permute-start | bytes 983048 | tf_op jit(solution)/shard_map/ppermute | solution.py:25
  32.4 3.7 %collective-permute-start.11 = (bf16[256,640]{1,0:T(8,128)(2,1)S(1)}, bf16[256,640]{1,0:T(8,128)(2,1)S(1)}, u32[]{:S(2)}, u32[]{:S(2)}) collective-permute-start(bf16[256,640]{1,0:T(8,128)(2,1)S(1)} %collective-permute-done.2.refs_2_), channel_id=1, source_target_pairs={{0,1},{1,0},{2,3},{3,2},{4,5},{5,4},{6,7},{7,6},{8,9},{9,8},{10,11... | collective-permute-start | bytes 983048 | tf_op jit(solution)/shard_map/ppermute | solution.py:25
  33.0 11.5 %collective-permute-start.13 = (bf16[256,640]{1,0:T(8,128)(2,1)S(1)}, bf16[256,640]{1,0:T(8,128)(2,1)S(1)}, u32[]{:S(2)}, u32[]{:S(2)}) collective-permute-start(bf16[256,640]{1,0:T(8,128)(2,1)S(1)} %collective-permute-done.3.refs_4_), channel_id=1, source_target_pairs={{0,2},{2,4},{4,6},{6,0},{1,3},{3,5},{5,7},{7,1},{8,10},{10,12},{12... | collective-permute-start | bytes 983048 | tf_op jit(solution)/shard_map/ppermute | solution.py:20
  33.2 14.0 %collective-permute-start.4 = (bf16[2,128,1024]{2,1,0:T(8,128)(2,1)S(1)}, bf16[2,128,1024]{2,1,0:T(8,128)(2,1)S(1)}, u32[]{:S(2)}, u32[]{:S(2)}) collective-permute-start(bf16[2,128,1024]{2,1,0:T(8,128)(2,1)S(1)} %get-tuple-element.65), channel_id=1, source_target_pairs={{0,8},{8,16},{16,24},{24,0},{1,9},{9,17},{17,25},{25,1},{2,10},{10... | collective-permute-start | bytes 1572872 | tf_op jit(solution)/shard_map/ppermute | solution.py:20
  34.3 14.9 %collective-permute-start.5 = (bf16[2,128,1024]{2,1,0:T(8,128)(2,1)S(1)}, bf16[2,128,1024]{2,1,0:T(8,128)(2,1)S(1)}, u32[]{:S(2)}, u32[]{:S(2)}) collective-permute-start(bf16[2,128,1024]{2,1,0:T(8,128)(2,1)S(1)} %get-tuple-element.66), channel_id=1, source_target_pairs={{0,24},{8,0},{16,8},{24,16},{1,25},{9,1},{17,9},{25,17},{2,26},{10... | collective-permute-start | bytes 1572872 | tf_op jit(solution)/shard_map/ppermute | solution.py:20
  35.6 14.0 %copy-start.6 = (bf16[256,640]{1,0:T(8,128)(2,1)}, bf16[256,640]{1,0:T(8,128)(2,1)S(1)}, u32[]{:S(2)}) copy-start(bf16[256,640]{1,0:T(8,128)(2,1)S(1)} %collective-permute-done.12.refs_1_) | copy-start | bytes 983044
  35.6 17.3 %collective-permute-start.16 = (bf16[2,128,1024]{2,1,0:T(8,128)(2,1)S(1)}, bf16[2,128,1024]{2,1,0:T(8,128)(2,1)S(1)}, u32[]{:S(2)}, u32[]{:S(2)}) collective-permute-start(bf16[2,128,1024]{2,1,0:T(8,128)(2,1)S(1)} %get-tuple-element.81), channel_id=1, source_target_pairs={{0,32},{32,64},{64,96},{96,0},{1,33},{33,65},{65,97},{97,1},{2,34}... | collective-permute-start | bytes 1572872 | tf_op jit(solution)/shard_map/ppermute | solution.py:20
  36.2 13.4 %copy-start.8 = (bf16[256,640]{1,0:T(8,128)(2,1)}, bf16[256,640]{1,0:T(8,128)(2,1)S(1)}, u32[]{:S(2)}) copy-start(bf16[256,640]{1,0:T(8,128)(2,1)S(1)} %collective-permute-done.11.refs_3_) | copy-start | bytes 983044
  36.2 16.7 %collective-permute-start.17 = (bf16[2,128,1024]{2,1,0:T(8,128)(2,1)S(1)}, bf16[2,128,1024]{2,1,0:T(8,128)(2,1)S(1)}, u32[]{:S(2)}, u32[]{:S(2)}) collective-permute-start(bf16[2,128,1024]{2,1,0:T(8,128)(2,1)S(1)} %get-tuple-element.82), channel_id=1, source_target_pairs={{0,96},{32,0},{64,32},{96,64},{1,97},{33,1},{65,33},{97,65},{2,98}... | collective-permute-start | bytes 1572872 | tf_op jit(solution)/shard_map/ppermute | solution.py:20
  44.5 32.7 %copy-start.10 = (bf16[256,640]{1,0:T(8,128)(2,1)}, bf16[256,640]{1,0:T(8,128)(2,1)S(1)}, u32[]{:S(2)}) copy-start(bf16[256,640]{1,0:T(8,128)(2,1)S(1)} %collective-permute-done.13.refs_6_) | copy-start | bytes 983044
  44.5 1.6 %collective-permute-start.10 = (bf16[256,640]{1,0:T(8,128)(2,1)S(1)}, bf16[256,640]{1,0:T(8,128)(2,1)S(1)}, u32[]{:S(2)}, u32[]{:S(2)}) collective-permute-start(bf16[256,640]{1,0:T(8,128)(2,1)S(1)} %collective-permute-done.3.refs_4_), channel_id=1, source_target_pairs={{0,1},{1,0},{2,3},{3,2},{4,5},{5,4},{6,7},{7,6},{8,9},{9,8},{10,11... | collective-permute-start | bytes 983048 | tf_op jit(solution)/shard_map/ppermute | solution.py:25
  49.6 8.4 %collective-permute-start.6 = (bf16[2,64,1024]{2,1,0:T(8,128)(2,1)S(1)}, bf16[2,64,1024]{2,1,0:T(8,128)(2,1)S(1)}, u32[]{:S(2)}, u32[]{:S(2)}) collective-permute-start(bf16[2,64,1024]{2,1,0:T(8,128)(2,1)S(1)} %get-tuple-element.68), channel_id=1, source_target_pairs={{0,32},{32,64},{64,96},{96,0},{1,33},{33,65},{65,97},{97,1},{2,34}... | collective-permute-start | bytes 786440 | tf_op jit(solution)/shard_map/ppermute | solution.py:20
  50.5 7.6 %collective-permute-start.7 = (bf16[2,64,1024]{2,1,0:T(8,128)(2,1)S(1)}, bf16[2,64,1024]{2,1,0:T(8,128)(2,1)S(1)}, u32[]{:S(2)}, u32[]{:S(2)}) collective-permute-start(bf16[2,64,1024]{2,1,0:T(8,128)(2,1)S(1)} %get-tuple-element.69), channel_id=1, source_target_pairs={{0,96},{32,0},{64,32},{96,64},{1,97},{33,1},{65,33},{97,65},{2,98}... | collective-permute-start | bytes 786440 | tf_op jit(solution)/shard_map/ppermute | solution.py:20
  53.4 8.1 %collective-permute-start.18 = (bf16[2,64,1024]{2,1,0:T(8,128)(2,1)S(1)}, bf16[2,64,1024]{2,1,0:T(8,128)(2,1)S(1)}, u32[]{:S(2)}, u32[]{:S(2)}) collective-permute-start(bf16[2,64,1024]{2,1,0:T(8,128)(2,1)S(1)} %get-tuple-element.84), channel_id=1, source_target_pairs={{0,8},{8,16},{16,24},{24,0},{1,9},{9,17},{17,25},{25,1},{2,10},{10... | collective-permute-start | bytes 786440 | tf_op jit(solution)/shard_map/ppermute | solution.py:20
  53.7 7.8 %collective-permute-start.19 = (bf16[2,64,1024]{2,1,0:T(8,128)(2,1)S(1)}, bf16[2,64,1024]{2,1,0:T(8,128)(2,1)S(1)}, u32[]{:S(2)}, u32[]{:S(2)}) collective-permute-start(bf16[2,64,1024]{2,1,0:T(8,128)(2,1)S(1)} %get-tuple-element.85), channel_id=1, source_target_pairs={{0,24},{8,0},{16,8},{24,16},{1,25},{9,1},{17,9},{25,17},{2,26},{10... | collective-permute-start | bytes 786440 | tf_op jit(solution)/shard_map/ppermute | solution.py:20
  58.1 6.3 %collective-permute-start.8 = (bf16[1,64,1024]{2,1,0:T(8,128)(2,1)S(1)}, bf16[1,64,1024]{2,1,0:T(8,128)(2,1)S(1)}, u32[]{:S(2)}, u32[]{:S(2)}) collective-permute-start(bf16[1,64,1024]{2,1,0:T(8,128)(2,1)S(1)} %get-tuple-element.71), channel_id=1, source_target_pairs={{0,32},{32,64},{64,96},{96,0},{1,33},{33,65},{65,97},{97,1},{2,34}... | collective-permute-start | bytes 393224 | tf_op jit(solution)/shard_map/ppermute | solution.py:20
  59.1 5.2 %collective-permute-start.9 = (bf16[1,64,1024]{2,1,0:T(8,128)(2,1)S(1)}, bf16[1,64,1024]{2,1,0:T(8,128)(2,1)S(1)}, u32[]{:S(2)}, u32[]{:S(2)}) collective-permute-start(bf16[1,64,1024]{2,1,0:T(8,128)(2,1)S(1)} %get-tuple-element.72), channel_id=1, source_target_pairs={{0,96},{32,0},{64,32},{96,64},{1,97},{33,1},{65,33},{97,65},{2,98}... | collective-permute-start | bytes 393224 | tf_op jit(solution)/shard_map/ppermute | solution.py:20
  61.7 5.0 %collective-permute-start.20 = (bf16[1,64,1024]{2,1,0:T(8,128)(2,1)S(1)}, bf16[1,64,1024]{2,1,0:T(8,128)(2,1)S(1)}, u32[]{:S(2)}, u32[]{:S(2)}) collective-permute-start(bf16[1,64,1024]{2,1,0:T(8,128)(2,1)S(1)} %get-tuple-element.87), channel_id=1, source_target_pairs={{0,8},{8,16},{16,24},{24,0},{1,9},{9,17},{17,25},{25,1},{2,10},{10... | collective-permute-start | bytes 393224 | tf_op jit(solution)/shard_map/ppermute | solution.py:20
  62.2 6.2 %collective-permute-start.21 = (bf16[1,64,1024]{2,1,0:T(8,128)(2,1)S(1)}, bf16[1,64,1024]{2,1,0:T(8,128)(2,1)S(1)}, u32[]{:S(2)}, u32[]{:S(2)}) collective-permute-start(bf16[1,64,1024]{2,1,0:T(8,128)(2,1)S(1)} %get-tuple-element.88), channel_id=1, source_target_pairs={{0,24},{8,0},{16,8},{24,16},{1,25},{9,1},{17,9},{25,17},{2,26},{10... | collective-permute-start | bytes 393224 | tf_op jit(solution)/shard_map/ppermute | solution.py:20
  69.3 24.2 %all-to-all-start = ((bf16[16,128,128]{2,1,0:T(8,128)(2,1)}), bf16[16,128,128]{2,1,0:T(8,128)(2,1)S(1)}, u32[]{:S(2)}, u32[]{:S(2)}) async-start(bf16[16,128,128]{2,1,0:T(8,128)(2,1)} %pieces.1), calls=%async_computation | async-start | bytes 1048576 | tf_op jit(solution)/shard_map/all_to_all | solution.py:546
  77.2 1.7 %collective-permute-start.22 = (bf16[256,640]{1,0:T(8,128)(2,1)S(1)}, bf16[256,640]{1,0:T(8,128)(2,1)S(1)}, u32[]{:S(2)}, u32[]{:S(2)}) collective-permute-start(bf16[256,640]{1,0:T(8,128)(2,1)S(1)} %collective-permute-done.13.refs_6_), channel_id=1, source_target_pairs={{0,1},{1,0},{2,3},{3,2},{4,5},{5,4},{6,7},{7,6},{8,9},{9,8},{10,11... | collective-permute-start | bytes 983048 | tf_op jit(solution)/shard_map/ppermute | solution.py:25
  94.4 7.2 %collective-permute-start.23 = (bf16[2,128,128]{2,1,0:T(8,128)(2,1)S(1)}, bf16[2,128,128]{2,1,0:T(8,128)(2,1)S(1)}, u32[]{:S(2)}, u32[]{:S(2)}) collective-permute-start(bf16[2,128,128]{2,1,0:T(8,128)(2,1)S(1)} %get-tuple-element.104), channel_id=1, source_target_pairs={{0,2},{2,4},{4,6},{6,0},{1,3},{3,5},{5,7},{7,1},{8,10},{10,12},{12... | collective-permute-start | bytes 196616 | tf_op jit(solution)/shard_map/ppermute | solution.py:20
  96.3 7.8 %collective-permute-start.24 = (bf16[2,128,128]{2,1,0:T(8,128)(2,1)S(1)}, bf16[2,128,128]{2,1,0:T(8,128)(2,1)S(1)}, u32[]{:S(2)}, u32[]{:S(2)}) collective-permute-start(bf16[2,128,128]{2,1,0:T(8,128)(2,1)S(1)} %get-tuple-element.105), channel_id=1, source_target_pairs={{0,4},{2,6},{4,0},{6,2},{1,5},{3,7},{5,1},{7,3},{8,12},{10,14},{12... | collective-permute-start | bytes 196616 | tf_op jit(solution)/shard_map/ppermute | solution.py:20
  98.7 5.5 %collective-permute-start.25 = (bf16[2,128,128]{2,1,0:T(8,128)(2,1)S(1)}, bf16[2,128,128]{2,1,0:T(8,128)(2,1)S(1)}, u32[]{:S(2)}, u32[]{:S(2)}) collective-permute-start(bf16[2,128,128]{2,1,0:T(8,128)(2,1)S(1)} %get-tuple-element.106), channel_id=1, source_target_pairs={{0,6},{2,0},{4,2},{6,4},{1,7},{3,1},{5,3},{7,5},{8,14},{10,8},{12,... | collective-permute-start | bytes 196616 | tf_op jit(solution)/shard_map/ppermute | solution.py:20
  104.2 1.4 %collective-permute-start.26 = (bf16[4,128,128]{2,1,0:T(8,128)(2,1)S(1)}, bf16[4,128,128]{2,1,0:T(8,128)(2,1)S(1)}, u32[]{:S(2)}, u32[]{:S(2)}) collective-permute-start(bf16[4,128,128]{2,1,0:T(8,128)(2,1)S(1)} %split.1), channel_id=1, source_target_pairs={{0,1},{1,0},{2,3},{3,2},{4,5},{5,4},{6,7},{7,6},{8,9},{9,8},{10,11... | collective-permute-start | bytes 393224 | tf_op jit(solution)/shard_map/ppermute | solution.py:25
  (10 other events, 29.4 us)

commit v6 on v4

--- a/solution.py
+++ b/solution.py
@@ -522,7 +522,7 @@
     x_mid, x_own, y_mid, y_own = pack(keep_kernel, 16, sent, grads)
     near.append(shift(*after(x_mid, near[1]), "zl", 1))
     near.append(shift(near[2], "zl", 1))
-    (x_mid,) = after(near[2], x_mid)
+    (y_mid,) = after(near[2], y_mid)
     x_last = pass_on(x_mid, *x_ends)
     y_last = pass_on(y_mid, *y_ends)
     far = [swap(each, "c", 1) for each in near[:3]]

time: 115 us -> 112 us (0.974); the launches traced: 113 us -> 112 us
  waiting for transfers between devices: 38.6 us -> 35.1 us
  starting transfers between devices: 38.4 us -> 40.3 us
    ppermute x22, waiting for transfers between devices: 35 us -> 31.4 us  [shift(): lax.ppermute(array, axis, [(i, (i + step) % size) for i in range(size)])]
    ppermute x22, starting transfers between devices: 29.9 us -> 31.2 us  [shift(): lax.ppermute(array, axis, [(i, (i + step) % size) for i in range(size)])]
  transfers between devices with their start and end apart: 28 -> 28, of which waited for: 15 -> 16; matrix products, arithmetic and copies ran while one was open for 0% -> 0% of each run, Pallas kernels for 13% -> 13%
where the time goes in v6:
time: 112 us
  starting transfers between devices  40.3 us (36%)
  waiting for transfers between devices  35.1 us (31%)
  Pallas kernels  21.4 us (19%)
  blocking collectives  9.13 us (8%)
  local copies, waits for them, and re-layouts  5.01 us (4%)
    ppermute x22, waiting for transfers between devices, shift(): lax.ppermute(array, axis, [(i, (i + step) % size) for i in range(size)])  31.4 us
    ppermute x22, starting transfers between devices, shift(): lax.ppermute(array, axis, [(i, (i + step) % size) for i in range(size)])  31.2 us
    pallas_call x15, Pallas kernels, call(): pl.pallas_call(kernel, out_shape=out_shape, in_specs=in_specs, out_specs=...  12.7 us
    all_to_all x1, blocking collectives, local(): lax.all_to_all(totals, owner, split_axis=0, concat_axis=0, tiled=True)  9.13 us
    pallas_call x1, Pallas kernels, left_inverse_root(): pl.pallas_call(root_kernel, out_shape=(jax.ShapeDtypeStruct(matrix, jnp.b...  8.61 us
    all_to_all x1, starting transfers between devices, local(): lax.all_to_all(pieces, ('zh',) + owner, split_axis=0, concat_axis=0, tile...  7.7 us
    unnamed x16, local copies, waits for them, and re-layouts  5.01 us
    ppermute x5, waiting for transfers between devices, swap(): return lax.ppermute(array, axis, [(i, i ^ mask) for i in range(size)])  2.4 us
  transfers between devices with their start and end apart: 28, of which 16 were waited for; matrix products, arithmetic and copies ran while one was open for 0% of the time, Pallas kernels for 13%

profile of v6, /device:TPU:6, one launch (start us, length us, event | category | flops | bytes accessed | tf_op | source)
XLA Modules:
  0.0 111.7 jit_solution(16656892104314091448)
XLA Ops:
  0.1 3.5 %send.1 = (bf16[4,128,1024]{2,1,0:T(8,128)(2,1)S(1)}, bf16[4,128,1024]{2,1,0:T(8,128)(2,1)S(1)}, bf16[4,128,1024]{2,1,0:T(8,128)(2,1)S(1)}, bf16[4,128,1024]{2,1,0:T(8,128)(2,1)S(1)}) custom-call(s32[4]{0:T(128)S(1)} %pad_add_fusion.place_ref, bf16[2,4,4,128,1024]{4,3,2,1,0:T(8,128)(2,1)} %bitcast.7), custom_call_target="tpu_custom_call" | custom-call | bytes 8388608 | tf_op jit(solution)/shard_map/send/pallas_call | solution.py:46
  3.6 2.3 %collective-permute-start = (bf16[4,128,1024]{2,1,0:T(8,128)(2,1)S(1)}, bf16[4,128,1024]{2,1,0:T(8,128)(2,1)S(1)}, u32[]{:S(2)}, u32[]{:S(2)}) collective-permute-start(bf16[4,128,1024]{2,1,0:T(8,128)(2,1)S(1)} %get-tuple-element.54), channel_id=1, source_target_pairs={{0,8},{8,16},{16,24},{24,0},{1,9},{9,17},{17,25},{25,1},{2,10},{10... | collective-permute-start | bytes 3145736 | tf_op jit(solution)/shard_map/ppermute | solution.py:20
  5.9 1.4 %collective-permute-start.8 = (bf16[4,128,1024]{2,1,0:T(8,128)(2,1)S(1)}, bf16[4,128,1024]{2,1,0:T(8,128)(2,1)S(1)}, u32[]{:S(2)}, u32[]{:S(2)}) collective-permute-start(bf16[4,128,1024]{2,1,0:T(8,128)(2,1)S(1)} %get-tuple-element.68), channel_id=1, source_target_pairs={{0,32},{32,64},{64,96},{96,0},{1,33},{33,65},{65,97},{97,1},{2,34}... | collective-permute-start | bytes 3145736 | tf_op jit(solution)/shard_map/ppermute | solution.py:20
  7.3 1.9 %collective-permute-start.9 = (bf16[4,128,1024]{2,1,0:T(8,128)(2,1)S(1)}, bf16[4,128,1024]{2,1,0:T(8,128)(2,1)S(1)}, u32[]{:S(2)}, u32[]{:S(2)}) collective-permute-start(bf16[4,128,1024]{2,1,0:T(8,128)(2,1)S(1)} %get-tuple-element.69), channel_id=1, source_target_pairs={{0,96},{32,0},{64,32},{96,64},{1,97},{33,1},{65,33},{97,65},{2,98}... | collective-permute-start | bytes 3145736 | tf_op jit(solution)/shard_map/ppermute | solution.py:20
  9.8 1.2 %copy-done.3 = f32[1,1,256,1024]{3,2,1,0:T(8,128)S(1)} copy-done((f32[1,1,256,1024]{3,2,1,0:T(8,128)S(1)}, f32[1,1,256,1024]{3,2,1,0:T(8,128)}, u32[]{:S(2)}) %copy-start.3) | copy-done | bytes 1048600
  11.6 1.9 %collective-permute-start.10 = (bf16[256,640]{1,0:T(8,128)(2,1)S(1)}, bf16[256,640]{1,0:T(8,128)(2,1)S(1)}, u32[]{:S(2)}, u32[]{:S(2)}) collective-permute-start(bf16[256,640]{1,0:T(8,128)(2,1)S(1)} %trim.1.refs_0_), channel_id=1, source_target_pairs={{0,2},{2,4},{4,6},{6,0},{1,3},{3,5},{5,7},{7,1},{8,10},{10,12},{12... | collective-permute-start | bytes 983048 | tf_op jit(solution)/shard_map/ppermute | solution.py:20
  13.5 1.4 %keep.1 = (bf16[4,128,1024]{2,1,0:T(8,128)(2,1)S(1)}, bf16[4,128,1024]{2,1,0:T(8,128)(2,1)S(1)}, bf16[4,128,1024]{2,1,0:T(8,128)(2,1)S(1)}, bf16[4,128,1024]{2,1,0:T(8,128)(2,1)S(1)}) custom-call(s32[4]{0:T(128)S(1)} %pad_add_fusion.place_ref, bf16[2,4,4,128,1024]{4,3,2,1,0:T(8,128)(2,1)S(1)} %bitcast.8), custom_call_target="tpu_custom_call" | custom-call | bytes 8388608 | tf_op jit(solution)/shard_map/keep/pallas_call | solution.py:46
  14.9 7.8 %collective-permute-done.10.refs_2_ = bf16[256,640]{1,0:T(8,128)(2,1)S(1)} collective-permute-done((bf16[256,640]{1,0:T(8,128)(2,1)S(1)}, bf16[256,640]{1,0:T(8,128)(2,1)S(1)}, u32[]{:S(2)}, u32[]{:S(2)}) %collective-permute-start.10) | collective-permute-done | bytes 327712 | tf_op jit(solution)/shard_map/ppermute | solution.py:20
  22.8 5.8 %collective-permute-done.up_ref = bf16[4,128,1024]{2,1,0:T(8,128)(2,1)S(1)} collective-permute-done((bf16[4,128,1024]{2,1,0:T(8,128)(2,1)S(1)}, bf16[4,128,1024]{2,1,0:T(8,128)(2,1)S(1)}, u32[]{:S(2)}, u32[]{:S(2)}) %collective-permute-start) | collective-permute-done | bytes 1048608 | tf_op jit(solution)/shard_map/ppermute | solution.py:20
  28.6 1.3 %collective-permute-done.1.down_ref = bf16[4,128,1024]{2,1,0:T(8,128)(2,1)S(1)} collective-permute-done((bf16[4,128,1024]{2,1,0:T(8,128)(2,1)S(1)}, bf16[4,128,1024]{2,1,0:T(8,128)(2,1)S(1)}, u32[]{:S(2)}, u32[]{:S(2)}) %collective-permute-start.1) | collective-permute-done | bytes 1048608 | tf_op jit(solution)/shard_map/ppermute | solution.py:20
  30.6 1.6 %collective-permute-start.3 = (bf16[2,128,1024]{2,1,0:T(8,128)(2,1)S(1)}, bf16[2,128,1024]{2,1,0:T(8,128)(2,1)S(1)}, u32[]{:S(2)}, u32[]{:S(2)}) collective-permute-start(bf16[2,128,1024]{2,1,0:T(8,128)(2,1)S(1)} %get-tuple-element.60), channel_id=1, source_target_pairs={{0,24},{8,0},{16,8},{24,16},{1,25},{9,1},{17,9},{25,17},{2,26},{10... | collective-permute-start | bytes 1572872 | tf_op jit(solution)/shard_map/ppermute | solution.py:20
  32.5 1.7 %collective-permute-start.12 = (bf16[2,128,1024]{2,1,0:T(8,128)(2,1)S(1)}, bf16[2,128,1024]{2,1,0:T(8,128)(2,1)S(1)}, u32[]{:S(2)}, u32[]{:S(2)}) collective-permute-start(bf16[2,128,1024]{2,1,0:T(8,128)(2,1)S(1)} %get-tuple-element.73), channel_id=1, source_target_pairs={{0,32},{32,64},{64,96},{96,0},{1,33},{33,65},{65,97},{97,1},{2,34}... | collective-permute-start | bytes 1572872 | tf_op jit(solution)/shard_map/ppermute | solution.py:20
  34.3 1.6 %collective-permute-start.13 = (bf16[2,128,1024]{2,1,0:T(8,128)(2,1)S(1)}, bf16[2,128,1024]{2,1,0:T(8,128)(2,1)S(1)}, u32[]{:S(2)}, u32[]{:S(2)}) collective-permute-start(bf16[2,128,1024]{2,1,0:T(8,128)(2,1)S(1)} %get-tuple-element.74), channel_id=1, source_target_pairs={{0,96},{32,0},{64,32},{96,64},{1,97},{33,1},{65,33},{97,65},{2,98}... | collective-permute-start | bytes 1572872 | tf_op jit(solution)/shard_map/ppermute | solution.py:20
  35.8 5.8 %collective-permute-done.2.last_up_ref = bf16[2,128,1024]{2,1,0:T(8,128)(2,1)S(1)} collective-permute-done((bf16[2,128,1024]{2,1,0:T(8,128)(2,1)S(1)}, bf16[2,128,1024]{2,1,0:T(8,128)(2,1)S(1)}, u32[]{:S(2)}, u32[]{:S(2)}) %collective-permute-start.2) | collective-permute-done | bytes 524320 | tf_op jit(solution)/shard_map/ppermute | solution.py:20
  41.7 1.9 %collective-permute-done.3.last_down_ref = bf16[2,128,1024]{2,1,0:T(8,128)(2,1)S(1)} collective-permute-done((bf16[2,128,1024]{2,1,0:T(8,128)(2,1)S(1)}, bf16[2,128,1024]{2,1,0:T(8,128)(2,1)S(1)}, u32[]{:S(2)}, u32[]{:S(2)}) %collective-permute-start.3) | collective-permute-done | bytes 524320 | tf_op jit(solution)/shard_map/ppermute | solution.py:20
  44.1 2.3 %collective-permute-start.4 = (bf16[2,64,1024]{2,1,0:T(8,128)(2,1)S(1)}, bf16[2,64,1024]{2,1,0:T(8,128)(2,1)S(1)}, u32[]{:S(2)}, u32[]{:S(2)}) collective-permute-start(bf16[2,64,1024]{2,1,0:T(8,128)(2,1)S(1)} %get-tuple-element.62), channel_id=1, source_target_pairs={{0,32},{32,64},{64,96},{96,0},{1,33},{33,65},{65,97},{97,1},{2,34}... | collective-permute-start | bytes 786440 | tf_op jit(solution)/shard_map/ppermute | solution.py:20
  46.4 1.5 %collective-permute-start.5 = (bf16[2,64,1024]{2,1,0:T(8,128)(2,1)S(1)}, bf16[2,64,1024]{2,1,0:T(8,128)(2,1)S(1)}, u32[]{:S(2)}, u32[]{:S(2)}) collective-permute-start(bf16[2,64,1024]{2,1,0:T(8,128)(2,1)S(1)} %get-tuple-element.63), channel_id=1, source_target_pairs={{0,96},{32,0},{64,32},{96,64},{1,97},{33,1},{65,33},{97,65},{2,98}... | collective-permute-start | bytes 786440 | tf_op jit(solution)/shard_map/ppermute | solution.py:20
  49.0 1.7 %collective-permute-start.15 = (bf16[2,64,1024]{2,1,0:T(8,128)(2,1)S(1)}, bf16[2,64,1024]{2,1,0:T(8,128)(2,1)S(1)}, u32[]{:S(2)}, u32[]{:S(2)}) collective-permute-start(bf16[2,64,1024]{2,1,0:T(8,128)(2,1)S(1)} %get-tuple-element.77), channel_id=1, source_target_pairs={{0,24},{8,0},{16,8},{24,16},{1,25},{9,1},{17,9},{25,17},{2,26},{10... | collective-permute-start | bytes 786440 | tf_op jit(solution)/shard_map/ppermute | solution.py:20
  50.7 2.0 %collective-permute-start.21 = (bf16[256,640]{1,0:T(8,128)(2,1)S(1)}, bf16[256,640]{1,0:T(8,128)(2,1)S(1)}, u32[]{:S(2)}, u32[]{:S(2)}) collective-permute-start(bf16[256,640]{1,0:T(8,128)(2,1)S(1)} %collective-permute-done.11.refs_4_), channel_id=1, source_target_pairs={{0,2},{2,4},{4,6},{6,0},{1,3},{3,5},{5,7},{7,1},{8,10},{10,12},{12... | collective-permute-start | bytes 983048 | tf_op jit(solution)/shard_map/ppermute | solution.py:20
  52.9 1.7 %collective-permute-start.6 = (bf16[1,64,1024]{2,1,0:T(8,128)(2,1)S(1)}, bf16[1,64,1024]{2,1,0:T(8,128)(2,1)S(1)}, u32[]{:S(2)}, u32[]{:S(2)}) collective-permute-start(bf16[1,64,1024]{2,1,0:T(8,128)(2,1)S(1)} %get-tuple-element.65), channel_id=1, source_target_pairs={{0,32},{32,64},{64,96},{96,0},{1,33},{33,65},{65,97},{97,1},{2,34}... | collective-permute-start | bytes 393224 | tf_op jit(solution)/shard_map/ppermute | solution.py:20
  54.5 1.7 %collective-permute-start.7 = (bf16[1,64,1024]{2,1,0:T(8,128)(2,1)S(1)}, bf16[1,64,1024]{2,1,0:T(8,128)(2,1)S(1)}, u32[]{:S(2)}, u32[]{:S(2)}) collective-permute-start(bf16[1,64,1024]{2,1,0:T(8,128)(2,1)S(1)} %get-tuple-element.66), channel_id=1, source_target_pairs={{0,96},{32,0},{64,32},{96,64},{1,97},{33,1},{65,33},{97,65},{2,98}... | collective-permute-start | bytes 393224 | tf_op jit(solution)/shard_map/ppermute | solution.py:20
  59.5 2.2 %collective-permute-done.16.refs_8_ = bf16[1,64,1024]{2,1,0:T(8,128)(2,1)S(1)} collective-permute-done((bf16[1,64,1024]{2,1,0:T(8,128)(2,1)S(1)}, bf16[1,64,1024]{2,1,0:T(8,128)(2,1)S(1)}, u32[]{:S(2)}, u32[]{:S(2)}) %collective-permute-start.16) | collective-permute-done | bytes 131104 | tf_op jit(solution)/shard_map/ppermute | solution.py:20
  61.7 2.3 %collective-permute-done.17.refs_9_ = bf16[1,64,1024]{2,1,0:T(8,128)(2,1)S(1)} collective-permute-done((bf16[1,64,1024]{2,1,0:T(8,128)(2,1)S(1)}, bf16[1,64,1024]{2,1,0:T(8,128)(2,1)S(1)}, u32[]{:S(2)}, u32[]{:S(2)}) %collective-permute-start.17) | collective-permute-done | bytes 131104 | tf_op jit(solution)/shard_map/ppermute | solution.py:20
  64.9 7.7 %all-to-all-start = ((bf16[16,128,128]{2,1,0:T(8,128)(2,1)}), bf16[16,128,128]{2,1,0:T(8,128)(2,1)S(1)}, u32[]{:S(2)}, u32[]{:S(2)}) async-start(bf16[16,128,128]{2,1,0:T(8,128)(2,1)} %pieces.1), calls=%async_computation | async-start | bytes 1048576 | tf_op jit(solution)/shard_map/all_to_all | solution.py:544
  77.7 8.6 %left_root.1 = (bf16[1024,1024]{1,0:T(8,128)(2,1)S(1)}, bf16[4,256,640]{2,1,0:T(8,128)(2,1)S(1)}) custom-call(s32[4]{0:T(128)S(1)} %pad_add_fusion.place_ref, s32[1]{0:T(128)S(6)} %copy.4.table_ref, bf16[256,640]{1,0:T(8,128)(2,1)S(1)} %trim.1.refs_0_, bf16[256,640]{1,0:T(8,128)(2,1)S(1)} %collective-permute-done.18.refs_1_, ...), custom_call_target="tpu_custom_call" | custom-call | flops 6442450944 | bytes 4194304 | tf_op jit(solution)/shard_map/left_root/pallas_call | solution.py:307
  87.5 1.2 %all-to-all-done.pieces_ref = bf16[16,128,128]{2,1,0:T(8,128)(2,1)S(1)} async-done(((bf16[16,128,128]{2,1,0:T(8,128)(2,1)}), bf16[16,128,128]{2,1,0:T(8,128)(2,1)S(1)}, u32[]{:S(2)}, u32[]{:S(2)}) %all-to-all-start) | async-done | bytes 524320 | tf_op jit(solution)/shard_map/all_to_all | solution.py:544
  90.2 2.7 %collective-permute-start.24 = (bf16[2,128,128]{2,1,0:T(8,128)(2,1)S(1)}, bf16[2,128,128]{2,1,0:T(8,128)(2,1)S(1)}, u32[]{:S(2)}, u32[]{:S(2)}) collective-permute-start(bf16[2,128,128]{2,1,0:T(8,128)(2,1)S(1)} %get-tuple-element.97), channel_id=1, source_target_pairs={{0,4},{2,6},{4,0},{6,2},{1,5},{3,7},{5,1},{7,3},{8,12},{10,14},{12... | collective-permute-start | bytes 196616 | tf_op jit(solution)/shard_map/ppermute | solution.py:20
  92.8 1.4 %collective-permute-start.25 = (bf16[2,128,128]{2,1,0:T(8,128)(2,1)S(1)}, bf16[2,128,128]{2,1,0:T(8,128)(2,1)S(1)}, u32[]{:S(2)}, u32[]{:S(2)}) collective-permute-start(bf16[2,128,128]{2,1,0:T(8,128)(2,1)S(1)} %get-tuple-element.98), channel_id=1, source_target_pairs={{0,6},{2,0},{4,2},{6,4},{1,7},{3,1},{5,3},{7,5},{8,14},{10,8},{12,... | collective-permute-start | bytes 196616 | tf_op jit(solution)/shard_map/ppermute | solution.py:20
  94.3 1.4 %right_base.1 = (bf16[1024,1024]{1,0:T(8,128)(2,1)S(1)}, f32[8,1024]{1,0:T(8,128)S(1)}) custom-call(bf16[4,256,640]{2,1,0:T(8,128)(2,1)S(1)} %copy-done.2), custom_call_target="tpu_custom_call" | custom-call | flops 4194304 | bytes 4194304 | tf_op jit(solution)/shard_map/right_base/pallas_call | solution.py:46
  95.7 2.9 %collective-permute-done.24.refs_2_ = bf16[2,128,128]{2,1,0:T(8,128)(2,1)S(1)} collective-permute-done((bf16[2,128,128]{2,1,0:T(8,128)(2,1)S(1)}, bf16[2,128,128]{2,1,0:T(8,128)(2,1)S(1)}, u32[]{:S(2)}, u32[]{:S(2)}) %collective-permute-start.24) | collective-permute-done | bytes 65568 | tf_op jit(solution)/shard_map/ppermute | solution.py:20
  100.1 1.4 %condition.1 = (f32[128,1024]{1,0:T(8,128)S(1)}, f32[8,8,128]{2,1,0:T(8,128)S(1)}) custom-call(s32[1]{0:T(128)} %bitcast.zl_ref, s32[1]{0:T(128)} %bitcast.1.c_ref, bf16[2,128,128]{2,1,0:T(8,128)(2,1)S(1)} %get-tuple-element.95.refs_0_, bf16[2,128,128]{2,1,0:T(8,128)(2,1)S(1)} %collective-permute-done.23.refs_1_, ...), custom_call_target="tpu_custom_call" | custom-call | flops 1073741824 | bytes 2097152 | tf_op jit(solution)/shard_map/condition/pallas_call | solution.py:46
  101.6 9.1 %all_to_all.10.totals_ref = f32[8,8,128]{2,1,0:T(8,128)S(1)} all-to-all(f32[8,8,128]{2,1,0:T(8,128)S(1)} %get-tuple-element.101), channel_id=1, replica_groups=mesh['zh'=2,'y'=4,'x'=4,'zl'=4,'c'=2] {'zl','c'}, dimensions={0} | all-to-all | bytes 65536 | tf_op jit(solution)/shard_map/all_to_all | solution.py:550
  (58 shorter events, 17.8 us)
Async XLA Ops:
  0.1 13.4 %copy-start = (bf16[1,32,128,1024]{3,2,1,0:T(8,128)(2,1)S(1)}, bf16[1,32,128,1024]{3,2,1,0:T(8,128)(2,1)}, u32[]{:S(2)}) copy-start(bf16[1,32,128,1024]{3,2,1,0:T(8,128)(2,1)} %param.3) | copy-start | bytes 25165828
  3.6 25.0 %collective-permute-start = (bf16[4,128,1024]{2,1,0:T(8,128)(2,1)S(1)}, bf16[4,128,1024]{2,1,0:T(8,128)(2,1)S(1)}, u32[]{:S(2)}, u32[]{:S(2)}) collective-permute-start(bf16[4,128,1024]{2,1,0:T(8,128)(2,1)S(1)} %get-tuple-element.54), channel_id=1, source_target_pairs={{0,8},{8,16},{16,24},{24,0},{1,9},{9,17},{17,25},{25,1},{2,10},{10... | collective-permute-start | bytes 3145736 | tf_op jit(solution)/shard_map/ppermute | solution.py:20
  5.9 24.0 %collective-permute-start.1 = (bf16[4,128,1024]{2,1,0:T(8,128)(2,1)S(1)}, bf16[4,128,1024]{2,1,0:T(8,128)(2,1)S(1)}, u32[]{:S(2)}, u32[]{:S(2)}) collective-permute-start(bf16[4,128,1024]{2,1,0:T(8,128)(2,1)S(1)} %get-tuple-element.57), channel_id=1, source_target_pairs={{0,24},{8,0},{16,8},{24,16},{1,25},{9,1},{17,9},{25,17},{2,26},{10... | collective-permute-start | bytes 3145736 | tf_op jit(solution)/shard_map/ppermute | solution.py:20
  5.9 26.4 %collective-permute-start.8 = (bf16[4,128,1024]{2,1,0:T(8,128)(2,1)S(1)}, bf16[4,128,1024]{2,1,0:T(8,128)(2,1)S(1)}, u32[]{:S(2)}, u32[]{:S(2)}) collective-permute-start(bf16[4,128,1024]{2,1,0:T(8,128)(2,1)S(1)} %get-tuple-element.68), channel_id=1, source_target_pairs={{0,32},{32,64},{64,96},{96,0},{1,33},{33,65},{65,97},{97,1},{2,34}... | collective-permute-start | bytes 3145736 | tf_op jit(solution)/shard_map/ppermute | solution.py:20
  7.3 25.0 %collective-permute-start.9 = (bf16[4,128,1024]{2,1,0:T(8,128)(2,1)S(1)}, bf16[4,128,1024]{2,1,0:T(8,128)(2,1)S(1)}, u32[]{:S(2)}, u32[]{:S(2)}) collective-permute-start(bf16[4,128,1024]{2,1,0:T(8,128)(2,1)S(1)} %get-tuple-element.69), channel_id=1, source_target_pairs={{0,96},{32,0},{64,32},{96,64},{1,97},{33,1},{65,33},{97,65},{2,98}... | collective-permute-start | bytes 3145736 | tf_op jit(solution)/shard_map/ppermute | solution.py:20
  9.8 1.2 %copy-start.3 = (f32[1,1,256,1024]{3,2,1,0:T(8,128)S(1)}, f32[1,1,256,1024]{3,2,1,0:T(8,128)}, u32[]{:S(2)}) copy-start(f32[1,1,256,1024]{3,2,1,0:T(8,128)} %param.4) | copy-start | bytes 3145732
  11.6 11.2 %collective-permute-start.10 = (bf16[256,640]{1,0:T(8,128)(2,1)S(1)}, bf16[256,640]{1,0:T(8,128)(2,1)S(1)}, u32[]{:S(2)}, u32[]{:S(2)}) collective-permute-start(bf16[256,640]{1,0:T(8,128)(2,1)S(1)} %trim.1.refs_0_), channel_id=1, source_target_pairs={{0,2},{2,4},{4,6},{6,0},{1,3},{3,5},{5,7},{7,1},{8,10},{10,12},{12... | collective-permute-start | bytes 983048 | tf_op jit(solution)/shard_map/ppermute | solution.py:20
  22.8 9.5 %collective-permute-start.11 = (bf16[256,640]{1,0:T(8,128)(2,1)S(1)}, bf16[256,640]{1,0:T(8,128)(2,1)S(1)}, u32[]{:S(2)}, u32[]{:S(2)}) collective-permute-start(bf16[256,640]{1,0:T(8,128)(2,1)S(1)} %collective-permute-done.10.refs_2_), channel_id=1, source_target_pairs={{0,2},{2,4},{4,6},{6,0},{1,3},{3,5},{5,7},{7,1},{8,10},{10,12},{12... | collective-permute-start | bytes 983048 | tf_op jit(solution)/shard_map/ppermute | solution.py:20
  30.1 11.6 %collective-permute-start.2 = (bf16[2,128,1024]{2,1,0:T(8,128)(2,1)S(1)}, bf16[2,128,1024]{2,1,0:T(8,128)(2,1)S(1)}, u32[]{:S(2)}, u32[]{:S(2)}) collective-permute-start(bf16[2,128,1024]{2,1,0:T(8,128)(2,1)S(1)} %get-tuple-element.59), channel_id=1, source_target_pairs={{0,8},{8,16},{16,24},{24,0},{1,9},{9,17},{17,25},{25,1},{2,10},{10... | collective-permute-start | bytes 1572872 | tf_op jit(solution)/shard_map/ppermute | solution.py:20
  30.6 13.1 %collective-permute-start.3 = (bf16[2,128,1024]{2,1,0:T(8,128)(2,1)S(1)}, bf16[2,128,1024]{2,1,0:T(8,128)(2,1)S(1)}, u32[]{:S(2)}, u32[]{:S(2)}) collective-permute-start(bf16[2,128,1024]{2,1,0:T(8,128)(2,1)S(1)} %get-tuple-element.60), channel_id=1, source_target_pairs={{0,24},{8,0},{16,8},{24,16},{1,25},{9,1},{17,9},{25,17},{2,26},{10... | collective-permute-start | bytes 1572872 | tf_op jit(solution)/shard_map/ppermute | solution.py:20
  32.3 41.0 %copy-start.4 = (bf16[256,640]{1,0:T(8,128)(2,1)}, bf16[256,640]{1,0:T(8,128)(2,1)S(1)}, u32[]{:S(2)}) copy-start(bf16[256,640]{1,0:T(8,128)(2,1)S(1)} %collective-permute-done.11.refs_4_) | copy-start | bytes 983044
  32.5 15.4 %collective-permute-start.12 = (bf16[2,128,1024]{2,1,0:T(8,128)(2,1)S(1)}, bf16[2,128,1024]{2,1,0:T(8,128)(2,1)S(1)}, u32[]{:S(2)}, u32[]{:S(2)}) collective-permute-start(bf16[2,128,1024]{2,1,0:T(8,128)(2,1)S(1)} %get-tuple-element.73), channel_id=1, source_target_pairs={{0,32},{32,64},{64,96},{96,0},{1,33},{33,65},{65,97},{97,1},{2,34}... | collective-permute-start | bytes 1572872 | tf_op jit(solution)/shard_map/ppermute | solution.py:20
  34.3 13.7 %collective-permute-start.13 = (bf16[2,128,1024]{2,1,0:T(8,128)(2,1)S(1)}, bf16[2,128,1024]{2,1,0:T(8,128)(2,1)S(1)}, u32[]{:S(2)}, u32[]{:S(2)}) collective-permute-start(bf16[2,128,1024]{2,1,0:T(8,128)(2,1)S(1)} %get-tuple-element.74), channel_id=1, source_target_pairs={{0,96},{32,0},{64,32},{96,64},{1,97},{33,1},{65,33},{97,65},{2,98}... | collective-permute-start | bytes 1572872 | tf_op jit(solution)/shard_map/ppermute | solution.py:20
  44.1 8.7 %collective-permute-start.4 = (bf16[2,64,1024]{2,1,0:T(8,128)(2,1)S(1)}, bf16[2,64,1024]{2,1,0:T(8,128)(2,1)S(1)}, u32[]{:S(2)}, u32[]{:S(2)}) collective-permute-start(bf16[2,64,1024]{2,1,0:T(8,128)(2,1)S(1)} %get-tuple-element.62), channel_id=1, source_target_pairs={{0,32},{32,64},{64,96},{96,0},{1,33},{33,65},{65,97},{97,1},{2,34}... | collective-permute-start | bytes 786440 | tf_op jit(solution)/shard_map/ppermute | solution.py:20
  46.4 6.4 %collective-permute-start.5 = (bf16[2,64,1024]{2,1,0:T(8,128)(2,1)S(1)}, bf16[2,64,1024]{2,1,0:T(8,128)(2,1)S(1)}, u32[]{:S(2)}, u32[]{:S(2)}) collective-permute-start(bf16[2,64,1024]{2,1,0:T(8,128)(2,1)S(1)} %get-tuple-element.63), channel_id=1, source_target_pairs={{0,96},{32,0},{64,32},{96,64},{1,97},{33,1},{65,33},{97,65},{2,98}... | collective-permute-start | bytes 786440 | tf_op jit(solution)/shard_map/ppermute | solution.py:20
  48.4 7.8 %collective-permute-start.14 = (bf16[2,64,1024]{2,1,0:T(8,128)(2,1)S(1)}, bf16[2,64,1024]{2,1,0:T(8,128)(2,1)S(1)}, u32[]{:S(2)}, u32[]{:S(2)}) collective-permute-start(bf16[2,64,1024]{2,1,0:T(8,128)(2,1)S(1)} %get-tuple-element.76), channel_id=1, source_target_pairs={{0,8},{8,16},{16,24},{24,0},{1,9},{9,17},{17,25},{25,1},{2,10},{10... | collective-permute-start | bytes 786440 | tf_op jit(solution)/shard_map/ppermute | solution.py:20
  49.0 7.6 %collective-permute-start.15 = (bf16[2,64,1024]{2,1,0:T(8,128)(2,1)S(1)}, bf16[2,64,1024]{2,1,0:T(8,128)(2,1)S(1)}, u32[]{:S(2)}, u32[]{:S(2)}) collective-permute-start(bf16[2,64,1024]{2,1,0:T(8,128)(2,1)S(1)} %get-tuple-element.77), channel_id=1, source_target_pairs={{0,24},{8,0},{16,8},{24,16},{1,25},{9,1},{17,9},{25,17},{2,26},{10... | collective-permute-start | bytes 786440 | tf_op jit(solution)/shard_map/ppermute | solution.py:20
  50.7 22.9 %collective-permute-start.21 = (bf16[256,640]{1,0:T(8,128)(2,1)S(1)}, bf16[256,640]{1,0:T(8,128)(2,1)S(1)}, u32[]{:S(2)}, u32[]{:S(2)}) collective-permute-start(bf16[256,640]{1,0:T(8,128)(2,1)S(1)} %collective-permute-done.11.refs_4_), channel_id=1, source_target_pairs={{0,2},{2,4},{4,6},{6,0},{1,3},{3,5},{5,7},{7,1},{8,10},{10,12},{12... | collective-permute-start | bytes 983048 | tf_op jit(solution)/shard_map/ppermute | solution.py:20
  52.9 6.3 %collective-permute-start.6 = (bf16[1,64,1024]{2,1,0:T(8,128)(2,1)S(1)}, bf16[1,64,1024]{2,1,0:T(8,128)(2,1)S(1)}, u32[]{:S(2)}, u32[]{:S(2)}) collective-permute-start(bf16[1,64,1024]{2,1,0:T(8,128)(2,1)S(1)} %get-tuple-element.65), channel_id=1, source_target_pairs={{0,32},{32,64},{64,96},{96,0},{1,33},{33,65},{65,97},{97,1},{2,34}... | collective-permute-start | bytes 393224 | tf_op jit(solution)/shard_map/ppermute | solution.py:20
  54.5 5.0 %collective-permute-start.7 = (bf16[1,64,1024]{2,1,0:T(8,128)(2,1)S(1)}, bf16[1,64,1024]{2,1,0:T(8,128)(2,1)S(1)}, u32[]{:S(2)}, u32[]{:S(2)}) collective-permute-start(bf16[1,64,1024]{2,1,0:T(8,128)(2,1)S(1)} %get-tuple-element.66), channel_id=1, source_target_pairs={{0,96},{32,0},{64,32},{96,64},{1,97},{33,1},{65,33},{97,65},{2,98}... | collective-permute-start | bytes 393224 | tf_op jit(solution)/shard_map/ppermute | solution.py:20
  56.6 5.0 %collective-permute-start.16 = (bf16[1,64,1024]{2,1,0:T(8,128)(2,1)S(1)}, bf16[1,64,1024]{2,1,0:T(8,128)(2,1)S(1)}, u32[]{:S(2)}, u32[]{:S(2)}) collective-permute-start(bf16[1,64,1024]{2,1,0:T(8,128)(2,1)S(1)} %get-tuple-element.79), channel_id=1, source_target_pairs={{0,8},{8,16},{16,24},{24,0},{1,9},{9,17},{17,25},{25,1},{2,10},{10... | collective-permute-start | bytes 393224 | tf_op jit(solution)/shard_map/ppermute | solution.py:20
  57.8 6.2 %collective-permute-start.17 = (bf16[1,64,1024]{2,1,0:T(8,128)(2,1)S(1)}, bf16[1,64,1024]{2,1,0:T(8,128)(2,1)S(1)}, u32[]{:S(2)}, u32[]{:S(2)}) collective-permute-start(bf16[1,64,1024]{2,1,0:T(8,128)(2,1)S(1)} %get-tuple-element.80), channel_id=1, source_target_pairs={{0,24},{8,0},{16,8},{24,16},{1,25},{9,1},{17,9},{25,17},{2,26},{10... | collective-permute-start | bytes 393224 | tf_op jit(solution)/shard_map/ppermute | solution.py:20
  64.9 23.7 %all-to-all-start = ((bf16[16,128,128]{2,1,0:T(8,128)(2,1)}), bf16[16,128,128]{2,1,0:T(8,128)(2,1)S(1)}, u32[]{:S(2)}, u32[]{:S(2)}) async-start(bf16[16,128,128]{2,1,0:T(8,128)(2,1)} %pieces.1), calls=%async_computation | async-start | bytes 1048576 | tf_op jit(solution)/shard_map/all_to_all | solution.py:544
  72.7 1.9 %collective-permute-start.18 = (bf16[256,640]{1,0:T(8,128)(2,1)S(1)}, bf16[256,640]{1,0:T(8,128)(2,1)S(1)}, u32[]{:S(2)}, u32[]{:S(2)}) collective-permute-start(bf16[256,640]{1,0:T(8,128)(2,1)S(1)} %trim.1.refs_0_), channel_id=1, source_target_pairs={{0,1},{1,0},{2,3},{3,2},{4,5},{5,4},{6,7},{7,6},{8,9},{9,8},{10,11... | collective-permute-start | bytes 983048 | tf_op jit(solution)/shard_map/ppermute | solution.py:25
  73.1 1.8 %collective-permute-start.19 = (bf16[256,640]{1,0:T(8,128)(2,1)S(1)}, bf16[256,640]{1,0:T(8,128)(2,1)S(1)}, u32[]{:S(2)}, u32[]{:S(2)}) collective-permute-start(bf16[256,640]{1,0:T(8,128)(2,1)S(1)} %collective-permute-done.10.refs_2_), channel_id=1, source_target_pairs={{0,1},{1,0},{2,3},{3,2},{4,5},{5,4},{6,7},{7,6},{8,9},{9,8},{10,11... | collective-permute-start | bytes 983048 | tf_op jit(solution)/shard_map/ppermute | solution.py:25
  73.3 2.1 %collective-permute-start.20 = (bf16[256,640]{1,0:T(8,128)(2,1)S(1)}, bf16[256,640]{1,0:T(8,128)(2,1)S(1)}, u32[]{:S(2)}, u32[]{:S(2)}) collective-permute-start(bf16[256,640]{1,0:T(8,128)(2,1)S(1)} %collective-permute-done.11.refs_4_), channel_id=1, source_target_pairs={{0,1},{1,0},{2,3},{3,2},{4,5},{5,4},{6,7},{7,6},{8,9},{9,8},{10,11... | collective-permute-start | bytes 983048 | tf_op jit(solution)/shard_map/ppermute | solution.py:25
  73.6 2.2 %collective-permute-start.22 = (bf16[256,640]{1,0:T(8,128)(2,1)S(1)}, bf16[256,640]{1,0:T(8,128)(2,1)S(1)}, u32[]{:S(2)}, u32[]{:S(2)}) collective-permute-start(bf16[256,640]{1,0:T(8,128)(2,1)S(1)} %collective-permute-done.21.refs_6_), channel_id=1, source_target_pairs={{0,1},{1,0},{2,3},{3,2},{4,5},{5,4},{6,7},{7,6},{8,9},{9,8},{10,11... | collective-permute-start | bytes 983048 | tf_op jit(solution)/shard_map/ppermute | solution.py:25
  88.7 5.6 %copy-start.2 = (bf16[4,256,640]{2,1,0:T(8,128)(2,1)S(1)}, bf16[4,256,640]{2,1,0:T(8,128)(2,1)}, u32[]{:S(2)}) copy-start(bf16[4,256,640]{2,1,0:T(8,128)(2,1)} %copy-done.1) | copy-start | bytes 3932164
  89.5 6.2 %collective-permute-start.23 = (bf16[2,128,128]{2,1,0:T(8,128)(2,1)S(1)}, bf16[2,128,128]{2,1,0:T(8,128)(2,1)S(1)}, u32[]{:S(2)}, u32[]{:S(2)}) collective-permute-start(bf16[2,128,128]{2,1,0:T(8,128)(2,1)S(1)} %get-tuple-element.96), channel_id=1, source_target_pairs={{0,2},{2,4},{4,6},{6,0},{1,3},{3,5},{5,7},{7,1},{8,10},{10,12},{12... | collective-permute-start | bytes 196616 | tf_op jit(solution)/shard_map/ppermute | solution.py:20
  90.2 8.5 %collective-permute-start.24 = (bf16[2,128,128]{2,1,0:T(8,128)(2,1)S(1)}, bf16[2,128,128]{2,1,0:T(8,128)(2,1)S(1)}, u32[]{:S(2)}, u32[]{:S(2)}) collective-permute-start(bf16[2,128,128]{2,1,0:T(8,128)(2,1)S(1)} %get-tuple-element.97), channel_id=1, source_target_pairs={{0,4},{2,6},{4,0},{6,2},{1,5},{3,7},{5,1},{7,3},{8,12},{10,14},{12... | collective-permute-start | bytes 196616 | tf_op jit(solution)/shard_map/ppermute | solution.py:20
  92.8 5.8 %collective-permute-start.25 = (bf16[2,128,128]{2,1,0:T(8,128)(2,1)S(1)}, bf16[2,128,128]{2,1,0:T(8,128)(2,1)S(1)}, u32[]{:S(2)}, u32[]{:S(2)}) collective-permute-start(bf16[2,128,128]{2,1,0:T(8,128)(2,1)S(1)} %get-tuple-element.98), channel_id=1, source_target_pairs={{0,6},{2,0},{4,2},{6,4},{1,7},{3,1},{5,3},{7,5},{8,14},{10,8},{12,... | collective-permute-start | bytes 196616 | tf_op jit(solution)/shard_map/ppermute | solution.py:20
  98.7 1.4 %collective-permute-start.26 = (bf16[4,128,128]{2,1,0:T(8,128)(2,1)S(1)}, bf16[4,128,128]{2,1,0:T(8,128)(2,1)S(1)}, u32[]{:S(2)}, u32[]{:S(2)}) collective-permute-start(bf16[4,128,128]{2,1,0:T(8,128)(2,1)S(1)} %split.1), channel_id=1, source_target_pairs={{0,1},{1,0},{2,3},{3,2},{4,5},{5,4},{6,7},{7,6},{8,9},{9,8},{10,11... | collective-permute-start | bytes 393224 | tf_op jit(solution)/shard_map/ppermute | solution.py:25
  (4 other events, 3.8 us)
